TPU v7x, 32 devices: a whole 2x2x4 slice. The times are simulated.
32 devices in a mesh: seq: 8 (over z, x), fsdp: 4 (over y, core).
Axes of the slice: x: 2, y: 2, z: 4, core: 2. Of those that a mesh axis runs over, the one named last changes fastest.
Arguments:
- tokens: bfloat16 [2, 2048, 2048], P(None, 'seq'), may hold values from -6 to 6
- resets: int32 [2, 2048], P(None, 'seq'), may hold values 0 or 1
- norm_gain: bfloat16 [2048], replicated, may hold values from 0.5 to 1.5
- branch_weight: bfloat16 [2048, 2816], P('seq', 'fsdp'), may hold values from -0.125 to 0.125
- inner_weight: bfloat16 [2048, 2816], P('seq', 'fsdp'), may hold values from -0.125 to 0.125
- conv_weight: bfloat16 [4, 2816], P(None, 'fsdp'), may hold values from -3 to 3
- conv_bias: bfloat16 [2816], P('fsdp'), may hold values from -3 to 3
- gate_blocks: bfloat16 [16, 176, 176], P('fsdp'), may hold values from -0.4375 to 0.4375
- input_blocks: bfloat16 [16, 176, 176], P('fsdp'), may hold values from -0.4375 to 0.4375
- gate_bias: bfloat16 [2816], P('fsdp'), may hold values from -3 to 3
- input_bias: bfloat16 [2816], P('fsdp'), may hold values from -3 to 3
- decay_param: bfloat16 [2816], P('fsdp'), may hold values from 4 to 12
- out_weight: bfloat16 [2816, 2048], P('fsdp', 'seq'), may hold values from -0.109375 to 0.109375
- mlp_norm_gain: bfloat16 [2048], replicated, may hold values from 0.5 to 1.5
- gate_weight: bfloat16 [2048, 6144], P('seq', 'fsdp'), may hold values from -0.125 to 0.125
- up_weight: bfloat16 [2048, 6144], P('seq', 'fsdp'), may hold values from -0.125 to 0.125
- down_weight: bfloat16 [6144, 2048], P('fsdp', 'seq'), may hold values from -0.078125 to 0.078125
- cotangent: bfloat16 [2, 2048, 2048], P(None, 'seq'), may hold values from -6 to 6
Outputs:
- mixed: float32 [2, 2048, 2048], P(None, 'seq')
- tokens_grad: float32 [2, 2048, 2048], P(None, 'seq')
- norm_gain_grad: float32 [2048], replicated
- branch_weight_grad: float32 [2048, 2816], P('seq', 'fsdp')
- inner_weight_grad: float32 [2048, 2816], P('seq', 'fsdp')
- conv_weight_grad: float32 [4, 2816], P(None, 'fsdp')
- conv_bias_grad: float32 [2816], P('fsdp')
- gate_blocks_grad: float32 [16, 176, 176], P('fsdp')
- input_blocks_grad: float32 [16, 176, 176], P('fsdp')
- gate_bias_grad: float32 [2816], P('fsdp')
- input_bias_grad: float32 [2816], P('fsdp')
- decay_param_grad: float32 [2816], P('fsdp')
- out_weight_grad: float32 [2816, 2048], P('fsdp', 'seq')
- mlp_norm_gain_grad: float32 [2048], replicated
- gate_weight_grad: float32 [2048, 6144], P('seq', 'fsdp')
- up_weight_grad: float32 [2048, 6144], P('seq', 'fsdp')
- down_weight_grad: float32 [6144, 2048], P('fsdp', 'seq')
All inputs are finite; a program needn't handle non-finite values. No bound on the sum of `resets` on one device may be relied on, other than what follows from the above.
Results may differ from a plain program's by a relative error of at most 0.0083.
Values may be sent and summed in bfloat16 or wider, within the bound.
A program may use at most 320 MiB of HBM per device.

v0:
```python
import jax
import jax.numpy as jnp
from jax import lax
from jax.sharding import PartitionSpec as P

eps = 1e-06
decay_scale = 8.0


def passed_along(block, axis, distance):
    devices = range(lax.axis_size(axis))
    route = [(i - distance, i) for i in devices if i - distance in devices]
    return lax.ppermute(block, axis, route)


def prefix(value, axis, join, neutral, backward):
    count, mine = (lax.axis_size(axis), lax.axis_index(axis))
    pieces = jax.tree.map(lambda part: lax.all_gather(part, axis), value)
    if backward:
        pieces = jax.tree.map(lambda part: part[::-1], pieces)
        mine = count - 1 - mine
    total = jax.tree.map(
        lambda part, zero: jnp.full_like(part, 0) + jnp.asarray(zero, part.dtype), value, neutral
    )

    def turn(position, total):
        longer = join(total, jax.tree.map(lambda part: part[position], pieces))
        return jax.tree.map(lambda new, old: jnp.where(position < mine, new, old), longer, total)

    return lax.fori_loop(0, count - 1, turn, total)


def combine(earlier_map, later_map):
    return (earlier_map[0] * later_map[0], later_map[0] * earlier_map[1] + later_map[1])


def rms_norm(values, gain):
    return values * lax.rsqrt(jnp.mean(values * values, axis=-1, keepdims=True) + eps) * gain


def gelu_tanh(values):
    return jax.nn.gelu(values, approximate=True)


def gated_product(gate_pre, up_pre):
    return gelu_tanh(gate_pre) * up_pre


def gate_math(gate_pre, input_pre, conv_value, decay_param, reset_flags):
    rate_gate = jax.nn.sigmoid(gate_pre)
    inlet_gate = jax.nn.sigmoid(input_pre)
    log_decay = -decay_scale * jax.nn.softplus(-decay_param) * rate_gate
    fresh_start = reset_flags[:, None] > 0
    input_scale = jnp.where(fresh_start, 1.0, jnp.sqrt(-jnp.expm1(2.0 * log_decay)))
    carries = jnp.where(fresh_start, 0.0, jnp.exp(log_decay))
    return (carries, input_scale * inlet_gate * conv_value)


def matmul(left_side, right_side):
    return jnp.dot(left_side, right_side, preferred_element_type=jnp.float32)


def matmul_nt(left_side, right_side):
    return lax.dot_general(
        left_side, right_side, (((1,), (1,)), ((), ())), preferred_element_type=jnp.float32
    )


def matmul_tn(left_side, right_side):
    return lax.dot_general(
        left_side, right_side, (((0,), (0,)), ((), ())), preferred_element_type=jnp.float32
    )


def blockwise(values, blocks):
    shaped = values.reshape(values.shape[0], blocks.shape[0], blocks.shape[1])
    return jnp.einsum("shi,hij->shj", shaped, blocks, preferred_element_type=jnp.float32).reshape(
        values.shape[0], -1
    )


def blockwise_back(gradient, blocks):
    shaped = gradient.reshape(gradient.shape[0], blocks.shape[0], blocks.shape[2])
    return jnp.einsum("shj,hij->shi", shaped, blocks, preferred_element_type=jnp.float32).reshape(
        gradient.shape[0], -1
    )


def block_grad(values, gradient, blocks):
    left_side = values.reshape(values.shape[0], blocks.shape[0], blocks.shape[1])
    right_side = gradient.reshape(gradient.shape[0], blocks.shape[0], blocks.shape[2])
    return jnp.einsum("shi,shj->hij", left_side, right_side, preferred_element_type=jnp.float32)


def unit_sum(partial_sum):
    return lax.psum(partial_sum, "fsdp")


def add_up(running, addend):
    if running is None:
        return addend
    return jax.tree.map(jnp.add, running, addend)


def mixer_front(sequence_rows, reset_flags, gathered, params):
    row_count = sequence_rows.shape[0]
    values = sequence_rows.astype(jnp.float32)
    normed = rms_norm(values, params["norm_gain"]).astype(jnp.bfloat16)
    branch_pre = matmul(normed, gathered[0])
    inner_low = matmul(normed, gathered[1]).astype(jnp.bfloat16)
    edge_rows = passed_along(inner_low[-3:], "seq", 1)
    padded = jnp.concatenate([edge_rows, inner_low], 0).astype(jnp.float32)
    conv_taps = params["conv_weight"]
    conv_sum = (
        params["conv_bias"]
        + conv_taps[0] * padded[3 : 3 + row_count]
        + conv_taps[1] * padded[2 : 2 + row_count]
    )
    conv_sum = (
        conv_sum + conv_taps[2] * padded[1 : 1 + row_count] + conv_taps[3] * padded[0:row_count]
    )
    conv_low = conv_sum.astype(jnp.bfloat16)
    gate_pre = blockwise(conv_low, params["gate_blocks"]) + params["gate_bias"]
    input_pre = blockwise(conv_low, params["input_blocks"]) + params["input_bias"]
    conv_value = conv_low.astype(jnp.float32)
    carries, drives = gate_math(gate_pre, input_pre, conv_value, params["decay_param"], reset_flags)
    decay_prods, local_state = lax.associative_scan(combine, (carries, drives), axis=0)
    stored = dict(
        values=values,
        normed=normed,
        branch_pre=branch_pre,
        padded=padded,
        conv_low=conv_low,
        conv_value=conv_value,
        gate_pre=gate_pre,
        input_pre=input_pre,
        carries=carries,
        decay_prods=decay_prods,
        local_state=local_state,
        reset_flags=reset_flags,
    )
    return (stored, (decay_prods[-1:], local_state[-1:]))


def mixer_middle(stored, state_in, cot_rows, gathered, params, pending):
    states = stored["local_state"] + stored["decay_prods"] * state_in
    branch, branch_pull = jax.vjp(gelu_tanh, stored["branch_pre"])
    mixed_low = (states * branch).astype(jnp.bfloat16)
    middle = stored["values"] + unit_sum(matmul(mixed_low, gathered[2]))
    normed_two = rms_norm(middle, params["mlp_norm_gain"]).astype(jnp.bfloat16)
    gate_mlp = matmul(normed_two, gathered[3])
    up_mlp = matmul(normed_two, gathered[4])
    activated, act_pull = jax.vjp(gated_product, gate_mlp, up_mlp)
    hidden_low = activated.astype(jnp.bfloat16)
    result = middle + unit_sum(matmul(hidden_low, gathered[5]))
    grad_down = matmul_tn(hidden_low, cot_rows)
    grad_hidden = matmul_nt(cot_rows, gathered[5])
    grad_gate_mlp, grad_up_mlp = act_pull(grad_hidden)
    gate_mlp_low = grad_gate_mlp.astype(jnp.bfloat16)
    up_mlp_low = grad_up_mlp.astype(jnp.bfloat16)
    grad_gate = matmul_tn(normed_two, gate_mlp_low)
    grad_up = matmul_tn(normed_two, up_mlp_low)
    grad_normed_two = unit_sum(
        matmul_nt(gate_mlp_low, gathered[3]) + matmul_nt(up_mlp_low, gathered[4])
    )
    _, norm_two_pull = jax.vjp(rms_norm, middle, params["mlp_norm_gain"])
    middle_back, grad_gain_two = norm_two_pull(grad_normed_two)
    grad_middle = cot_rows.astype(jnp.float32) + middle_back
    middle_low = grad_middle.astype(jnp.bfloat16)
    grad_out = matmul_tn(mixed_low, middle_low)
    pending = add_up(pending, (grad_out, grad_gate, grad_up, grad_down))
    grad_mixed = matmul_nt(middle_low, gathered[2])
    grad_state = grad_mixed * branch
    (grad_branch_pre,) = branch_pull(grad_mixed * states)
    carries = stored["carries"]
    following = jnp.concatenate([carries[1:], jnp.ones_like(carries[:1])], 0)
    tail_prod, local_adjoint = lax.associative_scan(
        combine, (following, grad_state), axis=0, reverse=True
    )
    holding = dict(
        stored,
        states=states,
        state_in=state_in,
        tail_prod=tail_prod,
        local_adjoint=local_adjoint,
        grad_branch_pre=grad_branch_pre,
        grad_middle=grad_middle,
        grad_gain_two=grad_gain_two,
    )
    return (result, holding, (stored["decay_prods"][-1:], carries[:1] * local_adjoint[:1]), pending)


def mixer_tail(holding, adjoint_in, gathered, params):
    row_count = holding["values"].shape[0]
    adjoint = holding["local_adjoint"] + holding["tail_prod"] * adjoint_in
    state_before = jnp.concatenate([holding["state_in"][None], holding["states"][:-1]], 0)

    def local_gates(gate_pre, input_pre, conv_value, decay_param):
        return gate_math(gate_pre, input_pre, conv_value, decay_param, holding["reset_flags"])

    _, gate_pull = jax.vjp(
        local_gates,
        holding["gate_pre"],
        holding["input_pre"],
        holding["conv_value"],
        params["decay_param"],
    )
    grad_gate_pre, grad_input_pre, grad_conv, grad_decay = gate_pull(
        (adjoint * state_before, adjoint)
    )
    gate_low = grad_gate_pre.astype(jnp.bfloat16)
    input_low = grad_input_pre.astype(jnp.bfloat16)
    grad_conv = (
        grad_conv
        + blockwise_back(gate_low, params["gate_blocks"])
        + blockwise_back(input_low, params["input_blocks"])
    )
    grad_gate_blocks = block_grad(holding["conv_low"], gate_low, params["gate_blocks"])
    grad_input_blocks = block_grad(holding["conv_low"], input_low, params["input_blocks"])
    grad_gate_bias = jnp.sum(gate_low.astype(jnp.float32), 0)
    grad_input_bias = jnp.sum(input_low.astype(jnp.float32), 0)
    padded = holding["padded"]
    conv_taps = params["conv_weight"]
    grad_conv_bias = jnp.sum(grad_conv, 0)
    grad_taps = jnp.stack(
        [
            jnp.sum(grad_conv * padded[3 - tap_index : 3 - tap_index + row_count], 0)
            for tap_index in range(4)
        ],
        0,
    )
    border = jnp.zeros((3, grad_conv.shape[1]), jnp.float32)
    spread = jnp.concatenate([border, grad_conv, border], 0)
    grad_padded = (
        conv_taps[0] * spread[0 : row_count + 3] + conv_taps[1] * spread[1 : row_count + 4]
    )
    grad_padded = (
        grad_padded
        + conv_taps[2] * spread[2 : row_count + 5]
        + conv_taps[3] * spread[3 : row_count + 6]
    )
    returned = passed_along(grad_padded[:3], "seq", -1)
    grad_inner = grad_padded[3:] + jnp.concatenate([jnp.zeros_like(grad_padded[6:]), returned], 0)
    inner_grad_low = grad_inner.astype(jnp.bfloat16)
    branch_grad_low = holding["grad_branch_pre"].astype(jnp.bfloat16)
    grad_branch_weight = matmul_tn(holding["normed"], branch_grad_low)
    grad_inner_weight = matmul_tn(holding["normed"], inner_grad_low)
    grad_normed = unit_sum(
        matmul_nt(branch_grad_low, gathered[0]) + matmul_nt(inner_grad_low, gathered[1])
    )
    _, norm_pull = jax.vjp(rms_norm, holding["values"], params["norm_gain"])
    values_back, grad_gain = norm_pull(grad_normed)
    grad_tokens = holding["grad_middle"] + values_back
    front_grads = (grad_branch_weight, grad_inner_weight)
    minor_grads = (
        grad_gain,
        grad_taps,
        grad_conv_bias,
        grad_gate_blocks,
        grad_input_blocks,
        grad_gate_bias,
        grad_input_bias,
        grad_decay,
        holding["grad_gain_two"],
    )
    return (grad_tokens, front_grads, minor_grads)


def settle(large_total, front_grads, pending):
    return add_up(large_total, tuple(front_grads) + tuple(pending))


def local(
    tokens,
    resets,
    norm_gain,
    branch_weight,
    inner_weight,
    conv_weight,
    conv_bias,
    gate_blocks,
    input_blocks,
    gate_bias,
    input_bias,
    decay_param,
    out_weight,
    mlp_norm_gain,
    gate_weight,
    up_weight,
    down_weight,
    cotangent,
):
    gathered = (
        lax.all_gather(branch_weight, "seq", axis=0, tiled=True),
        lax.all_gather(inner_weight, "seq", axis=0, tiled=True),
        lax.all_gather(out_weight, "seq", axis=1, tiled=True),
        lax.all_gather(gate_weight, "seq", axis=0, tiled=True),
        lax.all_gather(up_weight, "seq", axis=0, tiled=True),
        lax.all_gather(down_weight, "seq", axis=1, tiled=True),
    )
    params = dict(
        norm_gain=norm_gain.astype(jnp.float32),
        conv_weight=conv_weight.astype(jnp.float32),
        conv_bias=conv_bias.astype(jnp.float32),
        gate_blocks=gate_blocks,
        input_blocks=input_blocks,
        gate_bias=gate_bias.astype(jnp.float32),
        input_bias=input_bias.astype(jnp.float32),
        decay_param=decay_param.astype(jnp.float32),
        mlp_norm_gain=mlp_norm_gain.astype(jnp.float32),
    )
    batches = tokens.shape[0]
    unit_count = conv_bias.shape[0]
    results = []
    token_grads = []
    large_total = None
    minor_total = None
    identity = (jnp.ones((1, unit_count), jnp.float32), jnp.zeros((1, unit_count), jnp.float32))
    for batch_index in range(batches):
        stored, end_maps = mixer_front(tokens[batch_index], resets[batch_index], gathered, params)
        starts = prefix(end_maps, "seq", combine, identity, False)
        result, holding, passing, pending = mixer_middle(
            stored, starts[1][0], cotangent[batch_index], gathered, params, None
        )
        incoming = prefix(passing, "seq", combine, identity, True)
        grad_tokens, front_grads, minor_grads = mixer_tail(
            holding, incoming[1][0], gathered, params
        )
        results.append(result)
        token_grads.append(grad_tokens)
        large_total = settle(large_total, front_grads, pending)
        minor_total = add_up(minor_total, minor_grads)
    large_total = (
        lax.psum_scatter(large_total[0], "seq", scatter_dimension=0, tiled=True),
        lax.psum_scatter(large_total[1], "seq", scatter_dimension=0, tiled=True),
        lax.psum_scatter(large_total[2], "seq", scatter_dimension=1, tiled=True),
        lax.psum_scatter(large_total[3], "seq", scatter_dimension=0, tiled=True),
        lax.psum_scatter(large_total[4], "seq", scatter_dimension=0, tiled=True),
        lax.psum_scatter(large_total[5], "seq", scatter_dimension=1, tiled=True),
    )
    minor_total = lax.psum(minor_total, "seq")
    return (
        jnp.stack(results, 0),
        jnp.stack(token_grads, 0),
        minor_total[0],
        large_total[0],
        large_total[1],
        minor_total[1],
        minor_total[2],
        minor_total[3],
        minor_total[4],
        minor_total[5],
        minor_total[6],
        minor_total[7],
        large_total[2],
        minor_total[8],
        large_total[3],
        large_total[4],
        large_total[5],
    )


def solution(mesh):
    placed = (
        P(None, "seq", None),
        P(None, "seq"),
        P(),
        P("seq", "fsdp"),
        P("seq", "fsdp"),
        P(None, "fsdp"),
        P("fsdp"),
        P("fsdp", None, None),
        P("fsdp", None, None),
        P("fsdp"),
        P("fsdp"),
        P("fsdp"),
        P("fsdp", "seq"),
        P(),
        P("seq", "fsdp"),
        P("seq", "fsdp"),
        P("fsdp", "seq"),
        P(None, "seq", None),
    )
    return jax.shard_map(
        local,
        mesh=mesh,
        in_specs=placed,
        out_specs=(
            P(None, "seq", None),
            P(None, "seq", None),
            P(),
            P("seq", "fsdp"),
            P("seq", "fsdp"),
            P(None, "fsdp"),
            P("fsdp"),
            P("fsdp", None, None),
            P("fsdp", None, None),
            P("fsdp"),
            P("fsdp"),
            P("fsdp"),
            P("fsdp", "seq"),
            P(),
            P("seq", "fsdp"),
            P("seq", "fsdp"),
            P("fsdp", "seq"),
        ),
        check_vma=False,
    )
```

profile of v0, /device:TPU:0, one launch (start us, length us, event | category | flops | bytes accessed | tf_op | source)
XLA Modules:
  0.0 4043.4 jit_solution(17894483324245398079)
XLA Ops:
  13.0 59.9 %all-gather.19.cloned.1.call-done = bf16[2048,704]{0,1:T(8,128)(2,1)} async-done(((bf16[256,704]{0,1:T(8,128)(2,1)}), bf16[2048,704]{0,1:T(8,128)(2,1)}) %all-gather.19.cloned.1.call-update) | async-done | bytes 2883600 | tf_op jit(solution)/shard_map/all_gather | solution.py:295
  133.5 17.0 slice.1200
  363.9 17.0 slice.1119
  992.1 17.1 slice.1173
  1135.1 30.5 all-gather.8
  1165.6 30.5 all-gather.9
  1196.4 30.3 all-gather.6
  1226.7 30.3 all-gather.7
  1274.8 82.1 %all-reduce.154.cloned.1.call-done = (f32[256,2048]{1,0:T(8,128)}, f32[256,2048]{1,0:T(8,128)}) async-done(((f32[256,2048]{1,0:T(8,128)}, f32[256,2048]{1,0:T(8,128)}), (f32[256,2048]{1,0:T(8,128)}, f32[256,2048]{1,0:T(8,128)})) %all-reduce.154.cloned.1.call-update) | async-done | bytes 4194320 | tf_op jit(solution)/shard_map/psum | solution.py:96
  1362.3 96.1 %all-gather.25.cloned.1.call-done = bf16[2048,1536]{1,0:T(8,128)(2,1)} async-done(((bf16[256,1536]{1,0:T(8,128)(2,1)}), bf16[2048,1536]{1,0:T(8,128)(2,1)}) %all-gather.25.cloned.1.call-update) | async-done | bytes 6291472 | tf_op jit(solution)/shard_map/all_gather | solution.py:297
  1464.1 93.8 %all-gather.27.cloned.1.call-done = bf16[2048,1536]{1,0:T(8,128)(2,1)} async-done(((bf16[256,1536]{1,0:T(8,128)(2,1)}), bf16[2048,1536]{1,0:T(8,128)(2,1)}) %all-gather.27.cloned.1.call-update) | async-done | bytes 6291472 | tf_op jit(solution)/shard_map/all_gather | solution.py:298
  1569.7 88.6 %all-gather.29.cloned.1.call-done = bf16[1536,2048]{1,0:T(8,128)(2,1)} async-done(((bf16[1536,256]{1,0:T(8,128)(2,1)}), bf16[1536,2048]{1,0:T(8,128)(2,1)}) %all-gather.29.cloned.1.call-update) | async-done | bytes 6291472 | tf_op jit(solution)/shard_map/all_gather | solution.py:299
  2029.6 17.2 slice.1339
  2662.5 30.4 all-gather.10
  2740.4 30.3 all-gather.11
  2866.4 96.1 %all-reduce.150.cloned.1.call-done = (f32[256,2048]{1,0:T(8,128)}, f32[256,2048]{1,0:T(8,128)}, f32[256,2048]{1,0:T(8,128)}, f32[256,2048]{1,0:T(8,128)}) async-done(((f32[256,2048]{1,0:T(8,128)}, f32[256,2048]{1,0:T(8,128)}, f32[256,2048]{1,0:T(8,128)}, f32[256,2048]{1,0:T(8,128)}), (f32[256,2048]{1,0:T(8,128)}, f32[256,2048]{1,0:T(8,128)}, f32[256,2048]{1,0:T(8,128)}, ...) | async-done | bytes 8388624 | tf_op jit(solution)/shard_map/psum | solution.py:96
  2966.0 38.9 all-reduce.138
  3017.8 37.1 all-reduce.148.cloned.1.call-done
  3054.9 114.4 %reduce-scatter.7.cloned.1.call-done = f32[256,704]{0,1:T(8,128)} async-done(((f32[2048,704]{0,1:T(8,128)}), f32[256,704]{0,1:T(8,128)}) %reduce-scatter.7.cloned.1.call-update) | async-done | bytes 720912 | tf_op jit(solution)/shard_map/reduce_scatter | solution.py:334
  3169.3 114.7 %reduce-scatter.11.cloned.1.call-done = f32[704,256]{1,0:T(8,128)} async-done(((f32[704,2048]{1,0:T(8,128)}), f32[704,256]{1,0:T(8,128)}) %reduce-scatter.11.cloned.1.call-update) | async-done | bytes 720912 | tf_op jit(solution)/shard_map/reduce_scatter | solution.py:336
  3284.0 114.8 %reduce-scatter.9.cloned.1.call-done = f32[256,704]{0,1:T(8,128)} async-done(((f32[2048,704]{0,1:T(8,128)}), f32[256,704]{0,1:T(8,128)}) %reduce-scatter.9.cloned.1.call-update) | async-done | bytes 720912 | tf_op jit(solution)/shard_map/reduce_scatter | solution.py:335
  3398.8 211.6 %reduce-scatter.13.cloned.1.call-done = f32[256,1536]{1,0:T(8,128)} async-done(((f32[2048,1536]{1,0:T(8,128)}), f32[256,1536]{1,0:T(8,128)}) %reduce-scatter.13.cloned.1.call-update) | async-done | bytes 1572880 | tf_op jit(solution)/shard_map/reduce_scatter | solution.py:337
  3610.4 210.8 %reduce-scatter.15.cloned.1.call-done = f32[256,1536]{1,0:T(8,128)} async-done(((f32[2048,1536]{1,0:T(8,128)}), f32[256,1536]{1,0:T(8,128)}) %reduce-scatter.15.cloned.1.call-update) | async-done | bytes 1572880 | tf_op jit(solution)/shard_map/reduce_scatter | solution.py:338
  3821.2 211.4 %reduce-scatter.17.cloned.1.call-done = f32[1536,256]{1,0:T(8,128)} async-done(((f32[1536,2048]{1,0:T(8,128)}), f32[1536,256]{1,0:T(8,128)}) %reduce-scatter.17.cloned.1.call-update) | async-done | bytes 1572880 | tf_op jit(solution)/shard_map/reduce_scatter | solution.py:339
  (1288 shorter events, 2215.3 us)
Async XLA Ops:
  7.3 65.6 %all-gather.19.cloned.1.call-start = ((), (), s32[]{:S(2)}) async-start(), calls=%async_computation.6 | async-start | bytes 3244032 | tf_op jit(solution)/shard_map/all_gather | solution.py:295
  8.0 1249.9 %all-gather.21.cloned.1.call-start = ((), (), s32[]{:S(2)}) async-start(), calls=%async_computation.7 | async-start | bytes 3244032 | tf_op jit(solution)/shard_map/all_gather | solution.py:294
  8.8 1256.8 %all-gather.23.cloned.1.call-start = ((), (), s32[]{:S(2)}) async-start(), calls=%async_computation.8 | async-start | bytes 3244032 | tf_op jit(solution)/shard_map/all_gather | solution.py:296
  9.5 1347.5 %all-reduce.154.cloned.1.call-start = ((), (), s32[]{:S(2)}) async-start(), calls=%async_computation.21 | async-start | bytes 8388608 | tf_op jit(solution)/shard_map/psum | solution.py:96
  10.3 1252.9 %copy-start.188 = (f32[2048]{0:T(1024)}, f32[2048]{0:T(1024)S(1)}, u32[]{:S(2)}) copy-start(f32[2048]{0:T(1024)S(1)} %convert_element_type.146) | copy-start | bytes 24580
  12.9 118.2 %copy-start.190 = (f32[704]{0:T(1024)}, f32[704]{0:T(1024)S(1)}, u32[]{:S(2)}) copy-start(f32[704]{0:T(1024)S(1)} %fusion.128) | copy-start | bytes 8452
  76.0 10.8 collective-permute-start
  80.6 10.6 collective-permute-start.1
  1272.4 186.0 %all-gather.25.cloned.1.call-start = ((), (), s32[]{:S(2)}) async-start(), calls=%async_computation.9 | async-start | bytes 7077888 | tf_op jit(solution)/shard_map/all_gather | solution.py:297
  1273.0 285.0 %all-gather.27.cloned.1.call-start = ((), (), s32[]{:S(2)}) async-start(), calls=%async_computation.10 | async-start | bytes 7077888 | tf_op jit(solution)/shard_map/all_gather | solution.py:298
  1273.5 384.8 %all-gather.29.cloned.1.call-start = ((), (), s32[]{:S(2)}) async-start(), calls=%async_computation.11 | async-start | bytes 7077888 | tf_op jit(solution)/shard_map/all_gather | solution.py:299
  1274.3 544.2 %all-reduce.152.cloned.1.call-start = ((), (), s32[]{:S(2)}) async-start(), calls=%async_computation.20 | async-start | bytes 8388608 | tf_op jit(solution)/shard_map/psum | solution.py:96
  1362.3 195.7 %copy-start.18 = (bf16[256,2048]{1,0:T(8,128)(2,1)}, bf16[256,2048]{1,0:T(8,128)(2,1)S(1)}, u32[]{:S(2)}) copy-start(bf16[256,2048]{1,0:T(8,128)(2,1)S(1)} %get-tuple-element.795) | copy-start | bytes 3145732
  1362.3 204.4 %copy-start.40 = (bf16[256,2048]{1,0:T(8,128)(2,1)}, bf16[256,2048]{1,0:T(8,128)(2,1)S(1)}, u32[]{:S(2)}) copy-start(bf16[256,2048]{1,0:T(8,128)(2,1)S(1)} %get-tuple-element.794) | copy-start | bytes 3145732
  1686.8 1275.7 %all-reduce.150.cloned.1.call-start = ((), (), s32[]{:S(2)}) async-start(), calls=%async_computation.19 | async-start | bytes 16777216 | tf_op jit(solution)/shard_map/psum | solution.py:96
  2794.2 9.3 collective-permute-start.3
  2795.5 11.8 collective-permute-start.2
  2810.7 244.2 %all-reduce.148.cloned.1.call-start = ((), (), s32[]{:S(2)}) async-start(), calls=%async_computation.18 | async-start | bytes 2883584 | tf_op jit(solution)/shard_map/psum | solution.py:341
  2814.5 354.8 %reduce-scatter.7.cloned.1.call-start = ((), (), s32[]{:S(2)}) async-start(), calls=%async_computation.12 | async-start | bytes 6488064 | tf_op jit(solution)/shard_map/reduce_scatter | solution.py:334
  2820.2 463.8 %reduce-scatter.11.cloned.1.call-start = ((), (), s32[]{:S(2)}) async-start(), calls=%async_computation.14 | async-start | bytes 6488064 | tf_op jit(solution)/shard_map/reduce_scatter | solution.py:336
  2827.3 571.6 %reduce-scatter.9.cloned.1.call-start = ((), (), s32[]{:S(2)}) async-start(), calls=%async_computation.13 | async-start | bytes 6488064 | tf_op jit(solution)/shard_map/reduce_scatter | solution.py:335
  2834.4 776.0 %reduce-scatter.13.cloned.1.call-start = ((), (), s32[]{:S(2)}) async-start(), calls=%async_computation.15 | async-start | bytes 14155776 | tf_op jit(solution)/shard_map/reduce_scatter | solution.py:337
  2844.5 976.7 %reduce-scatter.15.cloned.1.call-start = ((), (), s32[]{:S(2)}) async-start(), calls=%async_computation.16 | async-start | bytes 14155776 | tf_op jit(solution)/shard_map/reduce_scatter | solution.py:338
  2854.6 1178.0 %reduce-scatter.17.cloned.1.call-start = ((), (), s32[]{:S(2)}) async-start(), calls=%async_computation.17 | async-start | bytes 14155776 | tf_op jit(solution)/shard_map/reduce_scatter | solution.py:339
  (264 other events, 3342.2 us)
Sparse Core Ops, SparseCore 0:
  10.2 62.7 all-gather.18
  74.9 60.9 all-gather.20
  138.0 58.1 all-gather.22
  1272.5 84.4 all-reduce.153
  1359.2 99.1 all-gather.24
  1460.7 97.1 all-gather.26
  1560.2 98.1 all-gather.28
  1686.9 83.8 all-reduce.151
  2810.8 151.6 all-reduce.149
  2967.2 87.6 all-reduce.147
  3059.6 109.6 reduce-scatter.6
  3173.8 110.1 reduce-scatter.10
  3288.7 110.1 reduce-scatter.8
  3403.3 207.0 reduce-scatter.12
  3614.8 206.3 reduce-scatter.14
  3825.7 206.8 reduce-scatter.16
where the time goes:
time: 4070 us; the launch traced here: 4040 us
  local copies, waits for them, and re-layouts  1780 us (44%)
  waiting for transfers between devices  1550 us (38%)
  other arithmetic  325 us (8%)
  blocking collectives  221 us (5%)
  matrix products  139 us (3%)
    slice x96, local copies, waits for them, and re-layouts, mixer_middle(): lax.associative_scan(combine, (following, grad_state), axis=0, reverse=True)  531 us
    slice x86, local copies, waits for them, and re-layouts, mixer_front(): lax.associative_scan(combine, (carries, drives), axis=0)  519 us
    pad x56, local copies, waits for them, and re-layouts, mixer_front(): lax.associative_scan(combine, (carries, drives), axis=0)  328 us
    pad x56, local copies, waits for them, and re-layouts, mixer_middle(): lax.associative_scan(combine, (following, grad_state), axis=0, reverse=True)  288 us
    reduce_scatter x1, waiting for transfers between devices, local(): lax.psum_scatter(large_total[3], 'seq', scatter_dimension=0, tiled=True)  212 us
    reduce_scatter x1, waiting for transfers between devices, local(): lax.psum_scatter(large_total[5], 'seq', scatter_dimension=1, tiled=True)  211 us
    reduce_scatter x1, waiting for transfers between devices, local(): lax.psum_scatter(large_total[4], 'seq', scatter_dimension=0, tiled=True)  211 us
    all_gather x6, blocking collectives, prefix(): pieces = jax.tree.map(lambda part: lax.all_gather(part, axis), value)  182 us
  transfers between devices with their start and end apart: 20, of which 17 were waited for; matrix products, arithmetic and copies ran while one was open for 32% of the time, Pallas kernels for 0%

commit v1 on v0

v1 whole, which is shorter than its diff:
```python
import functools

import jax
import jax.numpy as jnp
from jax import lax
from jax.experimental import pallas as pl
from jax.experimental.pallas import tpu as pltpu
from jax.sharding import PartitionSpec as P

eps = 1e-06
decay_scale = 8.0
f32 = jnp.float32
bf16 = jnp.bfloat16
ring_limit = 16


def gelu_tanh(values):
    return jax.nn.gelu(values, approximate=True)


def gated_product(gate_pre, up_pre):
    return gelu_tanh(gate_pre) * up_pre


def gate_math(gate_pre, input_pre, conv_value, decay_param, fresh_start):
    rate_gate = jax.nn.sigmoid(gate_pre)
    inlet_gate = jax.nn.sigmoid(input_pre)
    log_decay = -decay_scale * jax.nn.softplus(-decay_param) * rate_gate
    input_scale = jnp.where(fresh_start, 1.0, jnp.sqrt(-jnp.expm1(2.0 * log_decay)))
    carries = jnp.where(fresh_start, 0.0, jnp.exp(log_decay))
    return (carries, input_scale * inlet_gate * conv_value)


def dot_nn(left, right):
    return jnp.dot(left, right, preferred_element_type=f32)


def dot_nt(left, right):
    return lax.dot_general(left, right, (((1,), (1,)), ((), ())), preferred_element_type=f32)


def dot_tn(left, right):
    return lax.dot_general(left, right, (((0,), (0,)), ((), ())), preferred_element_type=f32)


def inverse_rms(values):
    return lax.rsqrt(jnp.mean(values * values, axis=-1, keepdims=True) + eps)


def scan_body(backward, a_ref, b_ref, prod_ref, state_ref):
    batches, length, units = a_ref.shape
    tiles = length // 8
    rows = lax.broadcasted_iota(jnp.int32, (8, units), 0)

    def step(index, carry):
        tile = tiles - 1 - index if backward else index
        where_rows = pl.ds(pl.multiple_of(tile * 8, 8), 8)
        following = []
        for batch in range(batches):
            prod_in, state_in = carry[batch]
            a = a_ref[batch, where_rows, :]
            b = b_ref[batch, where_rows, :]
            for shift in (1, 2, 4):
                turn = 8 - shift if backward else shift
                inside = rows < 8 - shift if backward else rows >= shift
                a_moved = jnp.where(inside, pltpu.roll(a, turn, 0), 1.0)
                b_moved = jnp.where(inside, pltpu.roll(b, turn, 0), 0.0)
                b = a * b_moved + b
                a = a * a_moved
            b = b + a * state_in
            a = a * prod_in
            prod_ref[batch, where_rows, :] = a
            state_ref[batch, where_rows, :] = b
            edge = 0 if backward else 7
            following.append((a[edge : edge + 1], b[edge : edge + 1]))
        return tuple(following)

    first = tuple(
        (jnp.ones((1, units), f32), jnp.zeros((1, units), f32)) for _ in range(batches)
    )
    lax.fori_loop(0, tiles, step, first)


def local_scan(a, b, backward):
    shape = jax.ShapeDtypeStruct(a.shape, f32)
    elements = a.shape[0] * a.shape[1] * a.shape[2]
    return pl.pallas_call(
        functools.partial(scan_body, backward),
        out_shape=(shape, shape),
        in_specs=[pl.BlockSpec(memory_space=pltpu.VMEM)] * 2,
        out_specs=(pl.BlockSpec(memory_space=pltpu.VMEM),) * 2,
        compiler_params=pltpu.CompilerParams(vmem_limit_bytes=32 * 1024 * 1024),
        cost_estimate=pl.CostEstimate(
            flops=20 * elements, bytes_accessed=16 * elements, transcendentals=0
        ),
    )(a, b)


def move_body(table_ref, in_ref, out_ref):
    out_ref[...] = in_ref[...].astype(out_ref.dtype)


def move_slabs(values, table, dtype):
    rows, width = values.shape
    slabs = table.shape[0]
    return pl.pallas_call(
        move_body,
        out_shape=jax.ShapeDtypeStruct((rows, width), dtype),
        grid_spec=pltpu.PrefetchScalarGridSpec(
            num_scalar_prefetch=1,
            grid=(slabs,),
            in_specs=[pl.BlockSpec((rows, width // slabs), lambda k, where: (0, where[k]))],
            out_specs=pl.BlockSpec((rows, width // slabs), lambda k, where: (0, k)),
        ),
        cost_estimate=pl.CostEstimate(
            flops=0, bytes_accessed=8 * rows * width, transcendentals=0
        ),
    )(table, values)


class Ring:
    def __init__(self, count):
        self.count = count
        self.order = list(range(0, count, 2)) + list(range(count - 1, 0, -2))
        self.place = [self.order.index(i) for i in range(count)]
        self.forth = [(self.order[i], self.order[(i + 1) % count]) for i in range(count)]
        self.back = [(there, here) for here, there in self.forth]

    def tables(self):
        here = jnp.asarray(self.place, jnp.int32)[lax.axis_index("seq")]
        steps = jnp.arange(self.count, dtype=jnp.int32)
        to_ring = jnp.asarray(self.order, jnp.int32)[(here - steps) % self.count]
        to_plain = (here - jnp.asarray(self.place, jnp.int32)) % self.count
        return to_ring, to_plain

    def gather(self, forth_piece, back_piece):
        forth, back = [forth_piece], [back_piece]
        for _ in range(self.count - 1):
            forth.append(lax.ppermute(forth[-1], "seq", self.forth))
            back.append(lax.ppermute(back[-1], "seq", self.back))
        return forth, [back[-k % self.count] for k in range(self.count)]

    def scatter(self, forth_slabs, back_slabs):
        count = self.count
        forth, back = forth_slabs[1].astype(bf16), back_slabs[count - 1].astype(bf16)
        for step in range(2, count + 1):
            forth = lax.ppermute(forth, "seq", self.forth).astype(f32) + forth_slabs[step % count]
            back = lax.ppermute(back, "seq", self.back).astype(f32) + back_slabs[count - step]
            if step < count:
                forth, back = forth.astype(bf16), back.astype(bf16)
        return forth, back


def halves_summed(partial):
    count, mine = lax.axis_size("fsdp"), lax.axis_index("fsdp")
    bit = 1
    while bit < count:
        half = partial.shape[0] // 2
        upper = (mine // bit) % 2
        kept = lax.dynamic_slice_in_dim(partial, upper * half, half, 0)
        sent = lax.dynamic_slice_in_dim(partial, (1 - upper) * half, half, 0).astype(bf16)
        got = lax.ppermute(sent, "fsdp", [(i, i ^ bit) for i in range(count)])
        partial = kept + got.astype(f32)
        bit *= 2
    return partial


def own_rows(values):
    count, mine = lax.axis_size("fsdp"), lax.axis_index("fsdp")
    bit = 1
    while bit < count:
        half = values.shape[0] // 2
        values = lax.dynamic_slice_in_dim(values, ((mine // bit) % 2) * half, half, 0)
        bit *= 2
    return values


def halves_joined(own):
    count, mine = lax.axis_size("fsdp"), lax.axis_index("fsdp")
    bit = count // 2
    while bit:
        got = lax.ppermute(own, "fsdp", [(i, i ^ bit) for i in range(count)])
        upper = (mine // bit) % 2 > 0
        own = jnp.concatenate([jnp.where(upper, got, own), jnp.where(upper, own, got)], 0)
        bit //= 2
    return own


def passed_along(block, distance):
    devices = range(lax.axis_size("seq"))
    route = [(i - distance, i) for i in devices if i - distance in devices]
    return lax.ppermute(block, "seq", route)


def state_at_entry(prods, states, sign):
    pair = passed_along(jnp.stack([prods, states], 0), sign)
    distance = 1
    while distance < lax.axis_size("seq"):
        earlier = passed_along(pair, sign * distance)
        pair = jnp.stack([pair[0] * earlier[0], pair[1] + pair[0] * earlier[1]], 0)
        distance *= 2
    return pair[1]


def block_diagonal(blocks):
    count, width = blocks.shape[0], blocks.shape[1]
    return sum(
        jnp.pad(blocks[j], ((j * width, (count - 1 - j) * width),) * 2) for j in range(count)
    )


def diagonal_blocks(square, count):
    width = square.shape[0] // count
    return jnp.stack(
        [square[j * width : (j + 1) * width, j * width : (j + 1) * width] for j in range(count)], 0
    )


def local(
    tokens,
    resets,
    norm_gain,
    branch_weight,
    inner_weight,
    conv_weight,
    conv_bias,
    gate_blocks,
    input_blocks,
    gate_bias,
    input_bias,
    decay_param,
    out_weight,
    mlp_norm_gain,
    gate_weight,
    up_weight,
    down_weight,
    cotangent,
):
    count = lax.axis_size("seq")
    batches, length, width = tokens.shape
    slab = width // count
    units, hidden = conv_bias.shape[0], down_weight.shape[0]
    rows = batches * length
    ringed = count <= ring_limit
    out_turned, down_turned = out_weight.T, down_weight.T
    if ringed:
        ring = Ring(count)
        to_ring, to_plain = ring.tables()

        def moved(values, dtype):
            return move_slabs(values, to_ring, dtype)

        def restored(values, dtype):
            return move_slabs(values, to_plain, dtype)

        def gain_moved(gain):
            return gain.reshape(count, slab)[to_ring].reshape(width)

        def gain_restored(gain):
            return gain.reshape(count, slab)[to_plain].reshape(width)

        def gather(forth_piece, back_piece):
            forth, back = ring.gather(forth_piece, back_piece)
            return jnp.concatenate(forth, 0), jnp.concatenate(back, 0)

        def gather_rows(piece):
            forth, back = ring.gather(piece[: slab // 2], piece[slab // 2 :])
            return jnp.concatenate([part for pair in zip(forth, back) for part in pair], 0)

        def gather_columns(piece):
            middle = piece.shape[1] // 2
            forth, back = ring.gather(piece[:, :middle], piece[:, middle:])
            return jnp.concatenate(
                [jnp.concatenate(pair, 1) for pair in zip(forth, back)], 0
            )

        def slabs_of(whole):
            return [whole[k * slab : (k + 1) * slab] for k in range(count)]

        def scatter(forth_whole, back_whole):
            return ring.scatter(slabs_of(forth_whole), slabs_of(back_whole))

        def scatter_rows(whole):
            pieces = slabs_of(whole)
            parts = ring.scatter(
                [piece[: slab // 2] for piece in pieces], [piece[slab // 2 :] for piece in pieces]
            )
            return jnp.concatenate(parts, 0)

        def scatter_columns(whole):
            middle = whole.shape[1] // 2
            pieces = slabs_of(whole)
            parts = ring.scatter(
                [piece[:, :middle] for piece in pieces], [piece[:, middle:] for piece in pieces]
            )
            return jnp.concatenate(parts, 1)

    else:

        def moved(values, dtype):
            return values.astype(dtype)

        restored = moved

        def gain_moved(gain):
            return gain

        gain_restored = gain_moved

        def gather_rows(piece):
            return lax.all_gather(piece, "seq", axis=0, tiled=True)

        gather_columns = gather_rows

        def gather(forth_piece, back_piece):
            return gather_rows(forth_piece), gather_rows(back_piece)

        def scatter_rows(whole):
            return lax.psum_scatter(whole, "seq", scatter_dimension=0, tiled=True)

        scatter_columns = scatter_rows

        def scatter(forth_whole, back_whole):
            return scatter_rows(forth_whole), scatter_rows(back_whole)

    branch_all, inner_all = gather(branch_weight, inner_weight)
    out_all = gather_rows(out_turned)
    gate_all, up_all = gather(gate_weight, up_weight)
    down_all = gather_columns(down_turned)

    gain_one = gain_moved(norm_gain.astype(f32))
    gain_two = gain_moved(mlp_norm_gain.astype(f32))
    taps = conv_weight.astype(f32)
    decay = decay_param.astype(f32)
    gate_square, input_square = block_diagonal(gate_blocks), block_diagonal(input_blocks)
    fresh_start = resets[:, :, None] > 0

    tokens_low = moved(tokens.reshape(rows, width), bf16)
    cot_low = moved(cotangent.reshape(rows, width), bf16)
    values = tokens_low.astype(f32)
    normed = (values * inverse_rms(values) * gain_one).astype(bf16)
    inner_low = dot_nn(normed, inner_all).astype(bf16).reshape(batches, length, units)
    branch_pre = dot_nn(normed, branch_all).reshape(batches, length, units)
    edge_rows = passed_along(inner_low[:, -3:], 1)
    padded = jnp.concatenate([edge_rows, inner_low], 1).astype(f32)
    conv_sum = conv_bias.astype(f32) + taps[0] * padded[:, 3:] + taps[1] * padded[:, 2:-1]
    conv_sum = conv_sum + taps[2] * padded[:, 1:-2] + taps[3] * padded[:, :-3]
    conv_low = conv_sum.astype(bf16)
    conv_flat = conv_low.reshape(rows, units)
    gate_pre = dot_nn(conv_flat, gate_square).reshape(batches, length, units)
    gate_pre = gate_pre + gate_bias.astype(f32)
    input_pre = dot_nn(conv_flat, input_square).reshape(batches, length, units)
    input_pre = input_pre + input_bias.astype(f32)
    conv_value = conv_low.astype(f32)

    def gates(gate_pre, input_pre, conv_value, decay):
        return gate_math(gate_pre, input_pre, conv_value, decay, fresh_start)

    carries, drives = gates(gate_pre, input_pre, conv_value, decay)
    prods, local_state = local_scan(carries, drives, False)
    state_in = state_at_entry(prods[:, -1:], local_state[:, -1:], 1)
    states = local_state + prods * state_in

    branch, branch_pull = jax.vjp(gelu_tanh, branch_pre)
    mixed_low = (states * branch).astype(bf16).reshape(rows, units)
    own_middle = own_rows(tokens_low).astype(f32) + halves_summed(dot_nt(mixed_low, out_all))
    scale_two = inverse_rms(own_middle)
    unit_two = own_middle * scale_two
    normed_two = halves_joined((unit_two * gain_two).astype(bf16))

    gate_mlp = dot_nn(normed_two, gate_all)
    up_mlp = dot_nn(normed_two, up_all)
    activated, act_pull = jax.vjp(gated_product, gate_mlp, up_mlp)
    hidden_low = activated.astype(bf16)
    down_grad = scatter_columns(dot_tn(cot_low, hidden_low)).T
    grad_gate_mlp, grad_up_mlp = act_pull(dot_nn(cot_low, down_all))
    gate_mlp_low, up_mlp_low = grad_gate_mlp.astype(bf16), grad_up_mlp.astype(bf16)
    gate_grad, up_grad = scatter(dot_tn(normed_two, gate_mlp_low), dot_tn(normed_two, up_mlp_low))
    own_back = halves_summed(dot_nt(gate_mlp_low, gate_all) + dot_nt(up_mlp_low, up_all))
    own_mixed = own_middle + halves_summed(dot_nt(hidden_low, down_all))
    mixed = halves_joined(restored(own_mixed, bf16)).astype(f32).reshape(tokens.shape)

    gain_two_grad = jnp.sum(own_back * unit_two, 0)
    weighted = own_back * gain_two
    own_grad = own_rows(cot_low).astype(f32) + scale_two * (
        weighted - unit_two * jnp.mean(weighted * unit_two, axis=-1, keepdims=True)
    )
    middle_low = halves_joined(own_grad.astype(bf16))

    out_grad = scatter_rows(dot_tn(middle_low, mixed_low)).T
    grad_mixed = dot_nn(middle_low, out_all).reshape(batches, length, units)
    (grad_branch_pre,) = branch_pull(grad_mixed * states)
    branch_low = grad_branch_pre.astype(bf16).reshape(rows, units)
    following = jnp.concatenate([carries[:, 1:], jnp.ones_like(carries[:, :1])], 1)
    tail_prods, local_adjoint = local_scan(following, grad_mixed * branch, True)
    adjoint_in = state_at_entry(prods[:, -1:], carries[:, :1] * local_adjoint[:, :1], -1)
    adjoint = local_adjoint + tail_prods * adjoint_in
    state_before = jnp.concatenate([state_in, states[:, :-1]], 1)
    _, gate_pull = jax.vjp(gates, gate_pre, input_pre, conv_value, decay)
    grad_gate_pre, grad_input_pre, grad_conv, decay_grad = gate_pull(
        (adjoint * state_before, adjoint)
    )
    gate_low = grad_gate_pre.astype(bf16).reshape(rows, units)
    input_low = grad_input_pre.astype(bf16).reshape(rows, units)
    back_conv = dot_nt(gate_low, gate_square) + dot_nt(input_low, input_square)
    grad_conv = grad_conv + back_conv.reshape(batches, length, units)
    block_count = gate_blocks.shape[0]
    gate_blocks_grad = diagonal_blocks(dot_tn(conv_flat, gate_low), block_count)
    input_blocks_grad = diagonal_blocks(dot_tn(conv_flat, input_low), block_count)

    border = jnp.zeros((batches, 3, units), f32)
    spread = jnp.concatenate([border, grad_conv, border], 1)
    stop = length + 3
    grad_padded = taps[0] * spread[:, :stop] + taps[1] * spread[:, 1 : stop + 1]
    grad_padded = grad_padded + taps[2] * spread[:, 2 : stop + 2] + taps[3] * spread[:, 3:]
    returned = passed_along(grad_padded[:, :3], -1)
    grad_inner = jnp.concatenate(
        [grad_padded[:, 3:-3], grad_padded[:, -3:] + returned], 1
    )
    inner_grad_low = grad_inner.astype(bf16).reshape(rows, units)
    branch_grad, inner_grad = scatter(dot_tn(normed, branch_low), dot_tn(normed, inner_grad_low))
    own_front = halves_summed(dot_nt(branch_low, branch_all) + dot_nt(inner_grad_low, inner_all))

    own_values = own_rows(tokens_low).astype(f32)
    scale_one = inverse_rms(own_values)
    unit_one = own_values * scale_one
    gain_one_grad = jnp.sum(own_front * unit_one, 0)
    weighted = own_front * gain_one
    own_tokens = own_grad + scale_one * (
        weighted - unit_one * jnp.mean(weighted * unit_one, axis=-1, keepdims=True)
    )
    tokens_grad = halves_joined(restored(own_tokens, bf16)).astype(f32).reshape(tokens.shape)

    taps_grad = jnp.stack(
        [jnp.sum(grad_conv * padded[:, 3 - k : 3 - k + length], (0, 1)) for k in range(4)], 0
    )
    small = jnp.concatenate(
        [
            taps_grad,
            jnp.sum(grad_conv, (0, 1))[None],
            jnp.sum(gate_low.astype(f32), 0)[None],
            jnp.sum(input_low.astype(f32), 0)[None],
            decay_grad[None],
        ],
        0,
    )
    small, gate_blocks_grad, input_blocks_grad = lax.psum(
        (small, gate_blocks_grad, input_blocks_grad), "seq"
    )
    gains = jnp.stack([gain_restored(gain_one_grad), gain_restored(gain_two_grad)], 0)
    gains = lax.psum(gains, ("seq", "fsdp"))
    return (
        mixed,
        tokens_grad,
        gains[0],
        branch_grad,
        inner_grad,
        small[:4],
        small[4],
        gate_blocks_grad,
        input_blocks_grad,
        small[5],
        small[6],
        small[7],
        out_grad,
        gains[1],
        gate_grad,
        up_grad,
        down_grad,
    )


def solution(mesh):
    units, both = P("fsdp"), P("seq", "fsdp")
    blocks, turned = P("fsdp", None, None), P("fsdp", "seq")
    rows = P(None, "seq", None)
    return jax.shard_map(
        local,
        mesh=mesh,
        in_specs=(
            rows,
            P(None, "seq"),
            P(),
            both,
            both,
            P(None, "fsdp"),
            units,
            blocks,
            blocks,
            units,
            units,
            units,
            turned,
            P(),
            both,
            both,
            turned,
            rows,
        ),
        out_specs=(
            rows,
            rows,
            P(),
            both,
            both,
            P(None, "fsdp"),
            units,
            blocks,
            blocks,
            units,
            units,
            units,
            turned,
            P(),
            both,
            both,
            turned,
        ),
        check_vma=False,
    )
```

time: 4070 us -> 932 us (0.23)
  local copies, waits for them, and re-layouts: 1780 us -> 82.4 us
  waiting for transfers between devices: 1550 us -> 359 us
  other arithmetic: 325 us -> 96.1 us
  starting transfers between devices: 9.79 us -> 161 us
  blocking collectives: 221 us -> 81.6 us
  matrix products: 139 us -> 98.3 us
    slice x189 -> x16, local copies, waits for them, and re-layouts: 1050 us -> 11.3 us  [the longest x4 3.81 us: slabs_of(): return [whole[k * slab:(k + 1) * slab] for k in range(count)]]
    reduce_scatter x6 -> x0, waiting for transfers between devices: 978 us -> none  [the longest x1 212 us: local(): lax.psum_scatter(large_total[3], 'seq', scatter_dimension=0, tiled=True)]
    pad x112 -> x0, local copies, waits for them, and re-layouts: 615 us -> none  [the longest x56 328 us: mixer_front(): lax.associative_scan(combine, (carries, drives), axis=0)]
    ppermute x4 -> x138, waiting for transfers between devices: 14.1 us -> 359 us  [the longest x28 121 us: scatter(): lax.ppermute(forth, 'seq', self.forth).astype(f32)]
    all_gather x6 -> x0, waiting for transfers between devices: 338 us -> none  [the longest x1 96.1 us: local(): lax.all_gather(gate_weight, 'seq', axis=0, tiled=True)]
    psum x4 -> x1, waiting for transfers between devices: 215 us -> 0.01 us  [local(): lax.psum((small, gate_blocks_grad, input_blocks_grad), 'seq')]
    all_gather x6 -> x0, blocking collectives: 182 us -> none  [prefix(): pieces = jax.tree.map(lambda part: lax.all_gather(part, axis), value)]
    ppermute x4 -> x138, starting transfers between devices: 8.22 us -> 160 us  [the longest x28 44.9 us: gather(): back.append(lax.ppermute(back[-1], 'seq', self.back))]
  transfers between devices with their start and end apart: 20 -> 139, of which waited for: 17 -> 48; matrix products, arithmetic and copies ran while one was open for 32% -> 22% of each run, Pallas kernels for 0% -> 3%
where the time goes in v1:
time: 932 us; the launch traced here: 922 us
  waiting for transfers between devices  359 us (39%)
  starting transfers between devices  161 us (17%)
  matrix products  98.3 us (11%)
  other arithmetic  96.1 us (10%)
  local copies, waits for them, and re-layouts  82.4 us (9%)
  blocking collectives  81.6 us (9%)
  Pallas kernels  27.5 us (3%)
  between operations  17.3 us (2%)
    ppermute x28, waiting for transfers between devices, scatter(): lax.ppermute(forth, 'seq', self.forth).astype(f32)  121 us
    ppermute x28, waiting for transfers between devices, gather(): back.append(lax.ppermute(back[-1], 'seq', self.back))  78.9 us
    ppermute x28, waiting for transfers between devices, scatter(): lax.ppermute(back, 'seq', self.back).astype(f32) + back_slabs[count - step]  71.9 us
    ppermute x28, waiting for transfers between devices, gather(): forth.append(lax.ppermute(forth[-1], 'seq', self.forth))  70.4 us
    unnamed x289, local copies, waits for them, and re-layouts  50.5 us
    ppermute x28, starting transfers between devices, gather(): back.append(lax.ppermute(back[-1], 'seq', self.back))  44.9 us
    psum x1, blocking collectives, local(): lax.psum((small, gate_blocks_grad, input_blocks_grad), 'seq')  41.4 us
    dot_general x8, matrix products, dot_nt(): lax.dot_general(left, right, (((1,), (1,)), ((), ())), preferred_element_...  40.2 us
  transfers between devices with their start and end apart: 139, of which 48 were waited for; matrix products, arithmetic and copies ran while one was open for 22% of the time, Pallas kernels for 3%

profile of v1, /device:TPU:0, one launch (start us, length us, event | category | flops | bytes accessed | tf_op | source)
XLA Modules:
  0.0 922.4 jit_solution(152017328564290790)
XLA Ops:
  50.5 18.2 %collective-permute-done.27 = bf16[128,704]{0,1:T(8,128)(2,1)} collective-permute-done((bf16[128,704]{0,1:T(8,128)(2,1)}, bf16[128,704]{0,1:T(8,128)(2,1)}, u32[]{:S(2)}, u32[]{:S(2)}) %collective-permute-start.27) | collective-permute-done | bytes 180256 | tf_op jit(solution)/shard_map/ppermute | solution.py:139
  122.6 22.7 %collective-permute-done.3 = bf16[256,704]{0,1:T(8,128)(2,1)S(1)} collective-permute-done((bf16[256,704]{0,1:T(8,128)(2,1)S(1)}, bf16[256,704]{0,1:T(8,128)(2,1)S(1)}, u32[]{:S(2)}, u32[]{:S(2)}) %collective-permute-start.3) | collective-permute-done | bytes 360480 | tf_op jit(solution)/shard_map/ppermute | solution.py:140
  154.6 16.3 %collective-permute-done.32 = bf16[128,704]{0,1:T(8,128)(2,1)S(1)} collective-permute-done((bf16[128,704]{0,1:T(8,128)(2,1)S(1)}, bf16[128,704]{0,1:T(8,128)(2,1)S(1)}, u32[]{:S(2)}, u32[]{:S(2)}) %collective-permute-start.32) | collective-permute-done | bytes 180256 | tf_op jit(solution)/shard_map/ppermute | solution.py:139
  222.7 9.0 collective-permute-done.62
  261.5 8.0 collective-permute-done.10
  294.2 11.0 %collective-permute-done.48 = bf16[256,1536]{1,0:T(8,128)(2,1)S(1)} collective-permute-done((bf16[256,1536]{1,0:T(8,128)(2,1)S(1)}, bf16[256,1536]{1,0:T(8,128)(2,1)S(1)}, u32[]{:S(2)}, u32[]{:S(2)}) %collective-permute-start.48) | collective-permute-done | bytes 786464 | tf_op jit(solution)/shard_map/ppermute | solution.py:140
  314.6 9.0 collective-permute-done.49
  331.9 8.9 collective-permute-done.50
  353.0 10.5 %fusion.9 = (bf16[512,1536]{1,0:T(8,128)(2,1)}, bf16[512,1536]{1,0:T(8,128)(2,1)}, bf16[512,1536]{1,0:T(8,128)(2,1)S(1)}) fusion(f32[512,1536]{1,0:T(8,128)S(1)} %fusion.139, f32[512,1536]{1,0:T(8,128)S(1)} %fusion.117, bf16[2048,1536]{1,0:T(8,128)(2,1)} %constant_dynamic-update-slice_fusion.31, bf16[256,2048]{1,0:T(8,128)(2,1)S(1)} %get-tuple-element.113, ...), kind=kOutput, calls=%fused_computation.18 | convolution fusion | flops 3245867008 | bytes 19398656 | tf_op jit(solution)/shard_map/dot_general | solution.py:35
  363.5 7.9 fusion.138
  375.0 12.4 %fusion.140 = f32[512,2048]{1,0:T(8,128)} fusion(bf16[512,1536]{1,0:T(8,128)(2,1)S(1)} %copy-done.109, bf16[2048,1536]{1,0:T(8,128)(2,1)} %copy-done.72), kind=kOutput, calls=%fused_computation.418 | convolution fusion | flops 3221225472 | bytes 12058624 | tf_op jit(solution)/shard_map/dot_general | solution.py:39
  394.1 9.9 %convolution_add_fusion.1 = f32[512,2048]{1,0:T(8,128)} fusion(f32[512,2048]{1,0:T(8,128)} %fusion.140, bf16[512,1536]{1,0:T(8,128)(2,1)} %get-tuple-element.76, bf16[2048,1536]{1,0:T(8,128)(2,1)} %constant_dynamic-update-slice_fusion.31), kind=kOutput, calls=%fused_computation.22 | convolution fusion | flops 3222274048 | bytes 16252928 | tf_op jit(solution)/shard_map/dot_general | solution.py:39
  411.9 7.8 fusion.115
  421.2 16.4 %collective-permute-done.124 = bf16[256,768]{0,1:T(8,128)(2,1)S(1)} collective-permute-done((bf16[256,768]{0,1:T(8,128)(2,1)S(1)}, bf16[256,768]{0,1:T(8,128)(2,1)S(1)}, u32[]{:S(2)}, u32[]{:S(2)}) %collective-permute-start.124) | collective-permute-done | bytes 393248 | tf_op jit(solution)/shard_map/ppermute | solution.py:147
  444.3 13.9 %collective-permute-done.117 = bf16[256,1536]{1,0:T(8,128)(2,1)S(1)} collective-permute-done((bf16[256,1536]{1,0:T(8,128)(2,1)S(1)}, bf16[256,1536]{1,0:T(8,128)(2,1)S(1)}, u32[]{:S(2)}, u32[]{:S(2)}) %collective-permute-start.117) | collective-permute-done | bytes 786464 | tf_op jit(solution)/shard_map/ppermute | solution.py:148
  471.6 11.2 %collective-permute-done.126 = bf16[256,768]{0,1:T(8,128)(2,1)S(1)} collective-permute-done((bf16[256,768]{0,1:T(8,128)(2,1)S(1)}, bf16[256,768]{0,1:T(8,128)(2,1)S(1)}, u32[]{:S(2)}, u32[]{:S(2)}) %collective-permute-start.126) | collective-permute-done | bytes 393248 | tf_op jit(solution)/shard_map/ppermute | solution.py:147
  512.1 18.8 %collective-permute-done.128 = bf16[256,768]{0,1:T(8,128)(2,1)S(1)} collective-permute-done((bf16[256,768]{0,1:T(8,128)(2,1)S(1)}, bf16[256,768]{0,1:T(8,128)(2,1)S(1)}, u32[]{:S(2)}, u32[]{:S(2)}) %collective-permute-start.128) | collective-permute-done | bytes 393248 | tf_op jit(solution)/shard_map/ppermute | solution.py:147
  542.4 12.7 %collective-permute-done.136 = bf16[256,768]{0,1:T(8,128)(2,1)S(1)} collective-permute-done((bf16[256,768]{0,1:T(8,128)(2,1)S(1)}, bf16[256,768]{0,1:T(8,128)(2,1)S(1)}, u32[]{:S(2)}, u32[]{:S(2)}) %collective-permute-start.136) | collective-permute-done | bytes 393248 | tf_op jit(solution)/shard_map/ppermute | solution.py:148
  636.4 41.4 %psum.29 = f32[8,704]{1,0:T(8,128)S(1)} all-reduce(f32[8,704]{1,0:T(8,128)S(1)} %concatenate.124), channel_id=1, replica_groups=mesh['seq'=8,'fsdp'=4] {'seq'}, use_global_device_ids=true, to_apply=%region_16.17 | all-reduce | flops 5632 | bytes 45056 | tf_op jit(solution)/shard_map/psum | solution.py:447
  698.7 7.8 collective-permute-done.97
  709.0 19.5 %collective-permute-done.104 = bf16[128,704]{0,1:T(8,128)(2,1)S(1)} collective-permute-done((bf16[128,704]{0,1:T(8,128)(2,1)S(1)}, bf16[128,704]{0,1:T(8,128)(2,1)S(1)}, u32[]{:S(2)}, u32[]{:S(2)}) %collective-permute-start.104) | collective-permute-done | bytes 180256 | tf_op jit(solution)/shard_map/ppermute | solution.py:148
  761.6 32.5 %collective-permute-done.101 = bf16[128,704]{0,1:T(8,128)(2,1)S(1)} collective-permute-done((bf16[128,704]{0,1:T(8,128)(2,1)S(1)}, bf16[128,704]{0,1:T(8,128)(2,1)S(1)}, u32[]{:S(2)}, u32[]{:S(2)}) %collective-permute-start.101) | collective-permute-done | bytes 180256 | tf_op jit(solution)/shard_map/ppermute | solution.py:147
  799.4 8.0 collective-permute-done.102
  841.8 40.2 %psum.28 = f32[2,2048]{1,0:T(2,128)S(1)} all-reduce(f32[2,2048]{1,0:T(2,128)S(1)} %pad_maximum_fusion.14), channel_id=1, replica_groups=mesh['seq'=8,'fsdp'=4] {'seq','fsdp'}, use_global_device_ids=true, to_apply=%region_7.8 | all-reduce | flops 4096 | bytes 32768 | tf_op jit(solution)/shard_map/psum | solution.py:451
  (760 shorter events, 530.9 us)
Async XLA Ops:
  7.2 903.8 %all-reduce.14.cloned.1.call-start = ((), (), s32[]{:S(2)}) async-start(), calls=%async_computation | async-start | bytes 2883584 | tf_op jit(solution)/shard_map/psum | solution.py:447
  16.1 54.1 %collective-permute-start.52 = (bf16[256,768]{0,1:T(8,128)(2,1)}, bf16[256,768]{0,1:T(8,128)(2,1)S(1)}, u32[]{:S(2)}, u32[]{:S(2)}) collective-permute-start(bf16[256,768]{0,1:T(8,128)(2,1)} %get-tuple-element.128), channel_id=1, source_target_pairs={{8,0},{16,8},{24,16},{28,24},{20,28},{12,20},{4,12},{0,4},{9,1},{1... | collective-permute-start | bytes 1179656 | tf_op jit(solution)/shard_map/ppermute | solution.py:140
  44.0 50.5 %collective-permute-start.37 = (bf16[256,1536]{1,0:T(8,128)(2,1)}, bf16[256,1536]{1,0:T(8,128)(2,1)}, u32[]{:S(2)}, u32[]{:S(2)}) collective-permute-start(bf16[256,1536]{1,0:T(8,128)(2,1)} %param.35), channel_id=1, source_target_pairs={{0,8},{8,16},{16,24},{24,28},{28,20},{20,12},{12,4},{4,0},{1,9},{9... | collective-permute-start | bytes 2359304 | tf_op jit(solution)/shard_map/ppermute | solution.py:139
  101.3 49.6 %collective-permute-start.44 = (bf16[256,1536]{1,0:T(8,128)(2,1)S(1)}, bf16[256,1536]{1,0:T(8,128)(2,1)S(1)}, u32[]{:S(2)}, u32[]{:S(2)}) collective-permute-start(bf16[256,1536]{1,0:T(8,128)(2,1)S(1)} %copy-done.40), channel_id=1, source_target_pairs={{8,0},{16,8},{24,16},{28,24},{20,28},{12,20},{4,12},{0,4},{9,1},{1... | collective-permute-start | bytes 2359304 | tf_op jit(solution)/shard_map/ppermute | solution.py:140
  207.5 49.6 %collective-permute-start.46 = (bf16[256,1536]{1,0:T(8,128)(2,1)}, bf16[256,1536]{1,0:T(8,128)(2,1)}, u32[]{:S(2)}, u32[]{:S(2)}) collective-permute-start(bf16[256,1536]{1,0:T(8,128)(2,1)} %collective-permute-done.45), channel_id=1, source_target_pairs={{8,0},{16,8},{24,16},{28,24},{20,28},{12,20},{4,12},{0,4},{9,1},{1... | collective-permute-start | bytes 2359304 | tf_op jit(solution)/shard_map/ppermute | solution.py:140
  405.8 61.4 %collective-permute-start.69 = (bf16[256,2048]{1,0:T(8,128)(2,1)S(1)}, bf16[256,2048]{1,0:T(8,128)(2,1)S(1)}, u32[]{:S(2)}, u32[]{:S(2)}) collective-permute-start(bf16[256,2048]{1,0:T(8,128)(2,1)S(1)} %dynamic-slice_convert_fusion.1), channel_id=1, source_target_pairs={{0,1},{1,0},{2,3},{3,2},{4,5},{5,4},{6,7},{7,6},{8,9},{9,8},{10,11... | collective-permute-start | bytes 3145736 | tf_op jit(solution)/shard_map/ppermute | solution.py:162
  407.6 61.8 %collective-permute-start.65 = (bf16[256,2048]{1,0:T(8,128)(2,1)S(1)}, bf16[256,2048]{1,0:T(8,128)(2,1)S(1)}, u32[]{:S(2)}, u32[]{:S(2)}) collective-permute-start(bf16[256,2048]{1,0:T(8,128)(2,1)S(1)} %dynamic-slice_convert_fusion.2), channel_id=1, source_target_pairs={{0,1},{1,0},{2,3},{3,2},{4,5},{5,4},{6,7},{7,6},{8,9},{9,8},{10,11... | collective-permute-start | bytes 3145736 | tf_op jit(solution)/shard_map/ppermute | solution.py:162
  461.1 47.5 %collective-permute-start.118 = (bf16[256,1536]{1,0:T(8,128)(2,1)}, bf16[256,1536]{1,0:T(8,128)(2,1)}, u32[]{:S(2)}, u32[]{:S(2)}) collective-permute-start(bf16[256,1536]{1,0:T(8,128)(2,1)} %fusion.29), channel_id=1, source_target_pairs={{8,0},{16,8},{24,16},{28,24},{20,28},{12,20},{4,12},{0,4},{9,1},{1... | collective-permute-start | bytes 2359304 | tf_op jit(solution)/shard_map/ppermute | solution.py:148
  537.6 47.8 %collective-permute-start.68 = (bf16[256,2048]{1,0:T(8,128)(2,1)S(1)}, bf16[256,2048]{1,0:T(8,128)(2,1)S(1)}, u32[]{:S(2)}, u32[]{:S(2)}) collective-permute-start(bf16[256,2048]{1,0:T(8,128)(2,1)S(1)} %pad_maximum_fusion.8), channel_id=1, source_target_pairs={{0,1},{1,0},{2,3},{3,2},{4,5},{5,4},{6,7},{7,6},{8,9},{9,8},{10,11... | collective-permute-start | bytes 3145736 | tf_op jit(solution)/shard_map/ppermute | solution.py:182
  542.1 57.9 %collective-permute-start.113 = (bf16[256,1536]{1,0:T(8,128)(2,1)S(1)}, bf16[256,1536]{1,0:T(8,128)(2,1)S(1)}, u32[]{:S(2)}, u32[]{:S(2)}) collective-permute-start(bf16[256,1536]{1,0:T(8,128)(2,1)S(1)} %fusion.33), channel_id=1, source_target_pairs={{0,8},{8,16},{16,24},{24,28},{28,20},{20,12},{12,4},{4,0},{1,9},{9... | collective-permute-start | bytes 2359304 | tf_op jit(solution)/shard_map/ppermute | solution.py:147
  589.5 108.0 %collective-permute-start.82 = (bf16[256,704]{0,1:T(8,128)(2,1)}, bf16[256,704]{0,1:T(8,128)(2,1)}, u32[]{:S(2)}, u32[]{:S(2)}) collective-permute-start(bf16[256,704]{0,1:T(8,128)(2,1)} %slice.938), channel_id=1, source_target_pairs={{0,8},{8,16},{16,24},{24,28},{28,20},{20,12},{12,4},{4,0},{1,9},{9... | collective-permute-start | bytes 1081352 | tf_op jit(solution)/shard_map/ppermute | solution.py:147
  595.2 97.0 %collective-permute-start.96 = (bf16[128,704]{0,1:T(8,128)(2,1)}, bf16[128,704]{0,1:T(8,128)(2,1)S(1)}, u32[]{:S(2)}, u32[]{:S(2)}) collective-permute-start(bf16[128,704]{0,1:T(8,128)(2,1)} %get-tuple-element.95), channel_id=1, source_target_pairs={{0,8},{8,16},{16,24},{24,28},{28,20},{20,12},{12,4},{4,0},{1,9},{9... | collective-permute-start | bytes 540680 | tf_op jit(solution)/shard_map/ppermute | solution.py:147
  599.9 92.4 %collective-permute-start.103 = (bf16[128,704]{0,1:T(8,128)(2,1)}, bf16[128,704]{0,1:T(8,128)(2,1)}, u32[]{:S(2)}, u32[]{:S(2)}) collective-permute-start(bf16[128,704]{0,1:T(8,128)(2,1)} %get-tuple-element.96), channel_id=1, source_target_pairs={{8,0},{16,8},{24,16},{28,24},{20,28},{12,20},{4,12},{0,4},{9,1},{1... | collective-permute-start | bytes 540680 | tf_op jit(solution)/shard_map/ppermute | solution.py:148
  605.7 139.2 %collective-permute-start.114 = (bf16[256,1536]{1,0:T(8,128)(2,1)}, bf16[256,1536]{1,0:T(8,128)(2,1)}, u32[]{:S(2)}, u32[]{:S(2)}) collective-permute-start(bf16[256,1536]{1,0:T(8,128)(2,1)} %fusion.32), channel_id=1, source_target_pairs={{0,8},{8,16},{16,24},{24,28},{28,20},{20,12},{12,4},{4,0},{1,9},{9... | collective-permute-start | bytes 2359304 | tf_op jit(solution)/shard_map/ppermute | solution.py:147
  634.9 49.0 %collective-permute-start.77 = (f32[2,3,704]{2,1,0:T(4,128)S(1)}, f32[2,3,704]{2,1,0:T(4,128)S(1)}, u32[]{:S(2)}, u32[]{:S(2)}) collective-permute-start(f32[2,3,704]{2,1,0:T(4,128)S(1)} %slice.618), channel_id=1, source_target_pairs={{4,0},{8,4},{12,8},{16,12},{20,16},{24,20},{28,24},{5,1},{9,5},{13... | collective-permute-start | bytes 50696 | tf_op jit(solution)/shard_map/ppermute | solution.py:192
  683.9 64.9 %collective-permute-start.121 = (bf16[256,1536]{1,0:T(8,128)(2,1)S(1)}, bf16[256,1536]{1,0:T(8,128)(2,1)S(1)}, u32[]{:S(2)}, u32[]{:S(2)}) collective-permute-start(bf16[256,1536]{1,0:T(8,128)(2,1)S(1)} %copy-done.43), channel_id=1, source_target_pairs={{8,0},{16,8},{24,16},{28,24},{20,28},{12,20},{4,12},{0,4},{9,1},{1... | collective-permute-start | bytes 2359304 | tf_op jit(solution)/shard_map/ppermute | solution.py:148
  739.9 56.8 %collective-permute-start.78 = (bf16[256,2048]{1,0:T(8,128)(2,1)S(1)}, bf16[256,2048]{1,0:T(8,128)(2,1)S(1)}, u32[]{:S(2)}, u32[]{:S(2)}) collective-permute-start(bf16[256,2048]{1,0:T(8,128)(2,1)S(1)} %dynamic-slice_convert_fusion), channel_id=1, source_target_pairs={{0,1},{1,0},{2,3},{3,2},{4,5},{5,4},{6,7},{7,6},{8,9},{9,8},{10,11... | collective-permute-start | bytes 3145736 | tf_op jit(solution)/shard_map/ppermute | solution.py:162
  748.8 50.4 %collective-permute-start.91 = (bf16[256,704]{0,1:T(8,128)(2,1)S(1)}, bf16[256,704]{0,1:T(8,128)(2,1)S(1)}, u32[]{:S(2)}, u32[]{:S(2)}) collective-permute-start(bf16[256,704]{0,1:T(8,128)(2,1)S(1)} %fusion.71), channel_id=1, source_target_pairs={{8,0},{16,8},{24,16},{28,24},{20,28},{12,20},{4,12},{0,4},{9,1},{1... | collective-permute-start | bytes 1081352 | tf_op jit(solution)/shard_map/ppermute | solution.py:148
  756.8 69.1 %collective-permute-start.115 = (bf16[256,1536]{1,0:T(8,128)(2,1)S(1)}, bf16[256,1536]{1,0:T(8,128)(2,1)S(1)}, u32[]{:S(2)}, u32[]{:S(2)}) collective-permute-start(bf16[256,1536]{1,0:T(8,128)(2,1)S(1)} %fusion.31), channel_id=1, source_target_pairs={{0,8},{8,16},{16,24},{24,28},{28,20},{20,12},{12,4},{4,0},{1,9},{9... | collective-permute-start | bytes 2359304 | tf_op jit(solution)/shard_map/ppermute | solution.py:147
  818.7 63.9 %collective-permute-start.86 = (bf16[256,704]{0,1:T(8,128)(2,1)}, bf16[256,704]{0,1:T(8,128)(2,1)}, u32[]{:S(2)}, u32[]{:S(2)}) collective-permute-start(bf16[256,704]{0,1:T(8,128)(2,1)} %fusion.75), channel_id=1, source_target_pairs={{0,8},{8,16},{16,24},{24,28},{28,20},{20,12},{12,4},{4,0},{1,9},{9... | collective-permute-start | bytes 1081352 | tf_op jit(solution)/shard_map/ppermute | solution.py:147
  824.9 60.1 %collective-permute-start.93 = (bf16[256,704]{0,1:T(8,128)(2,1)}, bf16[256,704]{0,1:T(8,128)(2,1)}, u32[]{:S(2)}, u32[]{:S(2)}) collective-permute-start(bf16[256,704]{0,1:T(8,128)(2,1)} %fusion.69), channel_id=1, source_target_pairs={{8,0},{16,8},{24,16},{28,24},{20,28},{12,20},{4,12},{0,4},{9,1},{1... | collective-permute-start | bytes 1081352 | tf_op jit(solution)/shard_map/ppermute | solution.py:148
  827.6 70.3 %collective-permute-start.116 = (bf16[256,1536]{1,0:T(8,128)(2,1)S(1)}, bf16[256,1536]{1,0:T(8,128)(2,1)S(1)}, u32[]{:S(2)}, u32[]{:S(2)}) collective-permute-start(bf16[256,1536]{1,0:T(8,128)(2,1)S(1)} %fusion.30), channel_id=1, source_target_pairs={{0,8},{8,16},{16,24},{24,28},{28,20},{20,12},{12,4},{4,0},{1,9},{9... | collective-permute-start | bytes 2359304 | tf_op jit(solution)/shard_map/ppermute | solution.py:147
  830.3 70.3 %collective-permute-start.123 = (bf16[256,1536]{1,0:T(8,128)(2,1)S(1)}, bf16[256,1536]{1,0:T(8,128)(2,1)}, u32[]{:S(2)}, u32[]{:S(2)}) collective-permute-start(bf16[256,1536]{1,0:T(8,128)(2,1)S(1)} %fusion.24), channel_id=1, source_target_pairs={{8,0},{16,8},{24,16},{28,24},{20,28},{12,20},{4,12},{0,4},{9,1},{1... | collective-permute-start | bytes 2359304 | tf_op jit(solution)/shard_map/ppermute | solution.py:148
  839.6 48.0 %collective-permute-start.80 = (bf16[128,2048]{1,0:T(8,128)(2,1)}, bf16[128,2048]{1,0:T(8,128)(2,1)S(1)}, u32[]{:S(2)}, u32[]{:S(2)}) collective-permute-start(bf16[128,2048]{1,0:T(8,128)(2,1)} %shard_map.337), channel_id=1, source_target_pairs={{0,2},{1,3},{2,0},{3,1},{4,6},{5,7},{6,4},{7,5},{8,10},{9,11},{10,... | collective-permute-start | bytes 1572872 | tf_op jit(solution)/shard_map/ppermute | solution.py:182
  (234 other events, 4875.9 us)
Sparse Core Ops, SparseCore 0:
  684.0 106.8 all-reduce.13

commit v2 on v1

--- a/solution.py
+++ b/solution.py
@@ -125,6 +125,7 @@
         self.place = [self.order.index(i) for i in range(count)]
         self.forth = [(self.order[i], self.order[(i + 1) % count]) for i in range(count)]
         self.back = [(there, here) for here, there in self.forth]
+        self.sent, self.awaited = [], []
 
     def tables(self):
         here = jnp.asarray(self.place, jnp.int32)[lax.axis_index("seq")]
@@ -133,36 +134,181 @@
         to_plain = (here - jnp.asarray(self.place, jnp.int32)) % self.count
         return to_ring, to_plain
 
-    def gather(self, forth_piece, back_piece):
-        forth, back = [forth_piece], [back_piece]
-        for _ in range(self.count - 1):
-            forth.append(lax.ppermute(forth[-1], "seq", self.forth))
-            back.append(lax.ppermute(back[-1], "seq", self.back))
-        return forth, [back[-k % self.count] for k in range(self.count)]
-
-    def scatter(self, forth_slabs, back_slabs):
-        count = self.count
-        forth, back = forth_slabs[1].astype(bf16), back_slabs[count - 1].astype(bf16)
-        for step in range(2, count + 1):
-            forth = lax.ppermute(forth, "seq", self.forth).astype(f32) + forth_slabs[step % count]
-            back = lax.ppermute(back, "seq", self.back).astype(f32) + back_slabs[count - step]
-            if step < count:
-                forth, back = forth.astype(bf16), back.astype(bf16)
-        return forth, back
-
-
-def halves_summed(partial):
-    count, mine = lax.axis_size("fsdp"), lax.axis_index("fsdp")
-    bit = 1
-    while bit < count:
-        half = partial.shape[0] // 2
-        upper = (mine // bit) % 2
-        kept = lax.dynamic_slice_in_dim(partial, upper * half, half, 0)
-        sent = lax.dynamic_slice_in_dim(partial, (1 - upper) * half, half, 0).astype(bf16)
-        got = lax.ppermute(sent, "fsdp", [(i, i ^ bit) for i in range(count)])
-        partial = kept + got.astype(f32)
-        bit *= 2
-    return partial
+    def send(self, forth, back):
+        earlier = list(self.sent[-2]) if len(self.sent) > 1 else []
+        if earlier or self.awaited:
+            forth, back = lax.optimization_barrier((forth, back, *earlier, *self.awaited))[:2]
+        self.awaited = []
+        self.sent.append(
+            (lax.ppermute(forth, "seq", self.forth), lax.ppermute(back, "seq", self.back))
+        )
+        return self.sent[-1]
+
+    def first(self, *values):
+        self.awaited.extend(values)
+
+    def then(self, value, under_way=1):
+        if len(self.sent) <= under_way:
+            return value
+        return lax.optimization_barrier((value, *self.sent[-1 - under_way]))[0]
+
+
+class Gather:
+    def __init__(self, ring, forth, back):
+        self.ring, self.forth, self.back = ring, [forth], [back]
+
+    def step(self):
+        forth, back = self.ring.send(self.forth[-1], self.back[-1])
+        self.forth.append(forth)
+        self.back.append(back)
+
+    def slabs(self):
+        count = self.ring.count
+        return self.forth, [self.back[-k % count] for k in range(count)]
+
+
+class Scatter:
+    def __init__(self, ring, forth_slab, back_slab):
+        self.ring, self.forth_slab, self.back_slab = ring, forth_slab, back_slab
+        self.at = 1
+        self.forth = forth_slab(1).astype(bf16)
+        self.back = back_slab(ring.count - 1).astype(bf16)
+
+    def step(self):
+        count = self.ring.count
+        forth, back = self.ring.send(self.forth, self.back)
+        self.at += 1
+        self.forth = forth.astype(f32) + self.forth_slab(self.at % count)
+        self.back = back.astype(f32) + self.back_slab(count - self.at)
+        if self.at < count:
+            self.forth, self.back = self.forth.astype(bf16), self.back.astype(bf16)
+
+    def sums(self):
+        return self.forth, self.back
+
+
+class PlainGather:
+    def __init__(self, ring, forth, back):
+        self.pieces = (forth, back)
+
+    def step(self):
+        pass
+
+    def slabs(self):
+        return tuple(list(lax.all_gather(piece, "seq")) for piece in self.pieces)
+
+
+class PlainScatter:
+    def __init__(self, ring, forth_slab, back_slab):
+        self.terms = (forth_slab, back_slab)
+
+    def step(self):
+        pass
+
+    def sums(self):
+        count = lax.axis_size("seq")
+        return tuple(
+            lax.psum_scatter(
+                jnp.concatenate([term(k) for k in range(count)], 0),
+                "seq",
+                scatter_dimension=0,
+                tiled=True,
+            )
+            for term in self.terms
+        )
+
+
+def in_turn(*transfers):
+    for transfer in transfers:
+        transfer.step()
+
+
+def swapped(values, axis, bit):
+    return lax.ppermute(values, axis, [(i, i ^ bit) for i in range(lax.axis_size(axis))])
+
+
+class Exchange:
+    def __init__(self, ring, values, axis):
+        self.ring, self.values, self.axis = ring, values, axis
+        self.got = None
+        count = lax.axis_size(axis)
+        self.bits = [1 << i for i in range(count.bit_length() - 1)]
+        self.stages = self.plan()
+
+    def upper(self, bit):
+        return (lax.axis_index(self.axis) // bit) % 2 > 0
+
+    def step(self, under_way=None):
+        if self.got is not None:
+            got, bit, end = self.got
+            self.got = None
+            end(got if under_way is None else self.ring.then(got, under_way), bit)
+        if self.stages:
+            start, end, bit = self.stages.pop(0)
+            self.got = (swapped(start(bit), self.axis, bit), bit, end)
+        return self.values
+
+    def run(self, under_way=None):
+        while self.stages or self.got is not None:
+            self.step(under_way)
+        return self.values
+
+    def start_half(self, bit):
+        half = self.values.shape[0] // 2
+        kept, sent = [
+            jnp.where(self.upper(bit) == side, self.values[half:], self.values[:half])
+            for side in (True, False)
+        ]
+        self.values = kept
+        return sent.astype(bf16)
+
+    def end_half(self, got, bit):
+        self.values = self.values.astype(f32) + got.astype(f32)
+
+    def start_join(self, bit):
+        return self.values
+
+    def end_join(self, got, bit):
+        upper, own = self.upper(bit), self.values
+        self.values = jnp.concatenate([jnp.where(upper, got, own), jnp.where(upper, own, got)], 0)
+
+    def end_sum(self, got, bit):
+        self.values = self.values + got
+
+    def halving(self):
+        return [(self.start_half, self.end_half, bit) for bit in self.bits]
+
+    def joining(self):
+        return [(self.start_join, self.end_join, bit) for bit in reversed(self.bits)]
+
+
+class Halves(Exchange):
+    def plan(self):
+        return self.halving()
+
+
+class Joined(Exchange):
+    def plan(self):
+        return self.joining()
+
+
+class Everywhere(Exchange):
+    def plan(self):
+        stages = self.halving() + self.joining()
+        middle = len(self.bits)
+
+        def start_first_join(bit):
+            self.values = self.values.astype(bf16)
+            return self.values
+
+        if stages:
+            stages[middle] = (start_first_join, self.end_join, stages[middle][2])
+        return stages
+
+
+class SmallSum(Exchange):
+    def plan(self):
+        return [(self.start_join, self.end_sum, bit) for bit in self.bits]
 
 
 def own_rows(values):
@@ -192,14 +338,43 @@
     return lax.ppermute(block, "seq", route)
 
 
-def state_at_entry(prods, states, sign):
-    pair = passed_along(jnp.stack([prods, states], 0), sign)
-    distance = 1
-    while distance < lax.axis_size("seq"):
-        earlier = passed_along(pair, sign * distance)
-        pair = jnp.stack([pair[0] * earlier[0], pair[1] + pair[0] * earlier[1]], 0)
-        distance *= 2
-    return pair[1]
+def joined_maps(earlier, later):
+    return jnp.stack([earlier[0] * later[0], later[1] + later[0] * earlier[1]], 0)
+
+
+class Entry:
+    def __init__(self, prods, states, sign):
+        self.pair, self.sign = jnp.stack([prods, states], 0), sign
+        self.count = lax.axis_size("seq")
+        self.direct = self.count <= ring_limit and self.count % 2 == 0
+        if self.direct:
+            self.other = swapped(self.pair, "seq", 1)
+
+    def between(self, hold):
+        if not self.direct:
+            return
+        self.other = hold(self.other)
+        self.second = lax.axis_index("seq") % 2 == (1 if self.sign > 0 else 0)
+        earlier = jnp.where(self.second, self.other, self.pair)
+        later = jnp.where(self.second, self.pair, self.other)
+        both = joined_maps(earlier, later)
+        self.parts = [
+            passed_along(both, self.sign * distance) for distance in range(self.count - 2, 0, -2)
+        ]
+
+    def state(self, hold):
+        if self.direct:
+            parts = [hold(self.parts[0])] + self.parts[1:]
+            state = parts[0][1]
+            for part in parts[1:]:
+                state = part[1] + part[0] * state
+            return jnp.where(self.second, self.other[1] + self.other[0] * state, state)
+        pair = passed_along(self.pair, self.sign)
+        distance = 1
+        while distance < self.count:
+            pair = joined_maps(passed_along(pair, self.sign * distance), pair)
+            distance *= 2
+        return pair[1]
 
 
 def block_diagonal(blocks):
@@ -207,6 +382,10 @@
     return sum(
         jnp.pad(blocks[j], ((j * width, (count - 1 - j) * width),) * 2) for j in range(count)
     )
+
+
+def rows_joined(slab_pairs):
+    return jnp.concatenate([part for pair in zip(*slab_pairs) for part in pair], 0)
 
 
 def diagonal_blocks(square, count):
@@ -242,9 +421,11 @@
     units, hidden = conv_bias.shape[0], down_weight.shape[0]
     rows = batches * length
     ringed = count <= ring_limit
+    half = slab // 2
     out_turned, down_turned = out_weight.T, down_weight.T
+    ring = Ring(count)
     if ringed:
-        ring = Ring(count)
+        gather, scatter = functools.partial(Gather, ring), functools.partial(Scatter, ring)
         to_ring, to_plain = ring.tables()
 
         def moved(values, dtype):
@@ -259,43 +440,8 @@
         def gain_restored(gain):
             return gain.reshape(count, slab)[to_plain].reshape(width)
 
-        def gather(forth_piece, back_piece):
-            forth, back = ring.gather(forth_piece, back_piece)
-            return jnp.concatenate(forth, 0), jnp.concatenate(back, 0)
-
-        def gather_rows(piece):
-            forth, back = ring.gather(piece[: slab // 2], piece[slab // 2 :])
-            return jnp.concatenate([part for pair in zip(forth, back) for part in pair], 0)
-
-        def gather_columns(piece):
-            middle = piece.shape[1] // 2
-            forth, back = ring.gather(piece[:, :middle], piece[:, middle:])
-            return jnp.concatenate(
-                [jnp.concatenate(pair, 1) for pair in zip(forth, back)], 0
-            )
-
-        def slabs_of(whole):
-            return [whole[k * slab : (k + 1) * slab] for k in range(count)]
-
-        def scatter(forth_whole, back_whole):
-            return ring.scatter(slabs_of(forth_whole), slabs_of(back_whole))
-
-        def scatter_rows(whole):
-            pieces = slabs_of(whole)
-            parts = ring.scatter(
-                [piece[: slab // 2] for piece in pieces], [piece[slab // 2 :] for piece in pieces]
-            )
-            return jnp.concatenate(parts, 0)
-
-        def scatter_columns(whole):
-            middle = whole.shape[1] // 2
-            pieces = slabs_of(whole)
-            parts = ring.scatter(
-                [piece[:, :middle] for piece in pieces], [piece[:, middle:] for piece in pieces]
-            )
-            return jnp.concatenate(parts, 1)
-
     else:
+        gather, scatter = functools.partial(PlainGather, ring), functools.partial(PlainScatter, ring)
 
         def moved(values, dtype):
             return values.astype(dtype)
@@ -307,42 +453,48 @@
 
         gain_restored = gain_moved
 
-        def gather_rows(piece):
-            return lax.all_gather(piece, "seq", axis=0, tiled=True)
-
-        gather_columns = gather_rows
-
-        def gather(forth_piece, back_piece):
-            return gather_rows(forth_piece), gather_rows(back_piece)
-
-        def scatter_rows(whole):
-            return lax.psum_scatter(whole, "seq", scatter_dimension=0, tiled=True)
-
-        scatter_columns = scatter_rows
-
-        def scatter(forth_whole, back_whole):
-            return scatter_rows(forth_whole), scatter_rows(back_whole)
-
-    branch_all, inner_all = gather(branch_weight, inner_weight)
-    out_all = gather_rows(out_turned)
-    gate_all, up_all = gather(gate_weight, up_weight)
-    down_all = gather_columns(down_turned)
-
+    def slab_dots(turned, right, first=0, rows=slab):
+        def term(k):
+            start = k * slab + first
+            return dot_nn(turned[start : start + rows], right)
+
+        return term
+
+    steps = count - 1
+    front_weights = gather(branch_weight, inner_weight)
+    out_weights = gather(out_turned[:half], out_turned[half:])
+    mlp_weights = gather(gate_weight, up_weight)
+    down_weights = gather(down_turned[:half], down_turned[half:])
+    in_turn(front_weights, out_weights)
+    tokens_low = moved(tokens.reshape(rows, width), bf16)
+    ring.first(tokens_low)
+    in_turn(front_weights, out_weights)
     gain_one = gain_moved(norm_gain.astype(f32))
     gain_two = gain_moved(mlp_norm_gain.astype(f32))
+    values = ring.then(tokens_low, 2).astype(f32)
+    normed = (values * inverse_rms(values) * gain_one).astype(bf16)
+    ring.first(normed)
+    in_turn(front_weights, out_weights)
+    gate_square, input_square = block_diagonal(gate_blocks), block_diagonal(input_blocks)
+    ring.first(gate_square, input_square)
+    in_turn(front_weights, out_weights)
+    cot_low = moved(ring.then(cotangent, 2).reshape(rows, width), bf16)
+    ring.first(cot_low)
+    for _ in range(steps - 4):
+        in_turn(front_weights, out_weights)
+    branch_all, inner_all = (jnp.concatenate(slabs, 0) for slabs in front_weights.slabs())
+    out_all = rows_joined(out_weights.slabs())
+
     taps = conv_weight.astype(f32)
     decay = decay_param.astype(f32)
-    gate_square, input_square = block_diagonal(gate_blocks), block_diagonal(input_blocks)
     fresh_start = resets[:, :, None] > 0
-
-    tokens_low = moved(tokens.reshape(rows, width), bf16)
-    cot_low = moved(cotangent.reshape(rows, width), bf16)
-    values = tokens_low.astype(f32)
-    normed = (values * inverse_rms(values) * gain_one).astype(bf16)
+    in_turn(mlp_weights)
     inner_low = dot_nn(normed, inner_all).astype(bf16).reshape(batches, length, units)
     branch_pre = dot_nn(normed, branch_all).reshape(batches, length, units)
     edge_rows = passed_along(inner_low[:, -3:], 1)
-    padded = jnp.concatenate([edge_rows, inner_low], 1).astype(f32)
+    ring.first(inner_low, branch_pre)
+    in_turn(down_weights)
+    padded = jnp.concatenate([ring.then(edge_rows, 2), inner_low], 1).astype(f32)
     conv_sum = conv_bias.astype(f32) + taps[0] * padded[:, 3:] + taps[1] * padded[:, 2:-1]
     conv_sum = conv_sum + taps[2] * padded[:, 1:-2] + taps[3] * padded[:, :-3]
     conv_low = conv_sum.astype(bf16)
@@ -357,43 +509,88 @@
         return gate_math(gate_pre, input_pre, conv_value, decay, fresh_start)
 
     carries, drives = gates(gate_pre, input_pre, conv_value, decay)
-    prods, local_state = local_scan(carries, drives, False)
-    state_in = state_at_entry(prods[:, -1:], local_state[:, -1:], 1)
-    states = local_state + prods * state_in
+    ring.first(carries, drives)
+    in_turn(mlp_weights)
+    prods, local_state = local_scan(ring.then(carries, 2), drives, False)
+    entry = Entry(prods[:, -1:], local_state[:, -1:], 1)
+    ring.first(prods)
+    in_turn(down_weights)
+    entry.between(ring.then)
+    in_turn(mlp_weights)
+    state_in = entry.state(lambda part: ring.then(part, 1))
+    ring.first(state_in)
+    in_turn(down_weights)
+    states = local_state + prods * ring.then(state_in, 2)
 
     branch, branch_pull = jax.vjp(gelu_tanh, branch_pre)
     mixed_low = (states * branch).astype(bf16).reshape(rows, units)
-    own_middle = own_rows(tokens_low).astype(f32) + halves_summed(dot_nt(mixed_low, out_all))
+    middle_sum = Halves(ring, dot_nt(mixed_low, out_all), "fsdp")
+    middle_sum.step()
+    ring.first(middle_sum.step())
+    in_turn(mlp_weights, down_weights)
+    own_middle = own_rows(tokens_low).astype(f32) + middle_sum.run(2)
     scale_two = inverse_rms(own_middle)
     unit_two = own_middle * scale_two
-    normed_two = halves_joined((unit_two * gain_two).astype(bf16))
+    normed_join = Joined(ring, (unit_two * gain_two).astype(bf16), "fsdp")
+    ring.first(normed_join.step())
+    in_turn(mlp_weights)
+    normed_join.step(1)
+    normed_two = normed_join.run()
+    ring.first(normed_two)
+    in_turn(down_weights, mlp_weights)
+    in_turn(*[mlp_weights] * (steps - 6), *[down_weights] * (steps - 5))
+    gate_all, up_all = (jnp.concatenate(slabs, 0) for slabs in mlp_weights.slabs())
+    down_all = rows_joined(down_weights.slabs())
 
     gate_mlp = dot_nn(normed_two, gate_all)
     up_mlp = dot_nn(normed_two, up_all)
     activated, act_pull = jax.vjp(gated_product, gate_mlp, up_mlp)
     hidden_low = activated.astype(bf16)
-    down_grad = scatter_columns(dot_tn(cot_low, hidden_low)).T
-    grad_gate_mlp, grad_up_mlp = act_pull(dot_nn(cot_low, down_all))
+    down_grads = scatter(
+        slab_dots(cot_low.T, hidden_low, 0, half), slab_dots(cot_low.T, hidden_low, half, half)
+    )
+    in_turn(down_grads)
+    grad_gate_mlp, grad_up_mlp = act_pull(dot_nn(ring.then(cot_low, 0), down_all))
     gate_mlp_low, up_mlp_low = grad_gate_mlp.astype(bf16), grad_up_mlp.astype(bf16)
-    gate_grad, up_grad = scatter(dot_tn(normed_two, gate_mlp_low), dot_tn(normed_two, up_mlp_low))
-    own_back = halves_summed(dot_nt(gate_mlp_low, gate_all) + dot_nt(up_mlp_low, up_all))
-    own_mixed = own_middle + halves_summed(dot_nt(hidden_low, down_all))
-    mixed = halves_joined(restored(own_mixed, bf16)).astype(f32).reshape(tokens.shape)
-
+    in_turn(down_grads)
+    ring.first(gate_mlp_low, up_mlp_low)
+    in_turn(down_grads)
+    mlp_grads = scatter(
+        slab_dots(normed_two.T, gate_mlp_low), slab_dots(normed_two.T, up_mlp_low)
+    )
+    in_turn(mlp_grads, down_grads)
+    gate_mlp_low, up_mlp_low = lax.optimization_barrier(
+        (ring.then(gate_mlp_low, 2), up_mlp_low)
+    )
+    back_sum = Halves(
+        ring, dot_nt(gate_mlp_low, gate_all) + dot_nt(up_mlp_low, up_all), "fsdp"
+    )
+    back_sum.step()
+    ring.first(back_sum.step())
+    in_turn(mlp_grads, down_grads)
+    own_back = back_sum.run(2)
     gain_two_grad = jnp.sum(own_back * unit_two, 0)
     weighted = own_back * gain_two
     own_grad = own_rows(cot_low).astype(f32) + scale_two * (
         weighted - unit_two * jnp.mean(weighted * unit_two, axis=-1, keepdims=True)
     )
-    middle_low = halves_joined(own_grad.astype(bf16))
-
-    out_grad = scatter_rows(dot_tn(middle_low, mixed_low)).T
+    middle_join = Joined(ring, own_grad.astype(bf16), "fsdp")
+    ring.first(middle_join.step())
+    in_turn(mlp_grads, down_grads)
+    middle_join.step(2)
+    middle_low = middle_join.run()
+
     grad_mixed = dot_nn(middle_low, out_all).reshape(batches, length, units)
     (grad_branch_pre,) = branch_pull(grad_mixed * states)
     branch_low = grad_branch_pre.astype(bf16).reshape(rows, units)
     following = jnp.concatenate([carries[:, 1:], jnp.ones_like(carries[:, :1])], 1)
     tail_prods, local_adjoint = local_scan(following, grad_mixed * branch, True)
-    adjoint_in = state_at_entry(prods[:, -1:], carries[:, :1] * local_adjoint[:, :1], -1)
+    entry = Entry(prods[:, -1:], carries[:, :1] * local_adjoint[:, :1], -1)
+    ring.first(local_adjoint, branch_low)
+    in_turn(mlp_grads)
+    entry.between(ring.then)
+    in_turn(down_grads)
+    adjoint_in = entry.state(lambda part: ring.then(part, 1))
     adjoint = local_adjoint + tail_prods * adjoint_in
     state_before = jnp.concatenate([state_in, states[:, :-1]], 1)
     _, gate_pull = jax.vjp(gates, gate_pre, input_pre, conv_value, decay)
@@ -402,11 +599,10 @@
     )
     gate_low = grad_gate_pre.astype(bf16).reshape(rows, units)
     input_low = grad_input_pre.astype(bf16).reshape(rows, units)
+    ring.first(gate_low, input_low)
+    in_turn(mlp_grads)
     back_conv = dot_nt(gate_low, gate_square) + dot_nt(input_low, input_square)
     grad_conv = grad_conv + back_conv.reshape(batches, length, units)
-    block_count = gate_blocks.shape[0]
-    gate_blocks_grad = diagonal_blocks(dot_tn(conv_flat, gate_low), block_count)
-    input_blocks_grad = diagonal_blocks(dot_tn(conv_flat, input_low), block_count)
 
     border = jnp.zeros((batches, 3, units), f32)
     spread = jnp.concatenate([border, grad_conv, border], 1)
@@ -414,23 +610,40 @@
     grad_padded = taps[0] * spread[:, :stop] + taps[1] * spread[:, 1 : stop + 1]
     grad_padded = grad_padded + taps[2] * spread[:, 2 : stop + 2] + taps[3] * spread[:, 3:]
     returned = passed_along(grad_padded[:, :3], -1)
+    ring.first(grad_padded)
+    in_turn(mlp_grads)
     grad_inner = jnp.concatenate(
-        [grad_padded[:, 3:-3], grad_padded[:, -3:] + returned], 1
+        [grad_padded[:, 3:-3], grad_padded[:, -3:] + ring.then(returned)], 1
     )
     inner_grad_low = grad_inner.astype(bf16).reshape(rows, units)
-    branch_grad, inner_grad = scatter(dot_tn(normed, branch_low), dot_tn(normed, inner_grad_low))
-    own_front = halves_summed(dot_nt(branch_low, branch_all) + dot_nt(inner_grad_low, inner_all))
-
-    own_values = own_rows(tokens_low).astype(f32)
-    scale_one = inverse_rms(own_values)
-    unit_one = own_values * scale_one
-    gain_one_grad = jnp.sum(own_front * unit_one, 0)
-    weighted = own_front * gain_one
-    own_tokens = own_grad + scale_one * (
-        weighted - unit_one * jnp.mean(weighted * unit_one, axis=-1, keepdims=True)
-    )
-    tokens_grad = halves_joined(restored(own_tokens, bf16)).astype(f32).reshape(tokens.shape)
-
+    in_turn(*[mlp_grads] * (steps - 6))
+    out_grads = scatter(
+        slab_dots(middle_low.T, mixed_low, 0, half), slab_dots(middle_low.T, mixed_low, half, half)
+    )
+    front_grads = scatter(
+        slab_dots(normed.T, branch_low), slab_dots(normed.T, inner_grad_low)
+    )
+    in_turn(out_grads, front_grads)
+    front_sum = Halves(
+        ring,
+        dot_nt(ring.then(branch_low), branch_all) + dot_nt(inner_grad_low, inner_all),
+        "fsdp",
+    )
+    front_sum.step()
+    front_sum.step()
+
+    block_count = gate_blocks.shape[0]
+    conv_again = ring.then(conv_flat)
+    block_grads = jnp.concatenate(
+        [
+            diagonal_blocks(dot_tn(conv_again, gate_low), block_count),
+            diagonal_blocks(dot_tn(conv_again, input_low), block_count),
+        ],
+        0,
+    )
+    block_width = block_grads.shape[-1]
+    block_sum = Everywhere(ring, block_grads.reshape(-1, block_width), "seq")
+    block_sum.step()
     taps_grad = jnp.stack(
         [jnp.sum(grad_conv * padded[:, 3 - k : 3 - k + length], (0, 1)) for k in range(4)], 0
     )
@@ -444,11 +657,55 @@
         ],
         0,
     )
-    small, gate_blocks_grad, input_blocks_grad = lax.psum(
-        (small, gate_blocks_grad, input_blocks_grad), "seq"
+    in_turn(out_grads, front_grads)
+    block_sum.step(1)
+    own_front = front_sum.run(1)
+    own_values = own_rows(tokens_low).astype(f32)
+    scale_one = inverse_rms(own_values)
+    unit_one = own_values * scale_one
+    gain_one_grad = jnp.sum(own_front * unit_one, 0)
+    weighted = own_front * gain_one
+    own_tokens = own_grad + scale_one * (
+        weighted - unit_one * jnp.mean(weighted * unit_one, axis=-1, keepdims=True)
     )
     gains = jnp.stack([gain_restored(gain_one_grad), gain_restored(gain_two_grad)], 0)
-    gains = lax.psum(gains, ("seq", "fsdp"))
+    small_sum = SmallSum(ring, jnp.concatenate([small.reshape(-1), gains.reshape(-1)]), "seq")
+    tokens_join = Joined(ring, restored(own_tokens, bf16), "fsdp")
+    tokens_join.step()
+    small_sum.step()
+    in_turn(out_grads, front_grads)
+    block_sum.step(1)
+    small_sum.step(1)
+    tokens_join.step(1)
+    tokens_grad = tokens_join.run().astype(f32).reshape(tokens.shape)
+    in_turn(out_grads, front_grads)
+    block_sum.step(1)
+    small_sum.step(1)
+    mixed_sum = Halves(ring, dot_nt(ring.then(hidden_low), down_all), "fsdp")
+    mixed_sum.step()
+    mixed_sum.step()
+    in_turn(out_grads, front_grads)
+    block_sum.step(1)
+    small = small_sum.run(1)
+    gains = small[8 * units :]
+    small = small[: 8 * units].reshape(8, units)
+    gains_sum = SmallSum(ring, gains, "fsdp")
+    gains_sum.step()
+    mixed_join = Joined(ring, restored(own_middle + mixed_sum.run(1), bf16), "fsdp")
+    mixed_join.step()
+    in_turn(out_grads, front_grads)
+    block_sum.step(1)
+    gains_sum.step(1)
+    mixed_join.step(1)
+    mixed = mixed_join.run().astype(f32).reshape(tokens.shape)
+    in_turn(*[out_grads, front_grads] * (steps - 6))
+    block_grads = block_sum.run(1).astype(f32)
+    block_grads = block_grads.reshape(2, block_count, block_width, block_width)
+    gains = gains_sum.run(1).reshape(2, width)
+    branch_grad, inner_grad = front_grads.sums()
+    gate_grad, up_grad = mlp_grads.sums()
+    out_grad = jnp.concatenate(out_grads.sums(), 0)
+    down_grad = jnp.concatenate(down_grads.sums(), 0)
     return (
         mixed,
         tokens_grad,
@@ -457,16 +714,16 @@
         inner_grad,
         small[:4],
         small[4],
-        gate_blocks_grad,
-        input_blocks_grad,
+        block_grads[0],
+        block_grads[1],
         small[5],
         small[6],
         small[7],
-        out_grad,
+        out_grad.T,
         gains[1],
         gate_grad,
         up_grad,
-        down_grad,
+        down_grad.T,
     )
 
 

time: 932 us -> 773 us (0.83)
  blocking collectives: 81.6 us -> 0 us
  waiting for transfers between devices: 359 us -> 320 us
  other arithmetic: 96.1 us -> 65.7 us
  between operations: 17.3 us -> 4.5 us
  matrix products: 98.3 us -> 110 us
  starting transfers between devices: 161 us -> 150 us
    psum x2 -> x0, blocking collectives: 81.6 us -> none  [the longest x1 41.4 us: local(): lax.psum((small, gate_blocks_grad, input_blocks_grad), 'seq')]
    dot_general x8 -> x72, matrix products: 27.9 us -> 85.4 us  [dot_nn(): return jnp.dot(left, right, preferred_element_type=f32)]
    convert_element_type x41 -> x19, other arithmetic: 48.8 us -> 15.2 us  [the longest x11 5.18 us: start_half(): return sent.astype(bf16)]
    dot_general x8 -> x2, matrix products: 30.2 us -> 1.53 us  [dot_tn(): lax.dot_general(left, right, (((0,), (0,)), ((), ())), preferred_element_...]
    ppermute x128 -> x141, waiting for transfers between devices: 342 us -> 316 us  [the longest x56 190 us: send(): lax.ppermute(forth, 'seq', self.forth)]
    dot_general x8, matrix products: 40.2 us -> 22.7 us  [dot_nt(): lax.dot_general(left, right, (((1,), (1,)), ((), ())), preferred_element_...]
    ppermute x10 -> x8, waiting for transfers between devices: 16.5 us -> 4.41 us  [passed_along(): return lax.ppermute(block, 'seq', route)]
    ppermute x10 -> x8, starting transfers between devices: 23.5 us -> 14.9 us  [passed_along(): return lax.ppermute(block, 'seq', route)]
  transfers between devices with their start and end apart: 139 -> 149, of which waited for: 48 -> 80; matrix products, arithmetic and copies ran while one was open for 22% -> 29% of each run, Pallas kernels for 3% -> 4%
where the time goes in v2:
time: 773 us; the launch traced here: 762 us
  waiting for transfers between devices  320 us (41%)
  starting transfers between devices  150 us (19%)
  matrix products  110 us (14%)
  local copies, waits for them, and re-layouts  83.8 us (11%)
  other arithmetic  65.7 us (8%)
  Pallas kernels  27.6 us (4%)
    ppermute x56, waiting for transfers between devices, send(): lax.ppermute(forth, 'seq', self.forth)  190 us
    dot_general x72, matrix products, dot_nn(): return jnp.dot(left, right, preferred_element_type=f32)  85.4 us
    ppermute x56, starting transfers between devices, send(): lax.ppermute(forth, 'seq', self.forth)  82.2 us
    ppermute x56, waiting for transfers between devices, send(): lax.ppermute(back, 'seq', self.back)  77.5 us
    unnamed x400, local copies, waits for them, and re-layouts  58.8 us
    ppermute x29, waiting for transfers between devices, swapped(): lax.ppermute(values, axis, [(i, i ^ bit) for i in range(lax.axis_size(axi...  48.3 us
    ppermute x56, starting transfers between devices, send(): lax.ppermute(back, 'seq', self.back)  36.7 us
    pallas_call x4, Pallas kernels, move_slabs(): pl.pallas_call(move_body, out_shape=jax.ShapeDtypeStruct((rows, width), d...  24.4 us
  transfers between devices with their start and end apart: 149, of which 80 were waited for; matrix products, arithmetic and copies ran while one was open for 29% of the time, Pallas kernels for 4%

profile of v2, /device:TPU:0, one launch (start us, length us, event | category | flops | bytes accessed | tf_op | source)
XLA Modules:
  0.0 761.7 jit_solution(723127001352033626)
XLA Ops:
  14.4 6.5 shard_map.332
  65.5 6.5 shard_map.333
  131.6 10.8 %collective-permute-done.29 = bf16[256,1536]{1,0:T(8,128)(2,1)S(1)} collective-permute-done((bf16[256,1536]{1,0:T(8,128)(2,1)}, bf16[256,1536]{1,0:T(8,128)(2,1)S(1)}, u32[]{:S(2)}, u32[]{:S(2)}) %collective-permute-start.29) | collective-permute-done | bytes 786464 | tf_op jit(solution)/shard_map/ppermute | solution.py:143
  153.5 9.9 %collective-permute-done.37 = bf16[128,1536]{0,1:T(8,128)(2,1)S(1)} collective-permute-done((bf16[128,1536]{0,1:T(8,128)(2,1)S(1)}, bf16[128,1536]{0,1:T(8,128)(2,1)S(1)}, u32[]{:S(2)}, u32[]{:S(2)}) %collective-permute-start.37) | collective-permute-done | bytes 393248 | tf_op jit(solution)/shard_map/ppermute | solution.py:143
  200.5 7.3 collective-permute-done.43
  216.8 7.8 %collective-permute-done.49 = bf16[256,1536]{1,0:T(8,128)(2,1)} collective-permute-done((bf16[256,1536]{1,0:T(8,128)(2,1)}, bf16[256,1536]{1,0:T(8,128)(2,1)}, u32[]{:S(2)}, u32[]{:S(2)}) %collective-permute-start.49) | collective-permute-done | bytes 786464 | tf_op jit(solution)/shard_map/ppermute | solution.py:143
  236.2 12.6 %collective-permute-done.51 = bf16[256,1536]{1,0:T(8,128)(2,1)} collective-permute-done((bf16[256,1536]{1,0:T(8,128)(2,1)}, bf16[256,1536]{1,0:T(8,128)(2,1)}, u32[]{:S(2)}, u32[]{:S(2)}) %collective-permute-start.51) | collective-permute-done | bytes 786464 | tf_op jit(solution)/shard_map/ppermute | solution.py:143
  254.8 14.3 %collective-permute-done.53 = bf16[256,1536]{1,0:T(8,128)(2,1)S(1)} collective-permute-done((bf16[256,1536]{1,0:T(8,128)(2,1)}, bf16[256,1536]{1,0:T(8,128)(2,1)S(1)}, u32[]{:S(2)}, u32[]{:S(2)}) %collective-permute-start.53) | collective-permute-done | bytes 786464 | tf_op jit(solution)/shard_map/ppermute | solution.py:143
  276.9 18.7 %collective-permute-done.57 = bf16[128,1536]{0,1:T(8,128)(2,1)S(1)} collective-permute-done((bf16[128,1536]{0,1:T(8,128)(2,1)}, bf16[128,1536]{0,1:T(8,128)(2,1)S(1)}, u32[]{:S(2)}, u32[]{:S(2)}) %collective-permute-start.57) | collective-permute-done | bytes 393248 | tf_op jit(solution)/shard_map/ppermute | solution.py:143
  301.5 15.2 %collective-permute-done.59 = bf16[256,1536]{1,0:T(8,128)(2,1)S(1)} collective-permute-done((bf16[256,1536]{1,0:T(8,128)(2,1)S(1)}, bf16[256,1536]{1,0:T(8,128)(2,1)S(1)}, u32[]{:S(2)}, u32[]{:S(2)}) %collective-permute-start.59) | collective-permute-done | bytes 786464 | tf_op jit(solution)/shard_map/ppermute | solution.py:143
  341.0 6.3 collective-permute-done.65
  357.2 9.8 %multiply_convert_fusion = (bf16[512,1536]{1,0:T(8,128)(2,1)S(1)}, bf16[512,1536]{1,0:T(8,128)(2,1)S(1)}) fusion(f32[512,1536]{1,0:T(8,128)} %copy-done.161, f32[512,1536]{1,0:T(8,128)} %get-tuple-element.446, bf16[512,2048]{1,0:T(8,128)(2,1)S(1)} %copy-done.39, bf16[2048,1536]{0,1:T(8,128)(2,1)S(1)} %constant_dynamic-update-slice_fusion.47), kind=kOutput, calls=%fused_computation.19 | convolution fusion | flops 3240099840 | bytes 17825792 | tf_op jit(solution)/shard_map/dot_general | solution.py:35
  372.5 6.3 collective-permute-done.69
  400.4 6.0 collective-permute-done.76
  406.8 18.0 %collective-permute-done.77 = bf16[128,1536]{1,0:T(8,128)(2,1)S(1)} collective-permute-done((bf16[128,1536]{1,0:T(8,128)(2,1)S(1)}, bf16[128,1536]{1,0:T(8,128)(2,1)S(1)}, u32[]{:S(2)}, u32[]{:S(2)}) %collective-permute-start.77) | collective-permute-done | bytes 393248 | tf_op jit(solution)/shard_map/ppermute | solution.py:143
  428.5 6.4 collective-permute-done.88
  462.4 6.9 collective-permute-done.81
  496.3 11.9 %collective-permute-done.87 = f32[2,2,1,704]{3,1,2,0:T(2,128)S(1)} collective-permute-done((f32[2,2,1,704]{3,1,2,0:T(2,128)S(1)}, f32[2,2,1,704]{3,1,2,0:T(2,128)S(1)}, u32[]{:S(2)}, u32[]{:S(2)}) %collective-permute-start.87) | collective-permute-done | bytes 11296 | tf_op jit(solution)/shard_map/ppermute | solution.py:227
  560.2 10.4 %collective-permute-done.97 = bf16[256,1536]{1,0:T(8,128)(2,1)S(1)} collective-permute-done((bf16[256,1536]{1,0:T(8,128)(2,1)S(1)}, bf16[256,1536]{1,0:T(8,128)(2,1)S(1)}, u32[]{:S(2)}, u32[]{:S(2)}) %collective-permute-start.97) | collective-permute-done | bytes 786464 | tf_op jit(solution)/shard_map/ppermute | solution.py:143
  596.1 7.6 collective-permute-done.143
  636.5 8.4 %collective-permute-done.112 = bf16[128,704]{0,1:T(8,128)(2,1)S(1)} collective-permute-done((bf16[128,704]{0,1:T(8,128)(2,1)S(1)}, bf16[128,704]{0,1:T(8,128)(2,1)S(1)}, u32[]{:S(2)}, u32[]{:S(2)}) %collective-permute-start.112) | collective-permute-done | bytes 180256 | tf_op jit(solution)/shard_map/ppermute | solution.py:143
  723.6 5.7 shard_map.336
  735.5 7.0 collective-permute-done.111
  746.1 5.9 collective-permute-done.141
  (922 shorter events, 530.9 us)
Async XLA Ops:
  5.5 36.4 %collective-permute-start.2 = (bf16[256,704]{0,1:T(8,128)(2,1)}, bf16[256,704]{0,1:T(8,128)(2,1)}, u32[]{:S(2)}, u32[]{:S(2)}) collective-permute-start(bf16[256,704]{0,1:T(8,128)(2,1)} %param.24), channel_id=1, source_target_pairs={{0,8},{8,16},{16,24},{24,28},{28,20},{20,12},{12,4},{4,0},{1,9},{9... | collective-permute-start | bytes 1081352 | tf_op jit(solution)/shard_map/ppermute | solution.py:143
  7.6 34.4 %collective-permute-start.3 = (bf16[256,704]{0,1:T(8,128)(2,1)}, bf16[256,704]{0,1:T(8,128)(2,1)}, u32[]{:S(2)}, u32[]{:S(2)}) collective-permute-start(bf16[256,704]{0,1:T(8,128)(2,1)} %param.25), channel_id=1, source_target_pairs={{8,0},{16,8},{24,16},{28,24},{20,28},{12,20},{4,12},{0,4},{9,1},{1... | collective-permute-start | bytes 1081352 | tf_op jit(solution)/shard_map/ppermute | solution.py:143
  76.4 49.3 %collective-permute-start.26 = (bf16[128,704]{0,1:T(8,128)(2,1)}, bf16[128,704]{0,1:T(8,128)(2,1)}, u32[]{:S(2)}, u32[]{:S(2)}) collective-permute-start(bf16[128,704]{0,1:T(8,128)(2,1)} %collective-permute-done.24), channel_id=1, source_target_pairs={{0,8},{8,16},{16,24},{24,28},{28,20},{20,12},{12,4},{4,0},{1,9},{9... | collective-permute-start | bytes 540680 | tf_op jit(solution)/shard_map/ppermute | solution.py:143
  143.0 24.4 %collective-permute-start.32 = (bf16[256,1536]{1,0:T(8,128)(2,1)S(1)}, bf16[256,1536]{1,0:T(8,128)(2,1)S(1)}, u32[]{:S(2)}, u32[]{:S(2)}) collective-permute-start(bf16[256,1536]{1,0:T(8,128)(2,1)S(1)} %collective-permute-done.29), channel_id=1, source_target_pairs={{0,8},{8,16},{16,24},{24,28},{28,20},{20,12},{12,4},{4,0},{1,9},{9... | collective-permute-start | bytes 2359304 | tf_op jit(solution)/shard_map/ppermute | solution.py:143
  198.5 26.1 %collective-permute-start.49 = (bf16[256,1536]{1,0:T(8,128)(2,1)}, bf16[256,1536]{1,0:T(8,128)(2,1)}, u32[]{:S(2)}, u32[]{:S(2)}) collective-permute-start(bf16[256,1536]{1,0:T(8,128)(2,1)} %copy-done.69), channel_id=1, source_target_pairs={{0,8},{8,16},{16,24},{24,28},{28,20},{20,12},{12,4},{4,0},{1,9},{9... | collective-permute-start | bytes 2359304 | tf_op jit(solution)/shard_map/ppermute | solution.py:143
  200.2 26.0 %collective-permute-start.50 = (bf16[256,1536]{1,0:T(8,128)(2,1)}, bf16[256,1536]{1,0:T(8,128)(2,1)S(1)}, u32[]{:S(2)}, u32[]{:S(2)}) collective-permute-start(bf16[256,1536]{1,0:T(8,128)(2,1)} %copy-done.65), channel_id=1, source_target_pairs={{8,0},{16,8},{24,16},{28,24},{20,28},{12,20},{4,12},{0,4},{9,1},{1... | collective-permute-start | bytes 2359304 | tf_op jit(solution)/shard_map/ppermute | solution.py:143
  252.6 45.2 %collective-permute-start.48 = (bf16[256,2048]{1,0:T(8,128)(2,1)S(1)}, bf16[256,2048]{1,0:T(8,128)(2,1)S(1)}, u32[]{:S(2)}, u32[]{:S(2)}) collective-permute-start(bf16[256,2048]{1,0:T(8,128)(2,1)S(1)} %pad_maximum_fusion.6), channel_id=1, source_target_pairs={{0,1},{1,0},{2,3},{3,2},{4,5},{5,4},{6,7},{7,6},{8,9},{9,8},{10,11... | collective-permute-start | bytes 3145736 | tf_op jit(solution)/shard_map/ppermute | solution.py:227
  270.3 26.1 %collective-permute-start.55 = (bf16[256,1536]{1,0:T(8,128)(2,1)S(1)}, bf16[256,1536]{1,0:T(8,128)(2,1)S(1)}, u32[]{:S(2)}, u32[]{:S(2)}) collective-permute-start(bf16[256,1536]{1,0:T(8,128)(2,1)S(1)} %collective-permute-done.53), channel_id=1, source_target_pairs={{0,8},{8,16},{16,24},{24,28},{28,20},{20,12},{12,4},{4,0},{1,9},{9... | collective-permute-start | bytes 2359304 | tf_op jit(solution)/shard_map/ppermute | solution.py:143
  271.0 25.4 %collective-permute-start.56 = (bf16[256,1536]{1,0:T(8,128)(2,1)S(1)}, bf16[256,1536]{1,0:T(8,128)(2,1)S(1)}, u32[]{:S(2)}, u32[]{:S(2)}) collective-permute-start(bf16[256,1536]{1,0:T(8,128)(2,1)S(1)} %collective-permute-done.54), channel_id=1, source_target_pairs={{8,0},{16,8},{24,16},{28,24},{20,28},{12,20},{4,12},{0,4},{9,1},{1... | collective-permute-start | bytes 2359304 | tf_op jit(solution)/shard_map/ppermute | solution.py:143
  299.0 30.5 %collective-permute-start.61 = (bf16[128,1536]{0,1:T(8,128)(2,1)S(1)}, bf16[128,1536]{0,1:T(8,128)(2,1)S(1)}, u32[]{:S(2)}, u32[]{:S(2)}) collective-permute-start(bf16[128,1536]{0,1:T(8,128)(2,1)S(1)} %collective-permute-done.57), channel_id=1, source_target_pairs={{0,8},{8,16},{16,24},{24,28},{28,20},{20,12},{12,4},{4,0},{1,9},{9... | collective-permute-start | bytes 1179656 | tf_op jit(solution)/shard_map/ppermute | solution.py:143
  300.5 29.0 %collective-permute-start.62 = (bf16[128,1536]{0,1:T(8,128)(2,1)S(1)}, bf16[128,1536]{0,1:T(8,128)(2,1)S(1)}, u32[]{:S(2)}, u32[]{:S(2)}) collective-permute-start(bf16[128,1536]{0,1:T(8,128)(2,1)S(1)} %collective-permute-done.58), channel_id=1, source_target_pairs={{8,0},{16,8},{24,16},{28,24},{20,28},{12,20},{4,12},{0,4},{9,1},{1... | collective-permute-start | bytes 1179656 | tf_op jit(solution)/shard_map/ppermute | solution.py:143
  371.3 27.6 %collective-permute-start.79 = (bf16[256,1536]{1,0:T(8,128)(2,1)S(1)}, bf16[256,1536]{1,0:T(8,128)(2,1)S(1)}, u32[]{:S(2)}, u32[]{:S(2)}) collective-permute-start(bf16[256,1536]{1,0:T(8,128)(2,1)S(1)} %convolution_convert_fusion.1), channel_id=1, source_target_pairs={{0,8},{8,16},{16,24},{24,28},{28,20},{20,12},{12,4},{4,0},{1,9},{9... | collective-permute-start | bytes 2359304 | tf_op jit(solution)/shard_map/ppermute | solution.py:143
  394.0 33.4 %collective-permute-start.71 = (bf16[256,2048]{1,0:T(8,128)(2,1)S(1)}, bf16[256,2048]{1,0:T(8,128)(2,1)S(1)}, u32[]{:S(2)}, u32[]{:S(2)}) collective-permute-start(bf16[256,2048]{1,0:T(8,128)(2,1)S(1)} %select_convert_fusion.2), channel_id=1, source_target_pairs={{0,1},{1,0},{2,3},{3,2},{4,5},{5,4},{6,7},{7,6},{8,9},{9,8},{10,11... | collective-permute-start | bytes 3145736 | tf_op jit(solution)/shard_map/ppermute | solution.py:227
  397.5 45.5 %collective-permute-start.80 = (bf16[256,1536]{1,0:T(8,128)(2,1)S(1)}, bf16[256,1536]{1,0:T(8,128)(2,1)S(1)}, u32[]{:S(2)}, u32[]{:S(2)}) collective-permute-start(bf16[256,1536]{1,0:T(8,128)(2,1)S(1)} %convolution_convert_fusion), channel_id=1, source_target_pairs={{8,0},{16,8},{24,16},{28,24},{20,28},{12,20},{4,12},{0,4},{9,1},{1... | collective-permute-start | bytes 2359304 | tf_op jit(solution)/shard_map/ppermute | solution.py:143
  398.2 26.6 %collective-permute-start.77 = (bf16[128,1536]{1,0:T(8,128)(2,1)S(1)}, bf16[128,1536]{1,0:T(8,128)(2,1)S(1)}, u32[]{:S(2)}, u32[]{:S(2)}) collective-permute-start(bf16[128,1536]{1,0:T(8,128)(2,1)S(1)} %add_convert_fusion.17), channel_id=1, source_target_pairs={{8,0},{16,8},{24,16},{28,24},{20,28},{12,20},{4,12},{0,4},{9,1},{1... | collective-permute-start | bytes 1179656 | tf_op jit(solution)/shard_map/ppermute | solution.py:143
  578.4 47.7 %collective-permute-start.127 = (bf16[256,1536]{1,0:T(8,128)(2,1)S(1)}, bf16[256,1536]{1,0:T(8,128)(2,1)S(1)}, u32[]{:S(2)}, u32[]{:S(2)}) collective-permute-start(bf16[256,1536]{1,0:T(8,128)(2,1)S(1)} %add_convert_fusion.1), channel_id=1, source_target_pairs={{0,8},{8,16},{16,24},{24,28},{28,20},{20,12},{12,4},{4,0},{1,9},{9... | collective-permute-start | bytes 2359304 | tf_op jit(solution)/shard_map/ppermute | solution.py:143
  580.5 47.0 %collective-permute-start.128 = (bf16[256,1536]{1,0:T(8,128)(2,1)S(1)}, bf16[256,1536]{1,0:T(8,128)(2,1)S(1)}, u32[]{:S(2)}, u32[]{:S(2)}) collective-permute-start(bf16[256,1536]{1,0:T(8,128)(2,1)S(1)} %add_convert_fusion), channel_id=1, source_target_pairs={{8,0},{16,8},{24,16},{28,24},{20,28},{12,20},{4,12},{0,4},{9,1},{1... | collective-permute-start | bytes 2359304 | tf_op jit(solution)/shard_map/ppermute | solution.py:143
  590.8 70.4 %collective-permute-start.116 = (bf16[256,2048]{1,0:T(8,128)(2,1)S(1)}, bf16[256,2048]{1,0:T(8,128)(2,1)S(1)}, u32[]{:S(2)}, u32[]{:S(2)}) collective-permute-start(bf16[256,2048]{1,0:T(8,128)(2,1)S(1)} %select_convert_fusion), channel_id=1, source_target_pairs={{0,1},{1,0},{2,3},{3,2},{4,5},{5,4},{6,7},{7,6},{8,9},{9,8},{10,11... | collective-permute-start | bytes 3145736 | tf_op jit(solution)/shard_map/ppermute | solution.py:227
  623.8 66.1 %collective-permute-start.107 = (bf16[256,2048]{1,0:T(8,128)(2,1)}, bf16[256,2048]{1,0:T(8,128)(2,1)}, u32[]{:S(2)}, u32[]{:S(2)}) collective-permute-start(bf16[256,2048]{1,0:T(8,128)(2,1)} %select_convert_fusion.1), channel_id=1, source_target_pairs={{0,1},{1,0},{2,3},{3,2},{4,5},{5,4},{6,7},{7,6},{8,9},{9,8},{10,11... | collective-permute-start | bytes 3145736 | tf_op jit(solution)/shard_map/ppermute | solution.py:227
  631.7 26.8 %collective-permute-start.129 = (bf16[256,704]{0,1:T(8,128)(2,1)S(1)}, bf16[256,704]{0,1:T(8,128)(2,1)S(1)}, u32[]{:S(2)}, u32[]{:S(2)}) collective-permute-start(bf16[256,704]{0,1:T(8,128)(2,1)S(1)} %convolution_convert_fusion.6), channel_id=1, source_target_pairs={{0,8},{8,16},{16,24},{24,28},{28,20},{20,12},{12,4},{4,0},{1,9},{9... | collective-permute-start | bytes 1081352 | tf_op jit(solution)/shard_map/ppermute | solution.py:143
  633.9 25.3 %collective-permute-start.130 = (bf16[256,704]{0,1:T(8,128)(2,1)S(1)}, bf16[256,704]{0,1:T(8,128)(2,1)S(1)}, u32[]{:S(2)}, u32[]{:S(2)}) collective-permute-start(bf16[256,704]{0,1:T(8,128)(2,1)S(1)} %convolution_convert_fusion.5), channel_id=1, source_target_pairs={{8,0},{16,8},{24,16},{28,24},{20,28},{12,20},{4,12},{0,4},{9,1},{1... | collective-permute-start | bytes 1081352 | tf_op jit(solution)/shard_map/ppermute | solution.py:143
  676.3 25.9 %collective-permute-start.134 = (bf16[256,704]{0,1:T(8,128)(2,1)S(1)}, bf16[256,704]{0,1:T(8,128)(2,1)S(1)}, u32[]{:S(2)}, u32[]{:S(2)}) collective-permute-start(bf16[256,704]{0,1:T(8,128)(2,1)S(1)} %add_convert_fusion.33), channel_id=1, source_target_pairs={{8,0},{16,8},{24,16},{28,24},{20,28},{12,20},{4,12},{0,4},{9,1},{1... | collective-permute-start | bytes 1081352 | tf_op jit(solution)/shard_map/ppermute | solution.py:143
  686.2 34.8 %collective-permute-start.118 = (bf16[128,2048]{1,0:T(8,128)(2,1)}, bf16[128,2048]{1,0:T(8,128)(2,1)S(1)}, u32[]{:S(2)}, u32[]{:S(2)}) collective-permute-start(bf16[128,2048]{1,0:T(8,128)(2,1)} %shard_map.337), channel_id=1, source_target_pairs={{0,2},{1,3},{2,0},{3,1},{4,6},{5,7},{6,4},{7,5},{8,10},{9,11},{10,... | collective-permute-start | bytes 1572872 | tf_op jit(solution)/shard_map/ppermute | solution.py:227
  693.9 27.1 %collective-permute-start.108 = (bf16[128,2048]{1,0:T(8,128)(2,1)}, bf16[128,2048]{1,0:T(8,128)(2,1)}, u32[]{:S(2)}, u32[]{:S(2)}) collective-permute-start(bf16[128,2048]{1,0:T(8,128)(2,1)} %select_convert_fusion.5), channel_id=1, source_target_pairs={{0,2},{1,3},{2,0},{3,1},{4,6},{5,7},{6,4},{7,5},{8,10},{9,11},{10,... | collective-permute-start | bytes 1572872 | tf_op jit(solution)/shard_map/ppermute | solution.py:227
  (293 other events, 4594.5 us)

commit v3 on v2

--- a/solution.py
+++ b/solution.py
@@ -375,6 +375,348 @@
             pair = joined_maps(passed_along(pair, self.sign * distance), pair)
             distance *= 2
         return pair[1]
+
+
+def ring_index(place, count):
+    place = lax.rem(place + 2 * count, count)
+    odd = place // (count // 2)
+    return (1 - odd) * (2 * place) + odd * (2 * count - 1 - 2 * place)
+
+
+def ring_place(index, count):
+    odd = lax.rem(index, 2)
+    return (1 - odd) * (index // 2) + odd * (count - 1 - index // 2)
+
+
+def partner(index, bit):
+    return index + bit * (1 - 2 * lax.rem(index // bit, 2))
+
+
+class Copies:
+    def __init__(self, send_sems, recv_sems):
+        self.send_sems, self.recv_sems = send_sems, recv_sems
+        self.started = []
+
+    def start(self, source, target, device):
+        slot = len(self.started)
+        copy = pltpu.make_async_remote_copy(
+            src_ref=source,
+            dst_ref=target,
+            send_sem=self.send_sems.at[slot],
+            recv_sem=self.recv_sems.at[slot],
+            device_id=device,
+            device_id_type=pl.DeviceIdType.MESH,
+        )
+        copy.start()
+        self.started.append(copy)
+        return copy
+
+    def end(self):
+        for copy in self.started:
+            copy.wait_send()
+
+
+def greet(devices):
+    barrier = pltpu.get_barrier_semaphore()
+    for device in devices:
+        pl.semaphore_signal(
+            barrier, inc=1, device_id=device, device_id_type=pl.DeviceIdType.MESH
+        )
+    pl.semaphore_wait(barrier, len(devices))
+
+
+tail_copies = 28 + 4 + 6 + 3 + 5
+
+
+def tail_body(
+    count,
+    emb_ref,
+    mixed_ref,
+    normed_ref,
+    branch_ref,
+    inner_ref,
+    branch_all_ref,
+    inner_all_ref,
+    values_ref,
+    grad_ref,
+    gain_ref,
+    gain_two_ref,
+    small_ref,
+    blocks_ref,
+    branch_out,
+    inner_out,
+    out_out,
+    tokens_out,
+    gains_out,
+    small_out,
+    blocks_out,
+    wide_sent,
+    wide_got,
+    slim_sent,
+    slim_got,
+    half_sent,
+    half_kept,
+    half_got,
+    own_sent,
+    own_got,
+    small_sums,
+    small_got,
+    gain_sums,
+    gain_got,
+    blocks_one,
+    blocks_two,
+    blocks_got_one,
+    blocks_got_two,
+    blocks_got_three,
+    send_sems,
+    recv_sems,
+):
+    index, unit = lax.axis_index("seq"), lax.axis_index("fsdp")
+    place = ring_place(index, count)
+    forth, back = {"seq": ring_index(place + 1, count)}, {"seq": ring_index(place - 1, count)}
+    across = [{"seq": partner(index, bit)} for bit in (1, 2, 4)]
+    beside = [{"fsdp": partner(unit, bit)} for bit in (1, 2)]
+    copies = Copies(send_sems, recv_sems)
+    slab = normed_ref.shape[0] // count
+    half = slab // 2
+    last = count - 1
+
+    greet([forth, back] + across + beside)
+
+    bits = [lax.rem(index // bit, 2) for bit in (1, 2, 4)]
+    high = blocks_ref.shape[0]
+    firsts = [high // 2, high // 4, high // 8]
+
+    def rows_at(start, size):
+        return pl.ds(pl.multiple_of(start, 16), size)
+
+    blocks_copy = copies.start(
+        blocks_ref.at[rows_at((1 - bits[0]) * firsts[0], firsts[0])], blocks_got_one, across[0]
+    )
+    small_sums[0] = small_ref[...]
+    small_copy = copies.start(small_sums.at[0], small_got.at[0], across[0])
+
+    def out_term(k, way):
+        start = k * slab + way * half
+        return jnp.dot(
+            emb_ref[start : start + half, :], mixed_ref[...], preferred_element_type=f32
+        )
+
+    def front_term(k, way):
+        right = inner_ref if way else branch_ref
+        return jnp.dot(
+            normed_ref[k * slab : (k + 1) * slab, :], right[...], preferred_element_type=f32
+        )
+
+    rings = {}
+
+    def send(name, way, step, total):
+        sent, got = (slim_sent, slim_got) if name == "out" else (wide_sent, wide_got)
+        sent[way, step] = total.astype(bf16)
+        rings[name, way] = copies.start(
+            sent.at[way, step], got.at[way, step], back if way else forth
+        )
+
+    def term(name, way, step):
+        k = (count - step) % count if way else step % count
+        return out_term(k, way) if name == "out" else front_term(k, way)
+
+    def serve(name, step):
+        got = slim_got if name == "out" else wide_got
+        for way in (0, 1):
+            own = term(name, way, step)
+            rings[name, way].wait_recv()
+            total = got[way, step - 2].astype(f32) + own
+            if step < count:
+                send(name, way, step - 1, total)
+            elif name == "out":
+                out_out[way * half : (way + 1) * half, :] = total
+            else:
+                (inner_out if way else branch_out)[...] = total
+
+    for name in ("out", "front"):
+        for way in (0, 1):
+            send(name, way, 0, term(name, way, 1))
+
+    core, side = lax.rem(unit, 2), lax.rem(unit // 2, 2)
+    rows = branch_ref.shape[0]
+    mid, own = rows // 2, rows // 4
+
+    def front_back(start, k):
+        nt = (((1,), (1,)), ((), ()))
+        columns = slice(k * slab, (k + 1) * slab)
+        return lax.dot_general(
+            branch_ref[rows_at(start, mid), :],
+            branch_all_ref[columns, :],
+            nt,
+            preferred_element_type=f32,
+        ) + lax.dot_general(
+            inner_ref[rows_at(start, mid), :],
+            inner_all_ref[columns, :],
+            nt,
+            preferred_element_type=f32,
+        )
+
+    for k in range(count):
+        half_sent[:, k * slab : (k + 1) * slab] = front_back((1 - core) * mid, k).astype(bf16)
+    half_copy = copies.start(half_sent, half_got, beside[0])
+    serve("out", 2)
+    for k in range(count):
+        half_kept[:, k * slab : (k + 1) * slab] = front_back(core * mid, k)
+    half_copy.wait_recv()
+    other = rows_at((1 - side) * own, own)
+    mine = rows_at(side * own, own)
+    own_sent[...] = (half_kept[other, :] + half_got[other, :].astype(f32)).astype(bf16)
+    own_copy = copies.start(own_sent, own_got, beside[1])
+    serve("front", 2)
+
+    blocks_copy.wait_recv()
+    blocks_one[...] = (
+        blocks_ref[rows_at(bits[0] * firsts[0], firsts[0]), :].astype(f32)
+        + blocks_got_one[...].astype(f32)
+    ).astype(bf16)
+    blocks_copy = copies.start(
+        blocks_one.at[rows_at((1 - bits[1]) * firsts[1], firsts[1])], blocks_got_two, across[1]
+    )
+    small_copy.wait_recv()
+    small_sums[1] = small_sums[0] + small_got[0]
+    small_copy = copies.start(small_sums.at[1], small_got.at[1], across[1])
+    serve("out", 3)
+    serve("front", 3)
+
+    own_copy.wait_recv()
+    values = values_ref[...]
+    scale = lax.rsqrt(jnp.mean(values * values, axis=-1, keepdims=True) + eps)
+    unit_values = values * scale
+    front = half_kept[mine, :] + half_got[mine, :].astype(f32) + own_got[...].astype(f32)
+    gain_grad = jnp.sum(front * unit_values, 0, keepdims=True)
+    weighted = front * gain_ref[...]
+    result = grad_ref[...] + scale * (
+        weighted - unit_values * jnp.mean(weighted * unit_values, axis=-1, keepdims=True)
+    )
+    low = result.astype(bf16)
+    own_at = rows_at(core * mid + side * own, own)
+    gain_sums[0] = jnp.zeros_like(gain_sums[0])
+    for k in range(count):
+        to = pl.ds(pl.multiple_of(ring_index(place - k, count) * slab, slab), slab)
+        part = slice(k * slab, (k + 1) * slab)
+        tokens_out[own_at, to] = low[:, part]
+        gain_sums[0, 0:1, to] = gain_grad[:, part]
+        gain_sums[0, 1:2, to] = gain_two_ref[:, part]
+    tokens_copy = copies.start(tokens_out.at[own_at], tokens_out.at[own_at], beside[1])
+    gain_copy = copies.start(gain_sums.at[0], gain_got.at[0], across[0])
+    serve("out", 4)
+    serve("front", 4)
+
+    blocks_copy.wait_recv()
+    blocks_two[...] = (
+        blocks_one[rows_at(bits[1] * firsts[1], firsts[1]), :].astype(f32)
+        + blocks_got_two[...].astype(f32)
+    ).astype(bf16)
+    blocks_copy = copies.start(
+        blocks_two.at[rows_at((1 - bits[2]) * firsts[2], firsts[2])], blocks_got_three, across[2]
+    )
+    small_copy.wait_recv()
+    small_sums[2] = small_sums[1] + small_got[1]
+    small_copy = copies.start(small_sums.at[2], small_got.at[2], across[2])
+    gain_copy.wait_recv()
+    gain_sums[1] = gain_sums[0] + gain_got[0]
+    gain_copy = copies.start(gain_sums.at[1], gain_got.at[1], across[1])
+    tokens_copy.wait_recv()
+    both_at = rows_at(core * mid, mid)
+    tokens_copy = copies.start(tokens_out.at[both_at], tokens_out.at[both_at], beside[0])
+    serve("out", 5)
+    serve("front", 5)
+
+    blocks_copy.wait_recv()
+    starts = [bits[0] * firsts[0]]
+    for bit, first in zip(bits[1:], firsts[1:]):
+        starts.append(starts[-1] + bit * first)
+    at = [rows_at(start, first) for start, first in zip(starts, firsts)]
+    blocks_out[at[2], :] = (
+        blocks_two[rows_at(bits[2] * firsts[2], firsts[2]), :].astype(f32)
+        + blocks_got_three[...].astype(f32)
+    ).astype(bf16)
+    blocks_copy = copies.start(blocks_out.at[at[2]], blocks_out.at[at[2]], across[2])
+    gain_copy.wait_recv()
+    gain_sums[2] = gain_sums[1] + gain_got[1]
+    gain_copy = copies.start(gain_sums.at[2], gain_got.at[2], across[2])
+    small_copy.wait_recv()
+    small_out[...] = small_sums[2] + small_got[2]
+    serve("out", 6)
+    serve("front", 6)
+
+    blocks_copy.wait_recv()
+    blocks_copy = copies.start(blocks_out.at[at[1]], blocks_out.at[at[1]], across[1])
+    gain_copy.wait_recv()
+    gain_sums[3] = gain_sums[2] + gain_got[2]
+    gain_copy = copies.start(gain_sums.at[3], gain_got.at[3], beside[0])
+    serve("out", 7)
+    gain_copy.wait_recv()
+    gain_sums[4] = gain_sums[3] + gain_got[3]
+    gain_copy = copies.start(gain_sums.at[4], gain_got.at[4], beside[1])
+    serve("front", 7)
+    blocks_copy.wait_recv()
+    blocks_copy = copies.start(blocks_out.at[at[0]], blocks_out.at[at[0]], across[0])
+    serve("out", 8)
+    gain_copy.wait_recv()
+    gains_out[...] = gain_sums[4] + gain_got[4]
+    tokens_copy.wait_recv()
+    blocks_copy.wait_recv()
+    serve("front", 8)
+    copies.end()
+
+
+def tail(count, *operands, earlier):
+    operands = lax.optimization_barrier((*operands, *earlier))[: len(operands)]
+    emb, mixed, normed, *_ = operands
+    small, blocks = operands[-2:]
+    width, rows = emb.shape
+    units = mixed.shape[1]
+    slab = width // count
+    high, block_width = blocks.shape
+    whole = pl.BlockSpec(memory_space=pltpu.VMEM)
+    grad = jax.ShapeDtypeStruct((slab, units), f32)
+    steps = count - 1
+    return pl.pallas_call(
+        functools.partial(tail_body, count),
+        out_shape=(
+            grad,
+            grad,
+            grad,
+            jax.ShapeDtypeStruct((rows, width), bf16),
+            jax.ShapeDtypeStruct((8, width), f32),
+            jax.ShapeDtypeStruct(small.shape, f32),
+            jax.ShapeDtypeStruct(blocks.shape, bf16),
+        ),
+        in_specs=[whole] * len(operands),
+        out_specs=(whole,) * 7,
+        scratch_shapes=[
+            pltpu.VMEM((2, steps, slab, units), bf16),
+            pltpu.VMEM((2, steps, slab, units), bf16),
+            pltpu.VMEM((2, steps, slab // 2, units), bf16),
+            pltpu.VMEM((2, steps, slab // 2, units), bf16),
+            pltpu.VMEM((rows // 2, width), bf16),
+            pltpu.VMEM((rows // 2, width), f32),
+            pltpu.VMEM((rows // 2, width), bf16),
+            pltpu.VMEM((rows // 4, width), bf16),
+            pltpu.VMEM((rows // 4, width), bf16),
+            pltpu.VMEM((3, *small.shape), f32),
+            pltpu.VMEM((3, *small.shape), f32),
+            pltpu.VMEM((5, 8, width), f32),
+            pltpu.VMEM((5, 8, width), f32),
+            pltpu.VMEM((high // 2, block_width), bf16),
+            pltpu.VMEM((high // 4, block_width), bf16),
+            pltpu.VMEM((high // 2, block_width), bf16),
+            pltpu.VMEM((high // 4, block_width), bf16),
+            pltpu.VMEM((high // 8, block_width), bf16),
+            pltpu.SemaphoreType.DMA((tail_copies,)),
+            pltpu.SemaphoreType.DMA((tail_copies,)),
+        ],
+        compiler_params=pltpu.CompilerParams(
+            collective_id=0, has_side_effects=True, vmem_limit_bytes=60 * 1024 * 1024
+        ),
+    )(*operands)
 
 
 def block_diagonal(blocks):
@@ -576,7 +918,11 @@
     )
     middle_join = Joined(ring, own_grad.astype(bf16), "fsdp")
     ring.first(middle_join.step())
-    in_turn(mlp_grads, down_grads)
+    in_turn(mlp_grads)
+    mixed_sum = Halves(ring, dot_nt(ring.then(hidden_low, 2), down_all), "fsdp")
+    mixed_sum.step()
+    ring.first(mixed_sum.step())
+    in_turn(down_grads)
     middle_join.step(2)
     middle_low = middle_join.run()
 
@@ -610,40 +956,24 @@
     grad_padded = taps[0] * spread[:, :stop] + taps[1] * spread[:, 1 : stop + 1]
     grad_padded = grad_padded + taps[2] * spread[:, 2 : stop + 2] + taps[3] * spread[:, 3:]
     returned = passed_along(grad_padded[:, :3], -1)
-    ring.first(grad_padded)
+    mixed_join = Joined(ring, restored(own_middle + mixed_sum.run(1), bf16), "fsdp")
+    ring.first(grad_padded, mixed_join.step())
     in_turn(mlp_grads)
     grad_inner = jnp.concatenate(
         [grad_padded[:, 3:-3], grad_padded[:, -3:] + ring.then(returned)], 1
     )
     inner_grad_low = grad_inner.astype(bf16).reshape(rows, units)
     in_turn(*[mlp_grads] * (steps - 6))
-    out_grads = scatter(
-        slab_dots(middle_low.T, mixed_low, 0, half), slab_dots(middle_low.T, mixed_low, half, half)
-    )
-    front_grads = scatter(
-        slab_dots(normed.T, branch_low), slab_dots(normed.T, inner_grad_low)
-    )
-    in_turn(out_grads, front_grads)
-    front_sum = Halves(
-        ring,
-        dot_nt(ring.then(branch_low), branch_all) + dot_nt(inner_grad_low, inner_all),
-        "fsdp",
-    )
-    front_sum.step()
-    front_sum.step()
 
     block_count = gate_blocks.shape[0]
-    conv_again = ring.then(conv_flat)
     block_grads = jnp.concatenate(
         [
-            diagonal_blocks(dot_tn(conv_again, gate_low), block_count),
-            diagonal_blocks(dot_tn(conv_again, input_low), block_count),
+            diagonal_blocks(dot_tn(conv_flat, gate_low), block_count),
+            diagonal_blocks(dot_tn(conv_flat, input_low), block_count),
         ],
         0,
     )
     block_width = block_grads.shape[-1]
-    block_sum = Everywhere(ring, block_grads.reshape(-1, block_width), "seq")
-    block_sum.step()
     taps_grad = jnp.stack(
         [jnp.sum(grad_conv * padded[:, 3 - k : 3 - k + length], (0, 1)) for k in range(4)], 0
     )
@@ -657,54 +987,54 @@
         ],
         0,
     )
-    in_turn(out_grads, front_grads)
-    block_sum.step(1)
-    own_front = front_sum.run(1)
+    mixed_join.step()
+    mixed = mixed_join.run().astype(f32).reshape(tokens.shape)
+    gate_grad, up_grad = mlp_grads.sums()
     own_values = own_rows(tokens_low).astype(f32)
-    scale_one = inverse_rms(own_values)
-    unit_one = own_values * scale_one
-    gain_one_grad = jnp.sum(own_front * unit_one, 0)
-    weighted = own_front * gain_one
-    own_tokens = own_grad + scale_one * (
-        weighted - unit_one * jnp.mean(weighted * unit_one, axis=-1, keepdims=True)
-    )
-    gains = jnp.stack([gain_restored(gain_one_grad), gain_restored(gain_two_grad)], 0)
-    small_sum = SmallSum(ring, jnp.concatenate([small.reshape(-1), gains.reshape(-1)]), "seq")
-    tokens_join = Joined(ring, restored(own_tokens, bf16), "fsdp")
-    tokens_join.step()
-    small_sum.step()
-    in_turn(out_grads, front_grads)
-    block_sum.step(1)
-    small_sum.step(1)
-    tokens_join.step(1)
-    tokens_grad = tokens_join.run().astype(f32).reshape(tokens.shape)
-    in_turn(out_grads, front_grads)
-    block_sum.step(1)
-    small_sum.step(1)
-    mixed_sum = Halves(ring, dot_nt(ring.then(hidden_low), down_all), "fsdp")
-    mixed_sum.step()
-    mixed_sum.step()
-    in_turn(out_grads, front_grads)
-    block_sum.step(1)
-    small = small_sum.run(1)
-    gains = small[8 * units :]
-    small = small[: 8 * units].reshape(8, units)
-    gains_sum = SmallSum(ring, gains, "fsdp")
-    gains_sum.step()
-    mixed_join = Joined(ring, restored(own_middle + mixed_sum.run(1), bf16), "fsdp")
-    mixed_join.step()
-    in_turn(out_grads, front_grads)
-    block_sum.step(1)
-    gains_sum.step(1)
-    mixed_join.step(1)
-    mixed = mixed_join.run().astype(f32).reshape(tokens.shape)
-    in_turn(*[out_grads, front_grads] * (steps - 6))
-    block_grads = block_sum.run(1).astype(f32)
+    if ringed:
+        branch_grad, inner_grad, out_grad, tokens_grad, gains, small, block_grads = tail(
+            count,
+            middle_low.T,
+            mixed_low,
+            normed.T,
+            branch_low,
+            inner_grad_low,
+            branch_all,
+            inner_all,
+            own_values,
+            own_grad,
+            gain_one[None],
+            gain_two_grad[None],
+            small,
+            block_grads.reshape(-1, block_width).astype(bf16),
+            earlier=(gate_grad, up_grad, mixed),
+        )
+        block_grads = block_grads.astype(f32)
+    else:
+        out_grads = scatter(
+            slab_dots(middle_low.T, mixed_low, 0, half),
+            slab_dots(middle_low.T, mixed_low, half, half),
+        )
+        front_grads = scatter(
+            slab_dots(normed.T, branch_low), slab_dots(normed.T, inner_grad_low)
+        )
+        branch_grad, inner_grad = front_grads.sums()
+        out_grad = jnp.concatenate(out_grads.sums(), 0)
+        own_front = Halves(
+            ring, dot_nt(branch_low, branch_all) + dot_nt(inner_grad_low, inner_all), "fsdp"
+        ).run()
+        scale_one = inverse_rms(own_values)
+        unit_one = own_values * scale_one
+        weighted = own_front * gain_one
+        own_tokens = own_grad + scale_one * (
+            weighted - unit_one * jnp.mean(weighted * unit_one, axis=-1, keepdims=True)
+        )
+        gains = jnp.stack([jnp.sum(own_front * unit_one, 0), gain_two_grad], 0)
+        gains = lax.psum(gains, ("seq", "fsdp"))
+        small, block_grads = lax.psum((small, block_grads), "seq")
+        tokens_grad = Joined(ring, own_tokens.astype(bf16), "fsdp").run()
+    tokens_grad = tokens_grad.astype(f32).reshape(tokens.shape)
     block_grads = block_grads.reshape(2, block_count, block_width, block_width)
-    gains = gains_sum.run(1).reshape(2, width)
-    branch_grad, inner_grad = front_grads.sums()
-    gate_grad, up_grad = mlp_grads.sums()
-    out_grad = jnp.concatenate(out_grads.sums(), 0)
     down_grad = jnp.concatenate(down_grads.sums(), 0)
     return (
         mixed,

time: 773 us -> 764 us (0.988)
  Pallas kernels: 27.6 us -> 140 us
  waiting for transfers between devices: 320 us -> 273 us
  starting transfers between devices: 150 us -> 114 us
  matrix products: 110 us -> 81 us
  other arithmetic: 65.7 us -> 54.6 us
    pallas_call x0 -> x1, Pallas kernels: none -> 118 us  [tail(): pl.pallas_call(functools.partial(tail_body, count), out_shape=(grad, grad...]
    ppermute x56 -> x42, waiting for transfers between devices: 77.5 us -> 41.6 us  [send(): lax.ppermute(back, 'seq', self.back)]
    ppermute x29 -> x14, waiting for transfers between devices: 48.3 us -> 13 us  [swapped(): lax.ppermute(values, axis, [(i, i ^ bit) for i in range(lax.axis_size(axi...]
    dot_general x72 -> x40, matrix products: 85.4 us -> 59.1 us  [dot_nn(): return jnp.dot(left, right, preferred_element_type=f32)]
    ppermute x56 -> x42, starting transfers between devices: 82.2 us -> 59.1 us  [send(): lax.ppermute(forth, 'seq', self.forth)]
    ppermute x56 -> x42, waiting for transfers between devices: 190 us -> 208 us  [send(): lax.ppermute(forth, 'seq', self.forth)]
    ppermute x29 -> x14, starting transfers between devices: 16.6 us -> 8.76 us  [swapped(): lax.ppermute(values, axis, [(i, i ^ bit) for i in range(lax.axis_size(axi...]
    pallas_call x4 -> x3, Pallas kernels: 24.4 us -> 18.6 us  [move_slabs(): pl.pallas_call(move_body, out_shape=jax.ShapeDtypeStruct((rows, width), d...]
  transfers between devices with their start and end apart: 149 -> 106, of which waited for: 80 -> 54; matrix products, arithmetic and copies ran while one was open for 29% -> 20% of each run, Pallas kernels for 4% -> 2%
where the time goes in v3:
time: 764 us; the launch traced here: 755 us
  waiting for transfers between devices  273 us (36%)
  Pallas kernels  140 us (18%)
  starting transfers between devices  114 us (15%)
  local copies, waits for them, and re-layouts  88.9 us (12%)
  matrix products  81 us (11%)
  other arithmetic  54.6 us (7%)
    ppermute x42, waiting for transfers between devices, send(): lax.ppermute(forth, 'seq', self.forth)  208 us
    pallas_call x1, Pallas kernels, tail(): pl.pallas_call(functools.partial(tail_body, count), out_shape=(grad, grad...  118 us
    unnamed x347, local copies, waits for them, and re-layouts  62.3 us
    dot_general x40, matrix products, dot_nn(): return jnp.dot(left, right, preferred_element_type=f32)  59.1 us
    ppermute x42, starting transfers between devices, send(): lax.ppermute(forth, 'seq', self.forth)  59.1 us
    ppermute x42, waiting for transfers between devices, send(): lax.ppermute(back, 'seq', self.back)  41.6 us
    ppermute x42, starting transfers between devices, send(): lax.ppermute(back, 'seq', self.back)  31.6 us
    dot_general x6, matrix products, dot_nt(): lax.dot_general(left, right, (((1,), (1,)), ((), ())), preferred_element_...  19.3 us
  transfers between devices with their start and end apart: 106, of which 54 were waited for; matrix products, arithmetic and copies ran while one was open for 20% of the time, Pallas kernels for 2%

profile of v3, /device:TPU:0, one launch (start us, length us, event | category | flops | bytes accessed | tf_op | source)
XLA Modules:
  0.0 755.5 jit_solution(14005258625914525467)
XLA Ops:
  14.2 6.5 shard_map.332
  66.8 6.4 shard_map.333
  136.4 10.5 %collective-permute-done.29 = bf16[256,1536]{1,0:T(8,128)(2,1)S(1)} collective-permute-done((bf16[256,1536]{1,0:T(8,128)(2,1)S(1)}, bf16[256,1536]{1,0:T(8,128)(2,1)S(1)}, u32[]{:S(2)}, u32[]{:S(2)}) %collective-permute-start.29) | collective-permute-done | bytes 786464 | tf_op jit(solution)/shard_map/ppermute | solution.py:143
  161.0 7.1 collective-permute-done.37
  201.5 7.6 %collective-permute-done.43 = bf16[128,1536]{0,1:T(8,128)(2,1)} collective-permute-done((bf16[128,1536]{0,1:T(8,128)(2,1)}, bf16[128,1536]{0,1:T(8,128)(2,1)}, u32[]{:S(2)}, u32[]{:S(2)}) %collective-permute-start.43) | collective-permute-done | bytes 393248 | tf_op jit(solution)/shard_map/ppermute | solution.py:143
  213.2 11.9 %collective-permute-done.49 = bf16[256,1536]{1,0:T(8,128)(2,1)} collective-permute-done((bf16[256,1536]{1,0:T(8,128)(2,1)}, bf16[256,1536]{1,0:T(8,128)(2,1)}, u32[]{:S(2)}, u32[]{:S(2)}) %collective-permute-start.49) | collective-permute-done | bytes 786464 | tf_op jit(solution)/shard_map/ppermute | solution.py:143
  231.3 22.2 %collective-permute-done.46 = bf16[128,1536]{0,1:T(8,128)(2,1)S(1)} collective-permute-done((bf16[128,1536]{0,1:T(8,128)(2,1)}, bf16[128,1536]{0,1:T(8,128)(2,1)S(1)}, u32[]{:S(2)}, u32[]{:S(2)}) %collective-permute-start.46) | collective-permute-done | bytes 393248 | tf_op jit(solution)/shard_map/ppermute | solution.py:143
  257.2 14.3 %collective-permute-done.53 = bf16[256,1536]{1,0:T(8,128)(2,1)S(1)} collective-permute-done((bf16[256,1536]{1,0:T(8,128)(2,1)S(1)}, bf16[256,1536]{1,0:T(8,128)(2,1)S(1)}, u32[]{:S(2)}, u32[]{:S(2)}) %collective-permute-start.53) | collective-permute-done | bytes 786464 | tf_op jit(solution)/shard_map/ppermute | solution.py:143
  279.5 18.1 %collective-permute-done.57 = bf16[128,1536]{0,1:T(8,128)(2,1)S(1)} collective-permute-done((bf16[128,1536]{0,1:T(8,128)(2,1)S(1)}, bf16[128,1536]{0,1:T(8,128)(2,1)S(1)}, u32[]{:S(2)}, u32[]{:S(2)}) %collective-permute-start.57) | collective-permute-done | bytes 393248 | tf_op jit(solution)/shard_map/ppermute | solution.py:143
  304.5 13.7 %collective-permute-done.59 = bf16[256,1536]{1,0:T(8,128)(2,1)S(1)} collective-permute-done((bf16[256,1536]{1,0:T(8,128)(2,1)S(1)}, bf16[256,1536]{1,0:T(8,128)(2,1)S(1)}, u32[]{:S(2)}, u32[]{:S(2)}) %collective-permute-start.59) | collective-permute-done | bytes 786464 | tf_op jit(solution)/shard_map/ppermute | solution.py:143
  339.6 6.3 collective-permute-done.65
  354.0 6.8 multiply_convert_fusion
  372.3 5.9 fusion.184
  390.6 13.0 %collective-permute-done.69 = bf16[256,1536]{1,0:T(8,128)(2,1)S(1)} collective-permute-done((bf16[256,1536]{1,0:T(8,128)(2,1)S(1)}, bf16[256,1536]{1,0:T(8,128)(2,1)S(1)}, u32[]{:S(2)}, u32[]{:S(2)}) %collective-permute-start.69) | collective-permute-done | bytes 786464 | tf_op jit(solution)/shard_map/ppermute | solution.py:143
  405.5 6.2 collective-permute-done.78
  419.6 14.4 %collective-permute-done.74 = bf16[256,1536]{1,0:T(8,128)(2,1)S(1)} collective-permute-done((bf16[256,1536]{1,0:T(8,128)(2,1)S(1)}, bf16[256,1536]{1,0:T(8,128)(2,1)S(1)}, u32[]{:S(2)}, u32[]{:S(2)}) %collective-permute-start.74) | collective-permute-done | bytes 786464 | tf_op jit(solution)/shard_map/ppermute | solution.py:143
  447.9 7.5 collective-permute-done.82
  468.6 5.7 shard_map.335
  486.3 10.2 %collective-permute-done.89 = bf16[128,2048]{1,0:T(8,128)(2,1)} collective-permute-done((bf16[128,2048]{1,0:T(8,128)(2,1)}, bf16[128,2048]{1,0:T(8,128)(2,1)}, u32[]{:S(2)}, u32[]{:S(2)}) %collective-permute-start.89) | collective-permute-done | bytes 524320 | tf_op jit(solution)/shard_map/ppermute | solution.py:227
  524.0 9.9 %collective-permute-done.94 = f32[2,2,1,704]{3,2,1,0:T(1,128)S(1)} collective-permute-done((f32[2,2,1,704]{3,2,1,0:T(1,128)S(1)}, f32[2,2,1,704]{3,2,1,0:T(1,128)S(1)}, u32[]{:S(2)}, u32[]{:S(2)}) %collective-permute-start.94) | collective-permute-done | bytes 11296 | tf_op jit(solution)/shard_map/ppermute | solution.py:338
  563.0 12.3 %collective-permute-done.100 = bf16[256,1536]{1,0:T(8,128)(2,1)S(1)} collective-permute-done((bf16[256,1536]{1,0:T(8,128)(2,1)S(1)}, bf16[256,1536]{1,0:T(8,128)(2,1)S(1)}, u32[]{:S(2)}, u32[]{:S(2)}) %collective-permute-start.100) | collective-permute-done | bytes 786464 | tf_op jit(solution)/shard_map/ppermute | solution.py:143
  580.7 13.3 %collective-permute-done.102 = bf16[256,1536]{1,0:T(8,128)(2,1)S(1)} collective-permute-done((bf16[256,1536]{1,0:T(8,128)(2,1)S(1)}, bf16[256,1536]{1,0:T(8,128)(2,1)S(1)}, u32[]{:S(2)}, u32[]{:S(2)}) %collective-permute-start.102) | collective-permute-done | bytes 786464 | tf_op jit(solution)/shard_map/ppermute | solution.py:143
  604.2 9.1 %collective-permute-done.104 = bf16[256,1536]{1,0:T(8,128)(2,1)} collective-permute-done((bf16[256,1536]{1,0:T(8,128)(2,1)}, bf16[256,1536]{1,0:T(8,128)(2,1)}, u32[]{:S(2)}, u32[]{:S(2)}) %collective-permute-start.104) | collective-permute-done | bytes 786464 | tf_op jit(solution)/shard_map/ppermute | solution.py:143
  623.3 118.5 %shard_map.337 = (f32[256,704]{1,0:T(8,128)}, f32[256,704]{1,0:T(8,128)}, f32[256,704]{1,0:T(8,128)}, bf16[512,2048]{1,0:T(8,128)(2,1)}, f32[8,2048]{1,0:T(8,128...) custom-call(bf16[2048,512]{1,0:T(8,128)(2,1)} %copy.95.emb_ref, bf16[512,704]{1,0:T(8,128)(2,1)} %bitcast.223, ...), custom_call_target="tpu_custom_call" | custom-call | tf_op jit(solution)/shard_map/pallas_call | solution.py:681
  (708 shorter events, 394.2 us)
Async XLA Ops:
  1.8 22.7 %collective-permute-start = (bf16[128,704]{0,1:T(8,128)(2,1)S(1)}, bf16[128,704]{0,1:T(8,128)(2,1)}, u32[]{:S(2)}, u32[]{:S(2)}) collective-permute-start(bf16[128,704]{0,1:T(8,128)(2,1)S(1)} %get-tuple-element.364), channel_id=1, source_target_pairs={{0,8},{8,16},{16,24},{24,28},{28,20},{20,12},{12,4},{4,0},{1,9},{9... | collective-permute-start | bytes 540680 | tf_op jit(solution)/shard_map/ppermute | solution.py:143
  6.0 35.5 %collective-permute-start.2 = (bf16[256,704]{1,0:T(8,128)(2,1)S(1)}, bf16[256,704]{1,0:T(8,128)(2,1)}, u32[]{:S(2)}, u32[]{:S(2)}) collective-permute-start(bf16[256,704]{1,0:T(8,128)(2,1)S(1)} %copy.70), channel_id=1, source_target_pairs={{0,8},{8,16},{16,24},{24,28},{28,20},{20,12},{12,4},{4,0},{1,9},{9... | collective-permute-start | bytes 1081352 | tf_op jit(solution)/shard_map/ppermute | solution.py:143
  9.2 32.3 %collective-permute-start.3 = (bf16[256,704]{1,0:T(8,128)(2,1)S(1)}, bf16[256,704]{1,0:T(8,128)(2,1)S(1)}, u32[]{:S(2)}, u32[]{:S(2)}) collective-permute-start(bf16[256,704]{1,0:T(8,128)(2,1)S(1)} %copy.72), channel_id=1, source_target_pairs={{8,0},{16,8},{24,16},{28,24},{20,28},{12,20},{4,12},{0,4},{9,1},{1... | collective-permute-start | bytes 1081352 | tf_op jit(solution)/shard_map/ppermute | solution.py:143
  77.2 53.2 %collective-permute-start.26 = (bf16[128,704]{0,1:T(8,128)(2,1)}, bf16[128,704]{0,1:T(8,128)(2,1)}, u32[]{:S(2)}, u32[]{:S(2)}) collective-permute-start(bf16[128,704]{0,1:T(8,128)(2,1)} %collective-permute-done.24), channel_id=1, source_target_pairs={{0,8},{8,16},{16,24},{24,28},{28,20},{20,12},{12,4},{4,0},{1,9},{9... | collective-permute-start | bytes 540680 | tf_op jit(solution)/shard_map/ppermute | solution.py:143
  198.8 26.3 %collective-permute-start.49 = (bf16[256,1536]{1,0:T(8,128)(2,1)}, bf16[256,1536]{1,0:T(8,128)(2,1)}, u32[]{:S(2)}, u32[]{:S(2)}) collective-permute-start(bf16[256,1536]{1,0:T(8,128)(2,1)} %collective-permute-done.32), channel_id=1, source_target_pairs={{0,8},{8,16},{16,24},{24,28},{28,20},{20,12},{12,4},{4,0},{1,9},{9... | collective-permute-start | bytes 2359304 | tf_op jit(solution)/shard_map/ppermute | solution.py:143
  200.6 25.9 %collective-permute-start.50 = (bf16[256,1536]{1,0:T(8,128)(2,1)}, bf16[256,1536]{1,0:T(8,128)(2,1)S(1)}, u32[]{:S(2)}, u32[]{:S(2)}) collective-permute-start(bf16[256,1536]{1,0:T(8,128)(2,1)} %collective-permute-done.33), channel_id=1, source_target_pairs={{8,0},{16,8},{24,16},{28,24},{20,28},{12,20},{4,12},{0,4},{9,1},{1... | collective-permute-start | bytes 2359304 | tf_op jit(solution)/shard_map/ppermute | solution.py:143
  226.5 28.0 %collective-permute-start.51 = (bf16[256,1536]{1,0:T(8,128)(2,1)}, bf16[256,1536]{1,0:T(8,128)(2,1)S(1)}, u32[]{:S(2)}, u32[]{:S(2)}) collective-permute-start(bf16[256,1536]{1,0:T(8,128)(2,1)} %collective-permute-done.49), channel_id=1, source_target_pairs={{0,8},{8,16},{16,24},{24,28},{28,20},{20,12},{12,4},{4,0},{1,9},{9... | collective-permute-start | bytes 2359304 | tf_op jit(solution)/shard_map/ppermute | solution.py:143
  228.2 26.3 %collective-permute-start.52 = (bf16[256,1536]{1,0:T(8,128)(2,1)S(1)}, bf16[256,1536]{1,0:T(8,128)(2,1)S(1)}, u32[]{:S(2)}, u32[]{:S(2)}) collective-permute-start(bf16[256,1536]{1,0:T(8,128)(2,1)S(1)} %collective-permute-done.50), channel_id=1, source_target_pairs={{8,0},{16,8},{24,16},{28,24},{20,28},{12,20},{4,12},{0,4},{9,1},{1... | collective-permute-start | bytes 2359304 | tf_op jit(solution)/shard_map/ppermute | solution.py:143
  228.7 25.8 %collective-permute-start.45 = (bf16[128,2048]{1,0:T(8,128)(2,1)S(1)}, bf16[128,2048]{1,0:T(8,128)(2,1)S(1)}, u32[]{:S(2)}, u32[]{:S(2)}) collective-permute-start(bf16[128,2048]{1,0:T(8,128)(2,1)S(1)} %multiply_convert_fusion.3), channel_id=1, source_target_pairs={{0,2},{1,3},{2,0},{3,1},{4,6},{5,7},{6,4},{7,5},{8,10},{9,11},{10,... | collective-permute-start | bytes 1572872 | tf_op jit(solution)/shard_map/ppermute | solution.py:227
  229.2 24.3 %collective-permute-start.46 = (bf16[128,1536]{0,1:T(8,128)(2,1)}, bf16[128,1536]{0,1:T(8,128)(2,1)S(1)}, u32[]{:S(2)}, u32[]{:S(2)}) collective-permute-start(bf16[128,1536]{0,1:T(8,128)(2,1)} %collective-permute-done.43), channel_id=1, source_target_pairs={{0,8},{8,16},{16,24},{24,28},{28,20},{20,12},{12,4},{4,0},{1,9},{9... | collective-permute-start | bytes 1179656 | tf_op jit(solution)/shard_map/ppermute | solution.py:143
  231.0 23.5 %collective-permute-start.47 = (bf16[128,1536]{0,1:T(8,128)(2,1)}, bf16[128,1536]{0,1:T(8,128)(2,1)S(1)}, u32[]{:S(2)}, u32[]{:S(2)}) collective-permute-start(bf16[128,1536]{0,1:T(8,128)(2,1)} %collective-permute-done.44), channel_id=1, source_target_pairs={{8,0},{16,8},{24,16},{28,24},{20,28},{12,20},{4,12},{0,4},{9,1},{1... | collective-permute-start | bytes 1179656 | tf_op jit(solution)/shard_map/ppermute | solution.py:143
  257.0 43.0 %collective-permute-start.48 = (bf16[256,2048]{1,0:T(8,128)(2,1)S(1)}, bf16[256,2048]{1,0:T(8,128)(2,1)S(1)}, u32[]{:S(2)}, u32[]{:S(2)}) collective-permute-start(bf16[256,2048]{1,0:T(8,128)(2,1)S(1)} %pad_maximum_fusion.5), channel_id=1, source_target_pairs={{0,1},{1,0},{2,3},{3,2},{4,5},{5,4},{6,7},{7,6},{8,9},{9,8},{10,11... | collective-permute-start | bytes 3145736 | tf_op jit(solution)/shard_map/ppermute | solution.py:227
  272.5 27.3 %collective-permute-start.55 = (bf16[256,1536]{1,0:T(8,128)(2,1)S(1)}, bf16[256,1536]{1,0:T(8,128)(2,1)S(1)}, u32[]{:S(2)}, u32[]{:S(2)}) collective-permute-start(bf16[256,1536]{1,0:T(8,128)(2,1)S(1)} %collective-permute-done.53), channel_id=1, source_target_pairs={{0,8},{8,16},{16,24},{24,28},{28,20},{20,12},{12,4},{4,0},{1,9},{9... | collective-permute-start | bytes 2359304 | tf_op jit(solution)/shard_map/ppermute | solution.py:143
  274.1 25.7 %collective-permute-start.56 = (bf16[256,1536]{1,0:T(8,128)(2,1)S(1)}, bf16[256,1536]{1,0:T(8,128)(2,1)S(1)}, u32[]{:S(2)}, u32[]{:S(2)}) collective-permute-start(bf16[256,1536]{1,0:T(8,128)(2,1)S(1)} %collective-permute-done.54), channel_id=1, source_target_pairs={{8,0},{16,8},{24,16},{28,24},{20,28},{12,20},{4,12},{0,4},{9,1},{1... | collective-permute-start | bytes 2359304 | tf_op jit(solution)/shard_map/ppermute | solution.py:143
  302.4 25.7 %collective-permute-start.61 = (bf16[128,1536]{0,1:T(8,128)(2,1)S(1)}, bf16[128,1536]{0,1:T(8,128)(2,1)S(1)}, u32[]{:S(2)}, u32[]{:S(2)}) collective-permute-start(bf16[128,1536]{0,1:T(8,128)(2,1)S(1)} %collective-permute-done.57), channel_id=1, source_target_pairs={{0,8},{8,16},{16,24},{24,28},{28,20},{20,12},{12,4},{4,0},{1,9},{9... | collective-permute-start | bytes 1179656 | tf_op jit(solution)/shard_map/ppermute | solution.py:143
  302.6 25.5 %collective-permute-start.62 = (bf16[128,1536]{0,1:T(8,128)(2,1)S(1)}, bf16[128,1536]{0,1:T(8,128)(2,1)S(1)}, u32[]{:S(2)}, u32[]{:S(2)}) collective-permute-start(bf16[128,1536]{0,1:T(8,128)(2,1)S(1)} %collective-permute-done.58), channel_id=1, source_target_pairs={{8,0},{16,8},{24,16},{28,24},{20,28},{12,20},{4,12},{0,4},{9,1},{1... | collective-permute-start | bytes 1179656 | tf_op jit(solution)/shard_map/ppermute | solution.py:143
  387.2 24.5 %collective-permute-start.78 = (bf16[128,1536]{1,0:T(8,128)(2,1)S(1)}, bf16[128,1536]{1,0:T(8,128)(2,1)S(1)}, u32[]{:S(2)}, u32[]{:S(2)}) collective-permute-start(bf16[128,1536]{1,0:T(8,128)(2,1)S(1)} %add_convert_fusion.20), channel_id=1, source_target_pairs={{0,8},{8,16},{16,24},{24,28},{28,20},{20,12},{12,4},{4,0},{1,9},{9... | collective-permute-start | bytes 1179656 | tf_op jit(solution)/shard_map/ppermute | solution.py:143
  388.3 24.2 %collective-permute-start.79 = (bf16[128,1536]{1,0:T(8,128)(2,1)S(1)}, bf16[128,1536]{1,0:T(8,128)(2,1)S(1)}, u32[]{:S(2)}, u32[]{:S(2)}) collective-permute-start(bf16[128,1536]{1,0:T(8,128)(2,1)S(1)} %add_convert_fusion.19), channel_id=1, source_target_pairs={{8,0},{16,8},{24,16},{28,24},{20,28},{12,20},{4,12},{0,4},{9,1},{1... | collective-permute-start | bytes 1179656 | tf_op jit(solution)/shard_map/ppermute | solution.py:143
  417.5 24.8 %collective-permute-start.80 = (bf16[128,1536]{1,0:T(8,128)(2,1)S(1)}, bf16[128,1536]{1,0:T(8,128)(2,1)S(1)}, u32[]{:S(2)}, u32[]{:S(2)}) collective-permute-start(bf16[128,1536]{1,0:T(8,128)(2,1)S(1)} %add_convert_fusion.18), channel_id=1, source_target_pairs={{0,8},{8,16},{16,24},{24,28},{28,20},{20,12},{12,4},{4,0},{1,9},{9... | collective-permute-start | bytes 1179656 | tf_op jit(solution)/shard_map/ppermute | solution.py:143
  418.6 25.4 %collective-permute-start.81 = (bf16[128,1536]{1,0:T(8,128)(2,1)S(1)}, bf16[128,1536]{1,0:T(8,128)(2,1)S(1)}, u32[]{:S(2)}, u32[]{:S(2)}) collective-permute-start(bf16[128,1536]{1,0:T(8,128)(2,1)S(1)} %add_convert_fusion.17), channel_id=1, source_target_pairs={{8,0},{16,8},{24,16},{28,24},{20,28},{12,20},{4,12},{0,4},{9,1},{1... | collective-permute-start | bytes 1179656 | tf_op jit(solution)/shard_map/ppermute | solution.py:143
  474.3 23.6 %collective-permute-start.86 = (bf16[128,2048]{1,0:T(8,128)(2,1)}, bf16[128,2048]{1,0:T(8,128)(2,1)}, u32[]{:S(2)}, u32[]{:S(2)}) collective-permute-start(bf16[128,2048]{1,0:T(8,128)(2,1)} %shard_map.335), channel_id=1, source_target_pairs={{0,2},{1,3},{2,0},{3,1},{4,6},{5,7},{6,4},{7,5},{8,10},{9,11},{10,... | collective-permute-start | bytes 1572872 | tf_op jit(solution)/shard_map/ppermute | solution.py:227
  476.3 23.4 %collective-permute-start.95 = (bf16[256,1536]{1,0:T(8,128)(2,1)}, bf16[256,1536]{1,0:T(8,128)(2,1)}, u32[]{:S(2)}, u32[]{:S(2)}) collective-permute-start(bf16[256,1536]{1,0:T(8,128)(2,1)} %add_convert_fusion.9), channel_id=1, source_target_pairs={{0,8},{8,16},{16,24},{24,28},{28,20},{20,12},{12,4},{4,0},{1,9},{9... | collective-permute-start | bytes 2359304 | tf_op jit(solution)/shard_map/ppermute | solution.py:143
  477.3 24.3 %collective-permute-start.96 = (bf16[256,1536]{1,0:T(8,128)(2,1)}, bf16[256,1536]{1,0:T(8,128)(2,1)}, u32[]{:S(2)}, u32[]{:S(2)}) collective-permute-start(bf16[256,1536]{1,0:T(8,128)(2,1)} %add_convert_fusion.8), channel_id=1, source_target_pairs={{8,0},{16,8},{24,16},{28,24},{20,28},{12,20},{4,12},{0,4},{9,1},{1... | collective-permute-start | bytes 2359304 | tf_op jit(solution)/shard_map/ppermute | solution.py:143
  553.7 47.6 %collective-permute-start.99 = (f32[2,3,704]{2,1,0:T(4,128)S(1)}, f32[2,3,704]{2,1,0:T(4,128)S(1)}, u32[]{:S(2)}, u32[]{:S(2)}) collective-permute-start(f32[2,3,704]{2,1,0:T(4,128)S(1)} %slice.551), channel_id=1, source_target_pairs={{4,0},{8,4},{12,8},{16,12},{20,16},{24,20},{28,24},{5,1},{9,5},{13... | collective-permute-start | bytes 50696 | tf_op jit(solution)/shard_map/ppermute | solution.py:338
  (219 other events, 3122.7 us)

commit v4 on v3

--- a/solution.py
+++ b/solution.py
@@ -11,7 +11,7 @@
 decay_scale = 8.0
 f32 = jnp.float32
 bf16 = jnp.bfloat16
-ring_limit = 16
+ring_count = 8
 
 
 def gelu_tanh(values):
@@ -346,7 +346,7 @@
     def __init__(self, prods, states, sign):
         self.pair, self.sign = jnp.stack([prods, states], 0), sign
         self.count = lax.axis_size("seq")
-        self.direct = self.count <= ring_limit and self.count % 2 == 0
+        self.direct = self.count == ring_count
         if self.direct:
             self.other = swapped(self.pair, "seq", 1)
 
@@ -395,10 +395,10 @@
 class Copies:
     def __init__(self, send_sems, recv_sems):
         self.send_sems, self.recv_sems = send_sems, recv_sems
-        self.started = []
+        self.started, self.waiting = 0, []
 
     def start(self, source, target, device):
-        slot = len(self.started)
+        slot = self.started
         copy = pltpu.make_async_remote_copy(
             src_ref=source,
             dst_ref=target,
@@ -408,11 +408,16 @@
             device_id_type=pl.DeviceIdType.MESH,
         )
         copy.start()
-        self.started.append(copy)
+        self.started += 1
+        self.waiting.append(copy)
         return copy
 
+    def sent(self, copy):
+        copy.wait_send()
+        self.waiting.remove(copy)
+
     def end(self):
-        for copy in self.started:
+        for copy in self.waiting:
             copy.wait_send()
 
 
@@ -667,8 +672,7 @@
     copies.end()
 
 
-def tail(count, *operands, earlier):
-    operands = lax.optimization_barrier((*operands, *earlier))[: len(operands)]
+def tail(count, *operands):
     emb, mixed, normed, *_ = operands
     small, blocks = operands[-2:]
     width, rows = emb.shape
@@ -719,6 +723,843 @@
     )(*operands)
 
 
+def peers(count, units):
+    index, unit = lax.axis_index("seq"), lax.axis_index("fsdp")
+    along = [{"seq": lax.rem(index + distance, count)} for distance in range(1, count)]
+    beside = [{"fsdp": partner(unit, 1 << i)} for i in range(units.bit_length() - 1)]
+    return along, beside
+
+
+def rows_at(start, size, multiple=16):
+    return pl.ds(pl.multiple_of(start, multiple), size)
+
+
+def dot_slabs(left, right_ref, slab, count):
+    for k in range(count):
+        columns = slice(k * slab, (k + 1) * slab)
+        yield columns, lax.dot_general(
+            left,
+            right_ref[columns, :],
+            (((1,), (1,)), ((), ())),
+            preferred_element_type=f32,
+        )
+
+
+def scan_rows(a_ref, b_ref, prod_ref, state_ref, batches, backward):
+    length, units = a_ref.shape[0] // batches, a_ref.shape[1]
+    tiles = length // 8
+    rows = lax.broadcasted_iota(jnp.int32, (8, units), 0)
+
+    def step(index, carry):
+        tile = tiles - 1 - index if backward else index
+        following = []
+        for batch in range(batches):
+            prod_in, state_in, a_next = carry[batch]
+            at = rows_at(batch * length + tile * 8, 8, 8)
+            a, b = a_ref[at, :], b_ref[at, :]
+            a_first = a[0:1]
+            if backward:
+                a = jnp.where(rows < 7, pltpu.roll(a, 7, 0), a_next)
+            for shift in (1, 2, 4):
+                turn = 8 - shift if backward else shift
+                inside = rows < 8 - shift if backward else rows >= shift
+                a_moved = jnp.where(inside, pltpu.roll(a, turn, 0), 1.0)
+                b_moved = jnp.where(inside, pltpu.roll(b, turn, 0), 0.0)
+                b = a * b_moved + b
+                a = a * a_moved
+            b = b + a * state_in
+            a = a * prod_in
+            prod_ref[at, :] = a
+            state_ref[at, :] = b
+            edge = 0 if backward else 7
+            following.append((a[edge : edge + 1], b[edge : edge + 1], a_first))
+        return tuple(following)
+
+    one, zero = jnp.ones((1, units), f32), jnp.zeros((1, units), f32)
+    maps = lax.fori_loop(0, tiles, step, ((one, zero, one),) * batches)
+    return [(prod, state) for prod, state, _ in maps]
+
+
+def entry_states(ends_ref, got_ref, index, count, batches, sign):
+    states = []
+    for batch in range(batches):
+        state = jnp.zeros_like(ends_ref[0:1, :])
+        for distance in range(count - 1, 0, -1):
+            there = index - distance >= 0 if sign > 0 else index + distance < count
+            prods = got_ref[distance - 1, batch : batch + 1, :]
+            longer = got_ref[distance - 1, batches + batch : batches + batch + 1, :] + prods * state
+            state = jnp.where(there, longer, 0.0)
+        states.append(state)
+    return states
+
+
+head_copies = 9 * (ring_count - 1) + 5
+row_block = 32
+
+
+def head_body(
+    count,
+    fsdp,
+    batches,
+    tokens_ref,
+    cot_ref,
+    gain_one_ref,
+    gain_two_ref,
+    branch_ref,
+    inner_ref,
+    out_ref,
+    gate_ref,
+    up_ref,
+    down_ref,
+    taps_ref,
+    vectors_ref,
+    gate_square_ref,
+    input_square_ref,
+    fresh_ref,
+    branch_all,
+    inner_all,
+    out_all,
+    gate_all,
+    up_all,
+    down_all,
+    cot_out,
+    normed_out,
+    branch_pre,
+    padded,
+    conv_low,
+    gate_pre,
+    input_pre,
+    carries,
+    states,
+    ends,
+    mixed_low,
+    own_values,
+    own_middle,
+    normed_two,
+    tokens_low,
+    gains,
+    prods,
+    local_states,
+    edges_sent,
+    edges_got,
+    ends_sent,
+    ends_got,
+    half_sent,
+    half_kept,
+    half_got,
+    own_sent,
+    own_got,
+    local_sems,
+    send_sems,
+    recv_sems,
+):
+    index, unit = lax.axis_index("seq"), lax.axis_index("fsdp")
+    place = ring_place(index, count)
+    forth, back = {"seq": ring_index(place + 1, count)}, {"seq": ring_index(place - 1, count)}
+    along, beside = peers(count, fsdp)
+    copies = Copies(send_sems, recv_sems)
+    rows, width = tokens_ref.shape
+    units = branch_ref.shape[1]
+    length, slab = rows // batches, width // count
+    half = slab // 2
+    core, side = lax.rem(unit, 2), lax.rem(unit // 2, 2)
+    mid, own = rows // 2, rows // 4
+
+    locals_of = []
+    for source, target in zip(
+        (branch_ref, inner_ref, out_ref, gate_ref, up_ref, down_ref),
+        (branch_all, inner_all, out_all, gate_all, up_all, down_all),
+    ):
+        copy = pltpu.make_async_copy(
+            source, target.at[pl.ds(0, slab)], local_sems.at[len(locals_of)]
+        )
+        copy.start()
+        locals_of.append(copy)
+
+    greet(along + beside)
+
+    pairs = {
+        "front": ((branch_ref, branch_all, 0, slab), (inner_ref, inner_all, 0, slab)),
+        "out": ((out_ref, out_all, 0, half), (out_ref, out_all, half, half)),
+        "mlp": ((gate_ref, gate_all, 0, slab), (up_ref, up_all, 0, slab)),
+        "down": ((down_ref, down_all, 0, half), (down_ref, down_all, half, half)),
+    }
+    under_way = {}
+
+    def start(name, step):
+        for way in (0, 1):
+            shard, whole, first, size = pairs[name][way]
+            if step > 1:
+                under_way[name, way].wait_recv()
+            there = (count - step) % count if way else step
+            here = (there + 1) % count if way else step - 1
+            source = (
+                shard.at[pl.ds(first, size)]
+                if step == 1
+                else whole.at[pl.ds(here * slab + first, size)]
+            )
+            under_way[name, way] = copies.start(
+                source, whole.at[pl.ds(there * slab + first, size)], back if way else forth
+            )
+
+    def finish(name):
+        for way in (0, 1):
+            under_way[name, way].wait_recv()
+
+    start("front", 1)
+    start("out", 1)
+
+    for k in range(count):
+        plain = pl.ds(pl.multiple_of(ring_index(place - k, count) * slab, slab), slab)
+        part = slice(k * slab, (k + 1) * slab)
+        tokens_low[:, part] = tokens_ref[:, plain]
+        gains[0:1, part] = gain_one_ref[:, plain]
+        gains[1:2, part] = gain_two_ref[:, plain]
+    start("front", 2)
+    start("out", 2)
+
+    def norm_block(block, carry):
+        at = rows_at(block * row_block, row_block)
+        values = tokens_low[at, :].astype(f32)
+        scale = lax.rsqrt(jnp.mean(values * values, axis=-1, keepdims=True) + eps)
+        normed_out[at, :] = (values * scale * gains[0:1, :]).astype(bf16)
+        return carry
+
+    lax.fori_loop(0, rows // row_block, norm_block, 0)
+    own_values[...] = tokens_low[rows_at(core * mid + side * own, own), :].astype(f32)
+    start("front", 3)
+    start("out", 3)
+    for k in range(count):
+        plain = pl.ds(pl.multiple_of(ring_index(place - k, count) * slab, slab), slab)
+        cot_out[:, k * slab : (k + 1) * slab] = cot_ref[:, plain]
+    for step in range(4, count):
+        start("front", step)
+        start("out", step)
+    start("mlp", 1)
+    start("down", 1)
+    for copy in locals_of:
+        copy.wait()
+    finish("front")
+
+    for batch in range(batches):
+        at = slice(batch * length, (batch + 1) * length)
+        top = batch * (length + 8)
+        inner = jnp.dot(normed_out[at, :], inner_all[...], preferred_element_type=f32)
+        padded[top + 8 : top + 8 + length, :] = inner.astype(bf16).astype(f32)
+        edges_sent[batch] = padded[top + length : top + length + 8, :]
+    edge_copy = copies.start(edges_sent, edges_got, along[0])
+    for batch in range(batches):
+        at = slice(batch * length, (batch + 1) * length)
+        branch_pre[at, :] = jnp.dot(
+            normed_out[at, :], branch_all[...], preferred_element_type=f32
+        )
+    edge_copy.wait_recv()
+    for batch in range(batches):
+        top = batch * (length + 8)
+        padded[top : top + 8, :] = jnp.where(index > 0, edges_got[batch], 0.0)
+    start("mlp", 2)
+    bias, gate_bias, input_bias, rate = [vectors_ref[i : i + 1, :] for i in range(4)]
+
+    def conv_block(block, carry):
+        batch = block // (length // row_block)
+        wide = padded[rows_at(block * row_block + batch * 8, row_block + 8, 8), :]
+        total = bias + taps_ref[0:1, :] * wide[8:] + taps_ref[1:2, :] * wide[7:-1]
+        total = total + taps_ref[2:3, :] * wide[6:-2] + taps_ref[3:4, :] * wide[5:-3]
+        conv_low[rows_at(block * row_block, row_block), :] = total.astype(bf16)
+        return carry
+
+    lax.fori_loop(0, rows // row_block, conv_block, 0)
+    for batch in range(batches):
+        at = slice(batch * length, (batch + 1) * length)
+        conv = conv_low[at, :]
+        gate_pre[at, :] = (
+            jnp.dot(conv, gate_square_ref[...], preferred_element_type=f32) + gate_bias
+        )
+        input_pre[at, :] = (
+            jnp.dot(conv, input_square_ref[...], preferred_element_type=f32) + input_bias
+        )
+    start("down", 2)
+
+    def gate_block(block, carry):
+        at = rows_at(block * row_block, row_block)
+        rate_gate = jax.nn.sigmoid(gate_pre[at, :])
+        inlet_gate = jax.nn.sigmoid(input_pre[at, :])
+        log_decay = rate * rate_gate
+        decay = jnp.exp(log_decay)
+        fresh = fresh_ref[at, :] > 0
+        scale = jnp.sqrt(-jnp.tanh(log_decay) * (1.0 + decay * decay))
+        carries[at, :] = jnp.where(fresh, 0.0, decay)
+        local_states[at, :] = (
+            jnp.where(fresh, 1.0, scale) * inlet_gate * conv_low[at, :].astype(f32)
+        )
+        return carry
+
+    lax.fori_loop(0, rows // row_block, gate_block, 0)
+    scanned = scan_rows(carries, local_states, prods, local_states, batches, False)
+    ends_sent[...] = jnp.zeros_like(ends_sent)
+    for batch, (prod, state) in enumerate(scanned):
+        ends_sent[batch : batch + 1, :] = prod
+        ends_sent[batches + batch : batches + batch + 1, :] = state
+    ends[...] = ends_sent[...]
+    end_copies = [
+        copies.start(ends_sent, ends_got.at[distance - 1], along[distance - 1])
+        for distance in range(1, count)
+    ]
+    start("mlp", 3)
+    for copy in end_copies:
+        copy.wait_recv()
+    entries = entry_states(ends, ends_got, index, count, batches, 1)
+
+    for batch in range(batches):
+        entry = entries[batch]
+        top = batch * (length + 8)
+        states[top : top + 8, :] = jnp.broadcast_to(entry, (8, units))
+
+        def state_block(block, carry, batch=batch, entry=entry):
+            at = rows_at(batch * length + block * row_block, row_block)
+            state = local_states[at, :] + prods[at, :] * entry
+            states[rows_at(8 + batch * (length + 8) + block * row_block, row_block, 8), :] = state
+            mixed_low[at, :] = (state * gelu_tanh(branch_pre[at, :])).astype(bf16)
+            return carry
+
+        lax.fori_loop(0, length // row_block, state_block, 0)
+    start("down", 3)
+    finish("out")
+    for part, result in dot_slabs(
+        mixed_low[rows_at((1 - core) * mid, mid), :], out_all, slab, count
+    ):
+        half_sent[:, part] = result.astype(bf16)
+    half_copy = copies.start(half_sent, half_got, beside[0])
+    for part, result in dot_slabs(mixed_low[rows_at(core * mid, mid), :], out_all, slab, count):
+        half_kept[:, part] = result
+    half_copy.wait_recv()
+    other, mine = rows_at((1 - side) * own, own), rows_at(side * own, own)
+    own_sent[...] = (half_kept[other, :] + half_got[other, :].astype(f32)).astype(bf16)
+    own_copy = copies.start(own_sent, own_got, beside[1])
+    start("mlp", 4)
+    start("down", 4)
+    own_copy.wait_recv()
+    middle = own_values[...] + (
+        half_kept[mine, :] + half_got[mine, :].astype(f32) + own_got[...].astype(f32)
+    )
+    own_middle[...] = middle
+    scale = lax.rsqrt(jnp.mean(middle * middle, axis=-1, keepdims=True) + eps)
+    own_at, both_at = rows_at(core * mid + side * own, own), rows_at(core * mid, mid)
+    normed_two[own_at, :] = (middle * scale * gains[1:2, :]).astype(bf16)
+    join_copy = copies.start(normed_two.at[own_at], normed_two.at[own_at], beside[1])
+    start("mlp", 5)
+    join_copy.wait_recv()
+    join_copy = copies.start(normed_two.at[both_at], normed_two.at[both_at], beside[0])
+    start("down", 5)
+    join_copy.wait_recv()
+    for step in range(6, count):
+        start("mlp", step)
+        start("down", step)
+    finish("mlp")
+    finish("down")
+    copies.end()
+
+
+def head(count, fsdp, batches, *operands):
+    tokens = operands[0]
+    branch, gate = operands[4], operands[7]
+    rows, width = tokens.shape
+    slab, units = branch.shape
+    hidden = gate.shape[1]
+    length = rows // batches
+    whole, place = pl.BlockSpec(memory_space=pltpu.VMEM), pl.BlockSpec(memory_space=pl.ANY)
+
+    def array(dtype, *shape):
+        return jax.ShapeDtypeStruct(shape, dtype)
+
+    outs = (
+        [array(bf16, width, units)] * 3
+        + [array(bf16, width, hidden)] * 3
+        + [array(bf16, rows, width)] * 2
+        + [array(f32, rows, units), array(f32, rows + 8 * batches, units), array(bf16, rows, units)]
+        + [array(f32, rows, units)] * 3
+        + [array(f32, rows + 8 * batches, units)]
+        + [array(f32, 8, units), array(bf16, rows, units)]
+        + [array(f32, rows // 4, width)] * 2
+        + [array(bf16, rows, width)]
+    )
+    return pl.pallas_call(
+        functools.partial(head_body, count, fsdp, batches),
+        out_shape=tuple(outs),
+        in_specs=[whole] * 4 + [place] * 6 + [whole] * 5,
+        out_specs=tuple([whole] * 3 + [place] * 3 + [whole] * (len(outs) - 6)),
+        scratch_shapes=[
+            pltpu.VMEM((rows, width), bf16),
+            pltpu.VMEM((8, width), f32),
+            pltpu.VMEM((rows, units), f32),
+            pltpu.VMEM((rows, units), f32),
+            pltpu.VMEM((batches, 8, units), f32),
+            pltpu.VMEM((batches, 8, units), f32),
+            pltpu.VMEM((8, units), f32),
+            pltpu.VMEM((count - 1, 8, units), f32),
+            pltpu.VMEM((rows // 2, width), bf16),
+            pltpu.VMEM((rows // 2, width), f32),
+            pltpu.VMEM((rows // 2, width), bf16),
+            pltpu.VMEM((rows // 4, width), bf16),
+            pltpu.VMEM((rows // 4, width), bf16),
+            pltpu.SemaphoreType.DMA((6,)),
+            pltpu.SemaphoreType.DMA((head_copies,)),
+            pltpu.SemaphoreType.DMA((head_copies,)),
+        ],
+        compiler_params=pltpu.CompilerParams(
+            collective_id=1, has_side_effects=True, vmem_limit_bytes=60 * 1024 * 1024
+        ),
+    )(*operands)
+
+
+def gelu_slope(values):
+    constant = 0.7978845608028654
+    bent = jnp.tanh(constant * (values + 0.044715 * values * values * values))
+    inner = constant * (1.0 + 3.0 * 0.044715 * values * values)
+    return 0.5 * (1.0 + bent) + 0.5 * values * (1.0 - bent * bent) * inner
+
+
+ring_slots = 3
+back_sends = 2 * 2 * (ring_count - 1)
+back_copies = 4 + 4 + (ring_count - 1) + 1
+
+
+class RingSum:
+    def __init__(self, terms, slots, sends, arrivals, credits, count, neighbours):
+        self.terms, self.slots, self.count = terms, slots, count
+        self.sends, self.arrivals, self.credits = sends, arrivals, credits
+        self.neighbours = neighbours
+        self.copies = [[], []]
+
+    def send(self, way, step, total):
+        here, there = (step - 1) % ring_slots, step % ring_slots
+        self.slots[way, here] = total.astype(bf16)
+        if step >= ring_slots:
+            pl.semaphore_wait(self.credits.at[way], 1)
+        copy = pltpu.make_async_remote_copy(
+            src_ref=self.slots.at[way, here],
+            dst_ref=self.slots.at[way, there],
+            send_sem=self.sends.at[way, step - 1],
+            recv_sem=self.arrivals.at[way, step - 1],
+            device_id=self.neighbours[way],
+            device_id_type=pl.DeviceIdType.MESH,
+        )
+        copy.start()
+        self.copies[way].append(copy)
+        if step >= 2:
+            self.copies[way][step - 2].wait_send()
+            if step + 1 < self.count:
+                pl.semaphore_signal(
+                    self.credits.at[way],
+                    inc=1,
+                    device_id=self.neighbours[1 - way],
+                    device_id_type=pl.DeviceIdType.MESH,
+                )
+
+    def serve(self, step, end=None):
+        for way in (0, 1):
+            k = (self.count - step) % self.count if way else step % self.count
+            own = self.terms[way](k)
+            if step == 1:
+                self.send(way, 1, own)
+                continue
+            self.copies[way][step - 2].wait_recv()
+            total = self.slots[way, (step - 1) % ring_slots].astype(f32) + own
+            if step < self.count:
+                self.send(way, step, total)
+            else:
+                self.copies[way][step - 2].wait_send()
+                end(way, total)
+
+
+def back_body(
+    count,
+    fsdp,
+    batches,
+    cot_ref,
+    hidden_ref,
+    normed_ref,
+    gate_low_ref,
+    up_low_ref,
+    branch_pre,
+    padded,
+    conv_low,
+    gate_pre,
+    input_pre,
+    carries,
+    states,
+    ends_ref,
+    gate_square_ref,
+    input_square_ref,
+    own_middle,
+    fresh_ref,
+    taps_ref,
+    vectors_ref,
+    gain_two_ref,
+    gate_all,
+    up_all,
+    down_all,
+    out_all,
+    mixed_out,
+    middle_low,
+    own_grad,
+    branch_low,
+    inner_low,
+    gate_low,
+    input_low,
+    small_out,
+    gain_grad_out,
+    gate_grad,
+    up_grad,
+    down_grad,
+    half_sent,
+    half_kept,
+    half_got,
+    own_sent,
+    own_got,
+    prods,
+    adjoints,
+    conv_grad,
+    edges_sent,
+    edges_got,
+    ends_sent,
+    ends_got,
+    mlp_slots,
+    down_slots,
+    stream_one,
+    stream_two,
+    stream_out,
+    stage,
+    stream_sems,
+    stage_sems,
+    ring_sends,
+    ring_arrivals,
+    ring_credits,
+    send_sems,
+    recv_sems,
+):
+    index, unit = lax.axis_index("seq"), lax.axis_index("fsdp")
+    place = ring_place(index, count)
+    neighbours = (
+        {"seq": ring_index(place + 1, count)},
+        {"seq": ring_index(place - 1, count)},
+    )
+    along, beside = peers(count, fsdp)
+    copies = Copies(send_sems, recv_sems)
+    rows, width = cot_ref.shape
+    units = branch_pre.shape[1]
+    length, slab = rows // batches, width // count
+    half = slab // 2
+    core, side = lax.rem(unit, 2), lax.rem(unit // 2, 2)
+    mid, own = rows // 2, rows // 4
+    kept_at, sent_at = rows_at(core * mid, mid), rows_at((1 - core) * mid, mid)
+    mine, other = rows_at(side * own, own), rows_at((1 - side) * own, own)
+    own_at = rows_at(core * mid + side * own, own)
+    tn = (((0,), (0,)), ((), ()))
+
+    greet(along + beside)
+
+    def mlp_term(right):
+        return lambda k: lax.dot_general(
+            normed_ref[:, k * slab : (k + 1) * slab], right[...], tn, preferred_element_type=f32
+        )
+
+    def down_term(first):
+        return lambda k: lax.dot_general(
+            cot_ref[:, k * slab + first : k * slab + first + half],
+            hidden_ref[...],
+            tn,
+            preferred_element_type=f32,
+        )
+
+    mlp = RingSum(
+        [mlp_term(gate_low_ref), mlp_term(up_low_ref)],
+        mlp_slots,
+        ring_sends.at[0],
+        ring_arrivals.at[0],
+        ring_credits.at[0],
+        count,
+        neighbours,
+    )
+    down = RingSum(
+        [down_term(0), down_term(half)],
+        down_slots,
+        ring_sends.at[1],
+        ring_arrivals.at[1],
+        ring_credits.at[1],
+        count,
+        neighbours,
+    )
+    mlp.serve(1)
+    down.serve(1)
+
+    def streamed(sources, buffers, first_sem):
+        def fetch(k):
+            fetched = []
+            for number, (source, buffer) in enumerate(zip(sources, buffers)):
+                copy = pltpu.make_async_copy(
+                    source.at[pl.ds(k * slab, slab)],
+                    buffer.at[k % 2],
+                    stream_sems.at[first_sem + number * count + k],
+                )
+                copy.start()
+                fetched.append(copy)
+            return fetched
+
+        fetched = fetch(0)
+        for k in range(count):
+            for copy in fetched:
+                copy.wait()
+            if k + 1 < count:
+                fetched = fetch(k + 1)
+            yield k, [buffer[k % 2] for buffer in buffers]
+
+    def nt(left, right):
+        return lax.dot_general(
+            left, right, (((1,), (1,)), ((), ())), preferred_element_type=f32
+        )
+
+    for k, (gate, up) in streamed((gate_all, up_all), (stream_one, stream_two), 0):
+        part = slice(k * slab, (k + 1) * slab)
+        half_sent[:, part] = (
+            nt(gate_low_ref[sent_at, :], gate) + nt(up_low_ref[sent_at, :], up)
+        ).astype(bf16)
+        half_kept[:, part] = nt(gate_low_ref[kept_at, :], gate) + nt(up_low_ref[kept_at, :], up)
+    half_copy = copies.start(half_sent, half_got, beside[0])
+    half_copy.wait_recv()
+    own_sent[...] = (half_kept[other, :] + half_got[other, :].astype(f32)).astype(bf16)
+    own_copy = copies.start(own_sent, own_got, beside[1])
+    mlp.serve(2)
+    down.serve(2)
+    own_copy.wait_recv()
+    middle = own_middle[...]
+    scale = lax.rsqrt(jnp.mean(middle * middle, axis=-1, keepdims=True) + eps)
+    unit_values = middle * scale
+    front = half_kept[mine, :] + half_got[mine, :].astype(f32) + own_got[...].astype(f32)
+    gain_grad_out[...] = jnp.zeros_like(gain_grad_out)
+    gain_grad_out[0:1, :] = jnp.sum(front * unit_values, 0, keepdims=True)
+    weighted = front * gain_two_ref[...]
+    result = cot_ref[own_at, :].astype(f32) + scale * (
+        weighted - unit_values * jnp.mean(weighted * unit_values, axis=-1, keepdims=True)
+    )
+    own_grad[...] = result
+    middle_low[own_at, :] = result.astype(bf16)
+    join_copy = copies.start(middle_low.at[own_at], middle_low.at[own_at], beside[1])
+    mlp.serve(3)
+    join_copy.wait_recv()
+    join_copy = copies.start(middle_low.at[kept_at], middle_low.at[kept_at], beside[0])
+    down.serve(3)
+    join_copy.wait_recv()
+
+    for k, (out,) in streamed((out_all,), (stream_out,), 2 * count):
+        for batch in range(batches):
+            at = slice(batch * length, (batch + 1) * length)
+            more = jnp.dot(
+                middle_low[at, k * slab : (k + 1) * slab], out, preferred_element_type=f32
+            )
+            adjoints[at, :] = more if k == 0 else adjoints[at, :] + more
+
+    def mixed_block(block, carry):
+        batch = block // (length // row_block)
+        at = rows_at(block * row_block, row_block)
+        back, before = adjoints[at, :], branch_pre[at, :]
+        state = states[rows_at(block * row_block + batch * 8 + 8, row_block, 8), :]
+        branch_low[at, :] = (back * state * gelu_slope(before)).astype(bf16)
+        adjoints[at, :] = back * gelu_tanh(before)
+        return carry
+
+    lax.fori_loop(0, rows // row_block, mixed_block, 0)
+    scanned = scan_rows(carries, adjoints, prods, adjoints, batches, True)
+    ends_sent[...] = ends_ref[...]
+    for batch, (_, state) in enumerate(scanned):
+        top = batch * length
+        ends_sent[batches + batch : batches + batch + 1, :] = carries[top : top + 1, :] * state
+    end_copies = [
+        copies.start(ends_sent, ends_got.at[distance - 1], along[count - distance - 1])
+        for distance in range(1, count)
+    ]
+    mlp.serve(4)
+    for copy in end_copies:
+        copy.wait_recv()
+    entries = entry_states(ends_sent, ends_got, index, count, batches, -1)
+
+    bias, gate_bias, input_bias, rate, slope = [vectors_ref[i : i + 1, :] for i in range(5)]
+    zero = jnp.zeros((1, units), f32)
+    sums = (zero, zero, zero)
+    for batch in range(batches):
+        entry = entries[batch]
+
+        def gate_block(block, sums, batch=batch, entry=entry):
+            top = batch * length + block * row_block
+            at = rows_at(top, row_block)
+            rate_gate = jax.nn.sigmoid(gate_pre[at, :])
+            inlet_gate = jax.nn.sigmoid(input_pre[at, :])
+            log_decay = rate * rate_gate
+            decay = jnp.exp(log_decay)
+            fresh = fresh_ref[at, :] > 0
+            scale = jnp.sqrt(-jnp.tanh(log_decay) * (1.0 + decay * decay))
+            conv = conv_low[at, :].astype(f32)
+            lam = adjoints[at, :] + prods[at, :] * entry
+            before = states[rows_at(top + batch * 8, row_block + 8, 8), :][7:-1]
+            drawn = inlet_gate * conv
+            log_grad = jnp.where(
+                fresh, 0.0, lam * before * decay - lam * (decay * decay / scale) * drawn
+            )
+            passed = lam * jnp.where(fresh, 1.0, scale)
+            gate_grad_low = (log_grad * rate * (rate_gate * (1.0 - rate_gate))).astype(bf16)
+            input_grad_low = (passed * conv * (inlet_gate * (1.0 - inlet_gate))).astype(bf16)
+            gate_low[at, :] = gate_grad_low
+            input_low[at, :] = input_grad_low
+            conv_grad[rows_at(top + batch * 8, row_block, 8), :] = passed * inlet_gate
+            terms = (
+                gate_grad_low.astype(f32),
+                input_grad_low.astype(f32),
+                log_grad * rate_gate,
+            )
+            return tuple(
+                total + jnp.sum(more, 0, keepdims=True) for total, more in zip(sums, terms)
+            )
+
+        sums = lax.fori_loop(0, length // row_block, gate_block, sums)
+        if batch == 0:
+            down.serve(4)
+    for batch in range(batches):
+        at, top = slice(batch * length, (batch + 1) * length), batch * (length + 8)
+        conv_grad[top : top + length, :] = (
+            conv_grad[top : top + length, :]
+            + nt(gate_low[at, :], gate_square_ref[...])
+            + nt(input_low[at, :], input_square_ref[...])
+        )
+        edges_sent[batch] = conv_grad[top : top + 8, :]
+    edge_copy = copies.start(edges_sent, edges_got, along[count - 2])
+    mlp.serve(5)
+
+    copies.sent(half_copy)
+    copies.sent(own_copy)
+    for k, (turned,) in streamed((down_all,), (stream_one,), 3 * count):
+        part = slice(k * slab, (k + 1) * slab)
+        half_sent[:, part] = nt(hidden_ref[sent_at, :], turned).astype(bf16)
+        half_kept[:, part] = nt(hidden_ref[kept_at, :], turned)
+    mixed_copy = copies.start(half_sent, half_got, beside[0])
+    down.serve(5)
+
+    edge_copy.wait_recv()
+    for batch in range(batches):
+        top = batch * (length + 8) + length
+        conv_grad[top : top + 8, :] = jnp.where(index < count - 1, edges_got[batch], 0.0)
+
+    def conv_block(block, sums):
+        batch = block // (length // row_block)
+        at = rows_at(block * row_block + batch * 8, row_block + 8, 8)
+        wide, inner = conv_grad[at, :], padded[at, :]
+        total = taps_ref[0:1, :] * wide[:-8] + taps_ref[1:2, :] * wide[1:-7]
+        total = total + taps_ref[2:3, :] * wide[2:-6] + taps_ref[3:4, :] * wide[3:-5]
+        inner_low[rows_at(block * row_block, row_block), :] = total.astype(bf16)
+        near = wide[:-8]
+        terms = [near * inner[8 - k : 8 - k + row_block] for k in range(4)] + [near]
+        return tuple(
+            total + jnp.sum(more, 0, keepdims=True) for total, more in zip(sums, terms)
+        )
+
+    conv_sums = lax.fori_loop(0, rows // row_block, conv_block, (zero,) * 5)
+    for number, total in enumerate((*conv_sums, sums[0], sums[1], sums[2] * slope)):
+        small_out[number : number + 1, :] = total
+
+    mixed_copy.wait_recv()
+    own_sent[...] = (half_kept[other, :] + half_got[other, :].astype(f32)).astype(bf16)
+    own_copy = copies.start(own_sent, own_got, beside[1])
+    mlp.serve(6)
+    down.serve(6)
+    own_copy.wait_recv()
+    final = own_middle[...] + (
+        half_kept[mine, :] + half_got[mine, :].astype(f32) + own_got[...].astype(f32)
+    )
+    final = final.astype(bf16)
+    for k in range(count):
+        to = pl.ds(pl.multiple_of(ring_index(place - k, count) * slab, slab), slab)
+        mixed_out[own_at, to] = final[:, k * slab : (k + 1) * slab]
+    join_copy = copies.start(mixed_out.at[own_at], mixed_out.at[own_at], beside[1])
+    mlp.serve(7)
+    join_copy.wait_recv()
+    join_copy = copies.start(mixed_out.at[kept_at], mixed_out.at[kept_at], beside[0])
+    down.serve(7)
+    join_copy.wait_recv()
+
+    def mlp_end(way, total):
+        stage[...] = total
+        copy = pltpu.make_async_copy(stage, up_grad if way else gate_grad, stage_sems.at[way])
+        copy.start()
+        copy.wait()
+
+    def down_end(way, total):
+        stage[way * half : (way + 1) * half, :] = total
+
+    mlp.serve(8, mlp_end)
+    down.serve(8, down_end)
+    copy = pltpu.make_async_copy(stage, down_grad, stage_sems.at[2])
+    copy.start()
+    copy.wait()
+    copies.end()
+
+
+def back(count, fsdp, batches, *operands):
+    cot, hidden = operands[0], operands[1]
+    branch_pre = operands[5]
+    rows, width = cot.shape
+    units, inner = branch_pre.shape[1], hidden.shape[1]
+    slab, length = width // count, rows // batches
+    whole, place = pl.BlockSpec(memory_space=pltpu.VMEM), pl.BlockSpec(memory_space=pl.ANY)
+
+    def array(dtype, *shape):
+        return jax.ShapeDtypeStruct(shape, dtype)
+
+    outs = [
+        array(bf16, rows, width),
+        array(bf16, rows, width),
+        array(f32, rows // 4, width),
+        *[array(bf16, rows, units)] * 4,
+        array(f32, 8, units),
+        array(f32, 8, width),
+        *[array(f32, slab, inner)] * 3,
+    ]
+    return pl.pallas_call(
+        functools.partial(back_body, count, fsdp, batches),
+        out_shape=tuple(outs),
+        in_specs=[whole] * (len(operands) - 4) + [place] * 4,
+        out_specs=tuple([whole] * 9 + [place] * 3),
+        scratch_shapes=[
+            pltpu.VMEM((rows // 2, width), bf16),
+            pltpu.VMEM((rows // 2, width), f32),
+            pltpu.VMEM((rows // 2, width), bf16),
+            pltpu.VMEM((rows // 4, width), bf16),
+            pltpu.VMEM((rows // 4, width), bf16),
+            pltpu.VMEM((rows, units), f32),
+            pltpu.VMEM((rows, units), f32),
+            pltpu.VMEM((rows + 8 * batches, units), f32),
+            pltpu.VMEM((batches, 8, units), f32),
+            pltpu.VMEM((batches, 8, units), f32),
+            pltpu.VMEM((8, units), f32),
+            pltpu.VMEM((count - 1, 8, units), f32),
+            pltpu.VMEM((2, ring_slots, slab, inner), bf16),
+            pltpu.VMEM((2, ring_slots, slab // 2, inner), bf16),
+            pltpu.VMEM((2, slab, inner), bf16),
+            pltpu.VMEM((2, slab, inner), bf16),
+            pltpu.VMEM((2, slab, units), bf16),
+            pltpu.VMEM((slab, inner), f32),
+            pltpu.SemaphoreType.DMA((4 * count,)),
+            pltpu.SemaphoreType.DMA((3,)),
+            pltpu.SemaphoreType.DMA((2, 2, count - 1)),
+            pltpu.SemaphoreType.DMA((2, 2, count - 1)),
+            pltpu.SemaphoreType.REGULAR((2, 2)),
+            pltpu.SemaphoreType.DMA((back_copies,)),
+            pltpu.SemaphoreType.DMA((back_copies,)),
+        ],
+        compiler_params=pltpu.CompilerParams(
+            collective_id=2, has_side_effects=True, vmem_limit_bytes=63 * 1024 * 1024
+        ),
+    )(*operands)
+
+
 def block_diagonal(blocks):
     count, width = blocks.shape[0], blocks.shape[1]
     return sum(
@@ -762,7 +1603,7 @@
     slab = width // count
     units, hidden = conv_bias.shape[0], down_weight.shape[0]
     rows = batches * length
-    ringed = count <= ring_limit
+    ringed = count == ring_count and lax.axis_size("fsdp") == 4
     half = slab // 2
     out_turned, down_turned = out_weight.T, down_weight.T
     ring = Ring(count)
@@ -803,86 +1644,199 @@
         return term
 
     steps = count - 1
-    front_weights = gather(branch_weight, inner_weight)
-    out_weights = gather(out_turned[:half], out_turned[half:])
-    mlp_weights = gather(gate_weight, up_weight)
-    down_weights = gather(down_turned[:half], down_turned[half:])
-    in_turn(front_weights, out_weights)
-    tokens_low = moved(tokens.reshape(rows, width), bf16)
-    ring.first(tokens_low)
-    in_turn(front_weights, out_weights)
+    taps = conv_weight.astype(f32)
+    decay = decay_param.astype(f32)
+    gate_square, input_square = block_diagonal(gate_blocks), block_diagonal(input_blocks)
+    fresh_start = resets[:, :, None] > 0
     gain_one = gain_moved(norm_gain.astype(f32))
     gain_two = gain_moved(mlp_norm_gain.astype(f32))
-    values = ring.then(tokens_low, 2).astype(f32)
-    normed = (values * inverse_rms(values) * gain_one).astype(bf16)
-    ring.first(normed)
-    in_turn(front_weights, out_weights)
-    gate_square, input_square = block_diagonal(gate_blocks), block_diagonal(input_blocks)
-    ring.first(gate_square, input_square)
-    in_turn(front_weights, out_weights)
-    cot_low = moved(ring.then(cotangent, 2).reshape(rows, width), bf16)
-    ring.first(cot_low)
-    for _ in range(steps - 4):
-        in_turn(front_weights, out_weights)
-    branch_all, inner_all = (jnp.concatenate(slabs, 0) for slabs in front_weights.slabs())
-    out_all = rows_joined(out_weights.slabs())
-
-    taps = conv_weight.astype(f32)
-    decay = decay_param.astype(f32)
-    fresh_start = resets[:, :, None] > 0
-    in_turn(mlp_weights)
-    inner_low = dot_nn(normed, inner_all).astype(bf16).reshape(batches, length, units)
-    branch_pre = dot_nn(normed, branch_all).reshape(batches, length, units)
-    edge_rows = passed_along(inner_low[:, -3:], 1)
-    ring.first(inner_low, branch_pre)
-    in_turn(down_weights)
-    padded = jnp.concatenate([ring.then(edge_rows, 2), inner_low], 1).astype(f32)
-    conv_sum = conv_bias.astype(f32) + taps[0] * padded[:, 3:] + taps[1] * padded[:, 2:-1]
-    conv_sum = conv_sum + taps[2] * padded[:, 1:-2] + taps[3] * padded[:, :-3]
-    conv_low = conv_sum.astype(bf16)
-    conv_flat = conv_low.reshape(rows, units)
-    gate_pre = dot_nn(conv_flat, gate_square).reshape(batches, length, units)
-    gate_pre = gate_pre + gate_bias.astype(f32)
-    input_pre = dot_nn(conv_flat, input_square).reshape(batches, length, units)
-    input_pre = input_pre + input_bias.astype(f32)
-    conv_value = conv_low.astype(f32)
 
     def gates(gate_pre, input_pre, conv_value, decay):
         return gate_math(gate_pre, input_pre, conv_value, decay, fresh_start)
 
-    carries, drives = gates(gate_pre, input_pre, conv_value, decay)
-    ring.first(carries, drives)
-    in_turn(mlp_weights)
-    prods, local_state = local_scan(ring.then(carries, 2), drives, False)
-    entry = Entry(prods[:, -1:], local_state[:, -1:], 1)
-    ring.first(prods)
-    in_turn(down_weights)
-    entry.between(ring.then)
-    in_turn(mlp_weights)
-    state_in = entry.state(lambda part: ring.then(part, 1))
-    ring.first(state_in)
-    in_turn(down_weights)
-    states = local_state + prods * ring.then(state_in, 2)
-
+    def by_sequence(values):
+        return values.reshape(batches, -1, values.shape[-1])
+
+    if ringed:
+        vectors = jnp.stack(
+            [
+                conv_bias.astype(f32),
+                gate_bias.astype(f32),
+                input_bias.astype(f32),
+                -decay_scale * jax.nn.softplus(-decay),
+            ],
+            0,
+        )
+        (
+            branch_all,
+            inner_all,
+            out_all,
+            gate_all,
+            up_all,
+            down_all,
+            cot_low,
+            normed,
+            branch_pre,
+            padded,
+            conv_flat,
+            gate_pre,
+            input_pre,
+            carries,
+            states,
+            ends,
+            mixed_low,
+            own_values,
+            own_middle,
+            normed_two,
+        ) = head(
+            count,
+            lax.axis_size("fsdp"),
+            batches,
+            tokens.reshape(rows, width),
+            cotangent.reshape(rows, width),
+            norm_gain.astype(f32)[None],
+            mlp_norm_gain.astype(f32)[None],
+            branch_weight,
+            inner_weight,
+            out_turned,
+            gate_weight,
+            up_weight,
+            down_turned,
+            taps,
+            vectors,
+            gate_square,
+            input_square,
+            resets.reshape(rows, 1),
+        )
+        gate_mlp, up_mlp = dot_nn(normed_two, gate_all), dot_nn(normed_two, up_all)
+        activated, act_pull = jax.vjp(gated_product, gate_mlp, up_mlp)
+        hidden_low = activated.astype(bf16)
+        grad_gate_mlp, grad_up_mlp = act_pull(dot_nn(cot_low, down_all))
+        (
+            mixed,
+            middle_low,
+            own_grad,
+            branch_low,
+            inner_grad_low,
+            gate_low,
+            input_low,
+            small,
+            gain_two_grad,
+            gate_grad,
+            up_grad,
+            down_grad,
+        ) = back(
+            count,
+            lax.axis_size("fsdp"),
+            batches,
+            cot_low,
+            hidden_low,
+            normed_two,
+            grad_gate_mlp.astype(bf16),
+            grad_up_mlp.astype(bf16),
+            branch_pre,
+            padded,
+            conv_flat,
+            gate_pre,
+            input_pre,
+            carries,
+            states,
+            ends,
+            gate_square,
+            input_square,
+            own_middle,
+            resets.reshape(rows, 1),
+            taps,
+            jnp.concatenate([vectors, decay_scale * jax.nn.sigmoid(-decay)[None]], 0),
+            gain_two[None],
+            gate_all,
+            up_all,
+            down_all,
+            out_all,
+        )
+        block_count = gate_blocks.shape[0]
+        block_grads = jnp.concatenate(
+            [
+                diagonal_blocks(dot_tn(conv_flat, gate_low), block_count),
+                diagonal_blocks(dot_tn(conv_flat, input_low), block_count),
+            ],
+            0,
+        )
+        block_width = block_grads.shape[-1]
+        branch_grad, inner_grad, out_grad, tokens_grad, gains, small, block_grads = tail(
+            count,
+            middle_low.T,
+            mixed_low,
+            normed.T,
+            branch_low,
+            inner_grad_low,
+            branch_all,
+            inner_all,
+            own_values,
+            own_grad,
+            gain_one[None],
+            gain_two_grad[:1],
+            small,
+            block_grads.reshape(-1, block_width).astype(bf16),
+        )
+        block_grads = block_grads.astype(f32).reshape(2, block_count, block_width, block_width)
+        return (
+            mixed.astype(f32).reshape(tokens.shape),
+            tokens_grad.astype(f32).reshape(tokens.shape),
+            gains[0],
+            branch_grad,
+            inner_grad,
+            small[:4],
+            small[4],
+            block_grads[0],
+            block_grads[1],
+            small[5],
+            small[6],
+            small[7],
+            out_grad.T,
+            gains[1],
+            gate_grad,
+            up_grad,
+            down_grad.T,
+        )
+    else:
+        branch_all, inner_all, out_all, gate_all, up_all, down_all = [
+            lax.all_gather(piece, "seq", axis=0, tiled=True)
+            for piece in (
+                branch_weight,
+                inner_weight,
+                out_turned,
+                gate_weight,
+                up_weight,
+                down_turned,
+            )
+        ]
+        tokens_low, cot_low = tokens.reshape(rows, width), cotangent.reshape(rows, width)
+        values = tokens_low.astype(f32)
+        normed = (values * inverse_rms(values) * gain_one).astype(bf16)
+        inner_low = by_sequence(dot_nn(normed, inner_all).astype(bf16))
+        branch_pre = by_sequence(dot_nn(normed, branch_all))
+        edge_rows = passed_along(inner_low[:, -3:], 1)
+        padded = jnp.concatenate([edge_rows, inner_low], 1).astype(f32)
+        conv_sum = conv_bias.astype(f32) + taps[0] * padded[:, 3:] + taps[1] * padded[:, 2:-1]
+        conv_sum = conv_sum + taps[2] * padded[:, 1:-2] + taps[3] * padded[:, :-3]
+        conv_flat = conv_sum.astype(bf16).reshape(rows, units)
+        gate_pre = by_sequence(dot_nn(conv_flat, gate_square) + gate_bias.astype(f32))
+        input_pre = by_sequence(dot_nn(conv_flat, input_square) + input_bias.astype(f32))
+        conv_value = by_sequence(conv_flat).astype(f32)
+        carries, drives = gates(gate_pre, input_pre, conv_value, decay)
+        prods, local_state = local_scan(carries, drives, False)
+        prods_end = prods[:, -1:]
+        state_in = Entry(prods_end, local_state[:, -1:], 1).state(None)
+        states = local_state + prods * state_in
+        mixed_low = (states * gelu_tanh(branch_pre)).astype(bf16).reshape(rows, units)
+        own_values = own_rows(tokens_low).astype(f32)
+        own_middle = own_values + Halves(ring, dot_nt(mixed_low, out_all), "fsdp").run()
+        normed_two = own_middle * inverse_rms(own_middle) * gain_two
+        normed_two = Joined(ring, normed_two.astype(bf16), "fsdp").run()
     branch, branch_pull = jax.vjp(gelu_tanh, branch_pre)
-    mixed_low = (states * branch).astype(bf16).reshape(rows, units)
-    middle_sum = Halves(ring, dot_nt(mixed_low, out_all), "fsdp")
-    middle_sum.step()
-    ring.first(middle_sum.step())
-    in_turn(mlp_weights, down_weights)
-    own_middle = own_rows(tokens_low).astype(f32) + middle_sum.run(2)
     scale_two = inverse_rms(own_middle)
     unit_two = own_middle * scale_two
-    normed_join = Joined(ring, (unit_two * gain_two).astype(bf16), "fsdp")
-    ring.first(normed_join.step())
-    in_turn(mlp_weights)
-    normed_join.step(1)
-    normed_two = normed_join.run()
-    ring.first(normed_two)
-    in_turn(down_weights, mlp_weights)
-    in_turn(*[mlp_weights] * (steps - 6), *[down_weights] * (steps - 5))
-    gate_all, up_all = (jnp.concatenate(slabs, 0) for slabs in mlp_weights.slabs())
-    down_all = rows_joined(down_weights.slabs())
 
     gate_mlp = dot_nn(normed_two, gate_all)
     up_mlp = dot_nn(normed_two, up_all)
@@ -931,7 +1885,7 @@
     branch_low = grad_branch_pre.astype(bf16).reshape(rows, units)
     following = jnp.concatenate([carries[:, 1:], jnp.ones_like(carries[:, :1])], 1)
     tail_prods, local_adjoint = local_scan(following, grad_mixed * branch, True)
-    entry = Entry(prods[:, -1:], carries[:, :1] * local_adjoint[:, :1], -1)
+    entry = Entry(prods_end, carries[:, :1] * local_adjoint[:, :1], -1)
     ring.first(local_adjoint, branch_low)
     in_turn(mlp_grads)
     entry.between(ring.then)
@@ -990,7 +1944,6 @@
     mixed_join.step()
     mixed = mixed_join.run().astype(f32).reshape(tokens.shape)
     gate_grad, up_grad = mlp_grads.sums()
-    own_values = own_rows(tokens_low).astype(f32)
     if ringed:
         branch_grad, inner_grad, out_grad, tokens_grad, gains, small, block_grads = tail(
             count,
@@ -1007,7 +1960,6 @@
             gain_two_grad[None],
             small,
             block_grads.reshape(-1, block_width).astype(bf16),
-            earlier=(gate_grad, up_grad, mixed),
         )
         block_grads = block_grads.astype(f32)
     else:

time: 764 us -> 688 us (0.901)
  Pallas kernels: 140 us -> 609 us
  waiting for transfers between devices: 273 us -> 0 us
  starting transfers between devices: 114 us -> 0 us
  matrix products: 81 us -> 19.7 us
  local copies, waits for them, and re-layouts: 88.9 us -> 36.2 us
  other arithmetic: 54.6 us -> 11.6 us
    pallas_call x5 -> x2, Pallas kernels: 21.8 us -> 491 us  [the longest x1 292 us: head(): pl.pallas_call(functools.partial(head_body, count, fsdp, batches), out_sh...]
    ppermute x106 -> x0, waiting for transfers between devices: 273 us -> none  [the longest x42 208 us: send(): lax.ppermute(forth, 'seq', self.forth)]
    ppermute x106 -> x0, starting transfers between devices: 114 us -> none  [the longest x42 59.1 us: send(): lax.ppermute(forth, 'seq', self.forth)]
    unnamed x347 -> x79, local copies, waits for them, and re-layouts: 62.3 us -> 18.6 us
    dot_general x40 -> x3, matrix products: 59.1 us -> 16.9 us  [dot_nn(): return jnp.dot(left, right, preferred_element_type=f32)]
    dot_general x6 -> x0, matrix products: 19.3 us -> none  [dot_nt(): lax.dot_general(left, right, (((1,), (1,)), ((), ())), preferred_element_...]
    reduce_sum x6 -> x0, other arithmetic: 13.6 us -> none  [the longest x1 4.4 us: local(): jnp.sum(grad_conv * padded[:, 3 - k:3 - k + length], (0, 1))]
    convert_element_type x17 -> x2, other arithmetic: 13.3 us -> 1.2 us  [the longest x1 0.6 us: local(): norm_gain.astype(f32)[None]]
  transfers between devices with their start and end apart: 106 -> 0, of which waited for: 54 -> 0; matrix products, arithmetic and copies ran while one was open for 20% -> 0% of each run, Pallas kernels for 2% -> 0%
where the time goes in v4:
time: 688 us; the launch traced here: 678 us
  Pallas kernels  609 us (89%)
  local copies, waits for them, and re-layouts  36.2 us (5%)
  matrix products  19.7 us (3%)
  other arithmetic  11.6 us (2%)
    pallas_call x1, Pallas kernels, head(): pl.pallas_call(functools.partial(head_body, count, fsdp, batches), out_sh...  292 us
    pallas_call x1, Pallas kernels, back(): pl.pallas_call(functools.partial(back_body, count, fsdp, batches), out_sh...  199 us
    pallas_call x1, Pallas kernels, tail(): pl.pallas_call(functools.partial(tail_body, count), out_shape=(grad, grad...  118 us
    unnamed x79, local copies, waits for them, and re-layouts  18.6 us
    dot_general x3, matrix products, dot_nn(): return jnp.dot(left, right, preferred_element_type=f32)  16.9 us

profile of v4, /device:TPU:0, one launch (start us, length us, event | category | flops | bytes accessed | tf_op | source)
XLA Modules:
  0.0 677.9 jit_solution(4332702419240488948)
XLA Ops:
  0.7 1.1 slice_bitcast_fusion.11
  1.8 1.1 slice_bitcast_fusion.15
  3.0 1.7 pad_add_fusion
  6.9 1.2 copy.48
  12.0 292.1 %shard_map.323 = (bf16[2048,704]{1,0:T(8,128)(2,1)}, bf16[2048,704]{1,0:T(8,128)(2,1)}, bf16[2048,704]{1,0:T(8,128)(2,1)}, bf16[2048,1536]{1,0:T(8,128)(2,1)}, b...) custom-call(bf16[512,2048]{1,0:T(8,128)(2,1)} %bitcast.103, ...), custom_call_target="tpu_custom_call" | custom-call | tf_op jit(solution)/shard_map/pallas_call | solution.py:1086
  304.1 6.3 fusion.31
  310.4 3.4 fusion.30
  313.9 7.2 %multiply_convert_fusion = (bf16[512,1536]{1,0:T(8,128)(2,1)}, bf16[512,1536]{1,0:T(8,128)(2,1)}, bf16[512,1536]{1,0:T(8,128)(2,1)}) fusion(f32[512,1536]{1,0:T(8,128)S(1)} %fusion.30, f32[512,1536]{1,0:T(8,128)S(1)} %fusion.31, bf16[512,2048]{1,0:T(8,128)(2,1)S(1)} %copy-done.4, bf16[2048,1536]{1,0:T(8,128)(2,1)S(1)} %bitcast.97), kind=kOutput, calls=%fused_computation.12 | convolution fusion | flops 3241672704 | bytes 19398656 | tf_op jit(solution)/shard_map/dot_general | solution.py:35
  324.9 198.7 %shard_map.324 = (bf16[512,2048]{1,0:T(8,128)(2,1)}, bf16[512,2048]{1,0:T(8,128)(2,1)}, f32[128,2048]{1,0:T(8,128)}, bf16[512,704]{1,0:T(8,128)(2,1)}, bf16[512,...) custom-call(bf16[512,2048]{1,0:T(8,128)(2,1)} %get-tuple-element.56., ...), custom_call_target="tpu_custom_call" | custom-call | tf_op jit(solution)/shard_map/pallas_call | solution.py:1525
  523.7 2.0 convolution_convert_fusion
  527.1 4.3 copy.53
  531.3 1.4 slice.96.gain_two_ref
  532.8 2.7 copy.54
  536.7 118.0 %shard_map.325 = (f32[256,704]{1,0:T(8,128)}, f32[256,704]{1,0:T(8,128)}, f32[256,704]{1,0:T(8,128)}, bf16[512,2048]{1,0:T(8,128)(2,1)}, f32[8,2048]{1,0:T(8,128...) custom-call(bf16[2048,512]{1,0:T(8,128)(2,1)} %bitcast.94, bf16[512,704]{1,0:T(8,128)(2,1)} %get-tuple-element.73.mixed_ref, ...), custom_call_target="tpu_custom_call" | custom-call | tf_op jit(solution)/shard_map/pallas_call | solution.py:685
  654.7 4.2 convert.36
  658.9 1.2 fusion.28
  660.1 2.4 copy.55
  662.5 2.2 copy.56
  664.8 1.1 copy.57
  665.9 1.5 fusion.29
  668.7 2.5 convert.35
  671.2 3.1 copy.58
  674.3 1.1 copy.72
  676.3 1.1 copy.73
  (98 shorter events, 14.5 us)
Async XLA Ops:
  0.7 4.0 copy-start.20
  0.7 4.0 copy-start.21
  0.7 4.0 copy-start.22
  0.7 4.1 copy-start.23
  0.7 4.7 copy-start.24
  0.7 5.5 copy-start.19
  1.8 5.1 copy-start.10
  2.9 5.1 copy-start.13
  2.9 6.0 copy-start.14
  4.6 5.2 copy-start.15
  4.7 6.1 copy-start.18
  4.7 6.7 copy-start.17
  304.0 6.4 copy-start.1
  304.1 6.4 copy-start.5
  304.1 9.8 %slice-start = ((s8[6291456]{0:T(1024)(128)(4,1)}), s8[4194304]{0:T(1024)(128)(4,1)S(1)}, s32[]{:S(2)}) async-start(s8[6291456]{0:T(1024)(128)(4,1)} %bitcast.96), calls=%async_computation | async-start | bytes 8388608
  313.9 7.2 %copy-start.26 = (s32[8]{0:T(128)S(1)}, s32[8]{0:T(128)}, u32[]{:S(2)}) copy-start(s32[8]{0:T(128)} %constant.50.clone) | copy-start | bytes 100
  313.9 8.5 %copy-start = (s32[8]{0:T(128)S(1)}, s32[8]{0:T(128)}, u32[]{:S(2)}) copy-start(s32[8]{0:T(128)} %constant.51.clone) | copy-start | bytes 100
  324.9 198.8 %copy-start.12 = (bf16[512,704]{1,0:T(8,128)(2,1)S(1)}, bf16[512,704]{1,0:T(8,128)(2,1)}, u32[]{:S(2)}) copy-start(bf16[512,704]{1,0:T(8,128)(2,1)} %get-tuple-element.63.conv_low) | copy-start | bytes 2162692
  527.0 5.8 copy-start.6
  527.1 8.4 %copy-start.9 = (bf16[8,176,176]{2,1,0:T(8,128)(2,1)}, bf16[8,176,176]{2,1,0:T(8,128)(2,1)S(1)}, u32[]{:S(2)}) copy-start(bf16[8,176,176]{2,1,0:T(8,128)(2,1)S(1)} %fusion.7) | copy-start | bytes 1486852
  654.7 4.2 copy-start.2
  660.1 4.6 copy-start.11
  660.1 7.3 %copy-start.16 = (f32[8,704]{1,0:T(8,128)S(1)}, f32[8,704]{1,0:T(8,128)}, u32[]{:S(2)}) copy-start(f32[8,704]{1,0:T(8,128)} %get-tuple-element.89) | copy-start | bytes 67588
  660.1 8.5 %copy-start.3 = (bf16[512,2048]{1,0:T(8,128)(2,1)S(1)}, bf16[512,2048]{1,0:T(8,128)(2,1)}, u32[]{:S(2)}) copy-start(bf16[512,2048]{1,0:T(8,128)(2,1)} %get-tuple-element.71) | copy-start | bytes 6291460
  (5 other events, 14.0 us)

commit v5 on v4

--- a/solution.py
+++ b/solution.py
@@ -421,6 +421,23 @@
             copy.wait_send()
 
 
+class Moves:
+    def __init__(self, sems):
+        self.sems, self.started, self.waiting = sems, 0, []
+
+    def start(self, source, target):
+        copy = pltpu.make_async_copy(source, target, self.sems.at[self.started])
+        copy.start()
+        self.started += 1
+        self.waiting.append(copy)
+        return copy
+
+    def wait(self, number):
+        for copy in self.waiting[:number]:
+            copy.wait()
+        self.waiting = self.waiting[number:]
+
+
 def greet(devices):
     barrier = pltpu.get_barrier_semaphore()
     for device in devices:
@@ -440,8 +457,8 @@
     normed_ref,
     branch_ref,
     inner_ref,
-    branch_all_ref,
-    inner_all_ref,
+    branch_all_in,
+    inner_all_in,
     values_ref,
     grad_ref,
     gain_ref,
@@ -473,6 +490,9 @@
     blocks_got_one,
     blocks_got_two,
     blocks_got_three,
+    branch_all_ref,
+    inner_all_ref,
+    move_sems,
     send_sems,
     recv_sems,
 ):
@@ -482,9 +502,12 @@
     across = [{"seq": partner(index, bit)} for bit in (1, 2, 4)]
     beside = [{"fsdp": partner(unit, bit)} for bit in (1, 2)]
     copies = Copies(send_sems, recv_sems)
-    slab = normed_ref.shape[0] // count
-    half = slab // 2
-    last = count - 1
+    rows, units = branch_ref.shape
+    slab = normed_ref.shape[1] // count
+    tn = (((0,), (0,)), ((), ()))
+    moves = Moves(move_sems)
+    moves.start(branch_all_in, branch_all_ref)
+    moves.start(inner_all_in, inner_all_ref)
 
     greet([forth, back] + across + beside)
 
@@ -492,34 +515,39 @@
     high = blocks_ref.shape[0]
     firsts = [high // 2, high // 4, high // 8]
 
-    def rows_at(start, size):
-        return pl.ds(pl.multiple_of(start, 16), size)
-
     blocks_copy = copies.start(
         blocks_ref.at[rows_at((1 - bits[0]) * firsts[0], firsts[0])], blocks_got_one, across[0]
     )
     small_sums[0] = small_ref[...]
     small_copy = copies.start(small_sums.at[0], small_got.at[0], across[0])
 
+    cut = slim_got.shape[2]
+    parts = (slice(0, cut), slice(cut, units))
+
     def out_term(k, way):
-        start = k * slab + way * half
-        return jnp.dot(
-            emb_ref[start : start + half, :], mixed_ref[...], preferred_element_type=f32
+        return lax.dot_general(
+            mixed_ref[:, parts[way]],
+            emb_ref[:, k * slab : (k + 1) * slab],
+            tn,
+            preferred_element_type=f32,
         )
 
     def front_term(k, way):
-        right = inner_ref if way else branch_ref
-        return jnp.dot(
-            normed_ref[k * slab : (k + 1) * slab, :], right[...], preferred_element_type=f32
+        return lax.dot_general(
+            (inner_ref if way else branch_ref)[...],
+            normed_ref[:, k * slab : (k + 1) * slab],
+            tn,
+            preferred_element_type=f32,
         )
 
     rings = {}
 
     def send(name, way, step, total):
         sent, got = (slim_sent, slim_got) if name == "out" else (wide_sent, wide_got)
-        sent[way, step] = total.astype(bf16)
+        there = pl.ds(0, total.shape[0])
+        sent[way, step, there, :] = total.astype(bf16)
         rings[name, way] = copies.start(
-            sent.at[way, step], got.at[way, step], back if way else forth
+            sent.at[way, step, there], got.at[way, step, there], back if way else forth
         )
 
     def term(name, way, step):
@@ -528,37 +556,34 @@
 
     def serve(name, step):
         got = slim_got if name == "out" else wide_got
-        for way in (0, 1):
-            own = term(name, way, step)
+        terms = [term(name, way, step) for way in (0, 1)]
+        for way, own in enumerate(terms):
             rings[name, way].wait_recv()
-            total = got[way, step - 2].astype(f32) + own
+            total = got[way, step - 2, pl.ds(0, own.shape[0]), :].astype(f32) + own
             if step < count:
                 send(name, way, step - 1, total)
             elif name == "out":
-                out_out[way * half : (way + 1) * half, :] = total
+                out_out[parts[way], :] = total
             else:
                 (inner_out if way else branch_out)[...] = total
 
     for name in ("out", "front"):
         for way in (0, 1):
             send(name, way, 0, term(name, way, 1))
+    moves.wait(2)
 
     core, side = lax.rem(unit, 2), lax.rem(unit // 2, 2)
-    rows = branch_ref.shape[0]
     mid, own = rows // 2, rows // 4
 
     def front_back(start, k):
-        nt = (((1,), (1,)), ((), ()))
         columns = slice(k * slab, (k + 1) * slab)
-        return lax.dot_general(
+        return jnp.dot(
             branch_ref[rows_at(start, mid), :],
-            branch_all_ref[columns, :],
-            nt,
+            branch_all_ref[:, columns],
             preferred_element_type=f32,
-        ) + lax.dot_general(
+        ) + jnp.dot(
             inner_ref[rows_at(start, mid), :],
-            inner_all_ref[columns, :],
-            nt,
+            inner_all_ref[:, columns],
             preferred_element_type=f32,
         )
 
@@ -675,12 +700,12 @@
 def tail(count, *operands):
     emb, mixed, normed, *_ = operands
     small, blocks = operands[-2:]
-    width, rows = emb.shape
+    rows, width = emb.shape
     units = mixed.shape[1]
-    slab = width // count
+    slab, cut = width // count, -(-units // 256) * 128
     high, block_width = blocks.shape
     whole = pl.BlockSpec(memory_space=pltpu.VMEM)
-    grad = jax.ShapeDtypeStruct((slab, units), f32)
+    grad = jax.ShapeDtypeStruct((units, slab), f32)
     steps = count - 1
     return pl.pallas_call(
         functools.partial(tail_body, count),
@@ -693,13 +718,15 @@
             jax.ShapeDtypeStruct(small.shape, f32),
             jax.ShapeDtypeStruct(blocks.shape, bf16),
         ),
-        in_specs=[whole] * len(operands),
+        in_specs=[whole] * 5
+        + [pl.BlockSpec(memory_space=pl.ANY)] * 2
+        + [whole] * (len(operands) - 7),
         out_specs=(whole,) * 7,
         scratch_shapes=[
-            pltpu.VMEM((2, steps, slab, units), bf16),
-            pltpu.VMEM((2, steps, slab, units), bf16),
-            pltpu.VMEM((2, steps, slab // 2, units), bf16),
-            pltpu.VMEM((2, steps, slab // 2, units), bf16),
+            pltpu.VMEM((2, steps, units, slab), bf16),
+            pltpu.VMEM((2, steps, units, slab), bf16),
+            pltpu.VMEM((2, steps, cut, slab), bf16),
+            pltpu.VMEM((2, steps, cut, slab), bf16),
             pltpu.VMEM((rows // 2, width), bf16),
             pltpu.VMEM((rows // 2, width), f32),
             pltpu.VMEM((rows // 2, width), bf16),
@@ -714,6 +741,9 @@
             pltpu.VMEM((high // 2, block_width), bf16),
             pltpu.VMEM((high // 4, block_width), bf16),
             pltpu.VMEM((high // 8, block_width), bf16),
+            pltpu.VMEM((units, width), bf16),
+            pltpu.VMEM((units, width), bf16),
+            pltpu.SemaphoreType.DMA((2,)),
             pltpu.SemaphoreType.DMA((tail_copies,)),
             pltpu.SemaphoreType.DMA((tail_copies,)),
         ],
@@ -734,15 +764,14 @@
     return pl.ds(pl.multiple_of(start, multiple), size)
 
 
+def dot_nt_here(left, right):
+    return lax.dot_general(left, right, (((1,), (1,)), ((), ())), preferred_element_type=f32)
+
+
 def dot_slabs(left, right_ref, slab, count):
     for k in range(count):
         columns = slice(k * slab, (k + 1) * slab)
-        yield columns, lax.dot_general(
-            left,
-            right_ref[columns, :],
-            (((1,), (1,)), ((), ())),
-            preferred_element_type=f32,
-        )
+        yield columns, jnp.dot(left, right_ref[:, columns], preferred_element_type=f32)
 
 
 def scan_rows(a_ref, b_ref, prod_ref, state_ref, batches, backward):
@@ -813,15 +842,34 @@
     down_ref,
     taps_ref,
     vectors_ref,
-    gate_square_ref,
-    input_square_ref,
+    gate_blocks_ref,
+    input_blocks_ref,
     fresh_ref,
+    gate_all,
+    up_all,
+    down_all,
+    branch_all_far,
+    inner_all_far,
+    out_all_far,
+    cot_out_far,
+    normed_out_far,
+    branch_pre_far,
+    padded_far,
+    conv_low_far,
+    gate_pre_far,
+    input_pre_far,
+    carries_far,
+    states_far,
+    mixed_low_far,
+    gate_square_far,
+    input_square_far,
+    ends,
+    own_values,
+    own_middle,
+    normed_two,
     branch_all,
     inner_all,
     out_all,
-    gate_all,
-    up_all,
-    down_all,
     cot_out,
     normed_out,
     branch_pre,
@@ -831,11 +879,9 @@
     input_pre,
     carries,
     states,
-    ends,
     mixed_low,
-    own_values,
-    own_middle,
-    normed_two,
+    gate_square_ref,
+    input_square_ref,
     tokens_low,
     gains,
     prods,
@@ -850,6 +896,7 @@
     own_sent,
     own_got,
     local_sems,
+    far_sems,
     send_sems,
     recv_sems,
 ):
@@ -859,9 +906,8 @@
     along, beside = peers(count, fsdp)
     copies = Copies(send_sems, recv_sems)
     rows, width = tokens_ref.shape
-    units = branch_ref.shape[1]
+    units, hidden = branch_ref.shape[0], down_ref.shape[0]
     length, slab = rows // batches, width // count
-    half = slab // 2
     core, side = lax.rem(unit, 2), lax.rem(unit // 2, 2)
     mid, own = rows // 2, rows // 4
 
@@ -870,37 +916,47 @@
         (branch_ref, inner_ref, out_ref, gate_ref, up_ref, down_ref),
         (branch_all, inner_all, out_all, gate_all, up_all, down_all),
     ):
-        copy = pltpu.make_async_copy(
-            source, target.at[pl.ds(0, slab)], local_sems.at[len(locals_of)]
-        )
+        first = target.at[pl.ds(0, slab)]
+        if source.shape[1] == slab:
+            first = target.at[:, pl.ds(0, slab)]
+        copy = pltpu.make_async_copy(source, first, local_sems.at[len(locals_of)])
         copy.start()
         locals_of.append(copy)
 
     greet(along + beside)
 
     pairs = {
-        "front": ((branch_ref, branch_all, 0, slab), (inner_ref, inner_all, 0, slab)),
-        "out": ((out_ref, out_all, 0, half), (out_ref, out_all, half, half)),
-        "mlp": ((gate_ref, gate_all, 0, slab), (up_ref, up_all, 0, slab)),
-        "down": ((down_ref, down_all, 0, half), (down_ref, down_all, half, half)),
+        "front": ((branch_ref, branch_all, 0, units), (inner_ref, inner_all, 0, units)),
+        "out": (
+            (out_ref, out_all, 0, units // 2),
+            (out_ref, out_all, units // 2, units // 2),
+        ),
+        "mlp": ((gate_ref, gate_all, None, None), (up_ref, up_all, None, None)),
+        "down": (
+            (down_ref, down_all, 0, hidden // 2),
+            (down_ref, down_all, hidden // 2, hidden // 2),
+        ),
     }
     under_way = {}
 
     def start(name, step):
         for way in (0, 1):
             shard, whole, first, size = pairs[name][way]
+
+            def slab_at(k):
+                if first is None:
+                    return whole.at[pl.ds(k * slab, slab)]
+                return whole.at[pl.ds(first, size), pl.ds(k * slab, slab)]
+
             if step > 1:
                 under_way[name, way].wait_recv()
             there = (count - step) % count if way else step
             here = (there + 1) % count if way else step - 1
-            source = (
-                shard.at[pl.ds(first, size)]
-                if step == 1
-                else whole.at[pl.ds(here * slab + first, size)]
-            )
-            under_way[name, way] = copies.start(
-                source, whole.at[pl.ds(there * slab + first, size)], back if way else forth
-            )
+            if step > 1:
+                source = slab_at(here)
+            else:
+                source = shard if first is None else shard.at[pl.ds(first, size)]
+            under_way[name, way] = copies.start(source, slab_at(there), back if way else forth)
 
     def finish(name):
         for way in (0, 1):
@@ -929,6 +985,14 @@
     own_values[...] = tokens_low[rows_at(core * mid + side * own, own), :].astype(f32)
     start("front", 3)
     start("out", 3)
+    for blocks, square in (
+        (gate_blocks_ref, gate_square_ref),
+        (input_blocks_ref, input_square_ref),
+    ):
+        square[...] = jnp.zeros_like(square)
+        size = blocks.shape[1]
+        for j in range(blocks.shape[0]):
+            square[j * size : (j + 1) * size, j * size : (j + 1) * size] = blocks[j]
     for k in range(count):
         plain = pl.ds(pl.multiple_of(ring_index(place - k, count) * slab, slab), slab)
         cot_out[:, k * slab : (k + 1) * slab] = cot_ref[:, plain]
@@ -944,15 +1008,13 @@
     for batch in range(batches):
         at = slice(batch * length, (batch + 1) * length)
         top = batch * (length + 8)
-        inner = jnp.dot(normed_out[at, :], inner_all[...], preferred_element_type=f32)
+        inner = dot_nt_here(normed_out[at, :], inner_all[...])
         padded[top + 8 : top + 8 + length, :] = inner.astype(bf16).astype(f32)
         edges_sent[batch] = padded[top + length : top + length + 8, :]
     edge_copy = copies.start(edges_sent, edges_got, along[0])
     for batch in range(batches):
         at = slice(batch * length, (batch + 1) * length)
-        branch_pre[at, :] = jnp.dot(
-            normed_out[at, :], branch_all[...], preferred_element_type=f32
-        )
+        branch_pre[at, :] = dot_nt_here(normed_out[at, :], branch_all[...])
     edge_copy.wait_recv()
     for batch in range(batches):
         top = batch * (length + 8)
@@ -1055,8 +1117,28 @@
     for step in range(6, count):
         start("mlp", step)
         start("down", step)
+    moves = Moves(far_sems)
+    for source, target in (
+        (branch_all, branch_all_far),
+        (inner_all, inner_all_far),
+        (out_all, out_all_far),
+        (cot_out, cot_out_far),
+        (normed_out, normed_out_far),
+        (branch_pre, branch_pre_far),
+        (padded, padded_far),
+        (conv_low, conv_low_far),
+        (gate_pre, gate_pre_far),
+        (input_pre, input_pre_far),
+        (carries, carries_far),
+        (states, states_far),
+        (mixed_low, mixed_low_far),
+        (gate_square_ref, gate_square_far),
+        (input_square_ref, input_square_far),
+    ):
+        moves.start(source, target)
     finish("mlp")
     finish("down")
+    moves.wait(15)
     copies.end()
 
 
@@ -1064,22 +1146,25 @@
     tokens = operands[0]
     branch, gate = operands[4], operands[7]
     rows, width = tokens.shape
-    slab, units = branch.shape
-    hidden = gate.shape[1]
-    length = rows // batches
+    units, hidden = branch.shape[0], gate.shape[1]
     whole, place = pl.BlockSpec(memory_space=pltpu.VMEM), pl.BlockSpec(memory_space=pl.ANY)
 
     def array(dtype, *shape):
         return jax.ShapeDtypeStruct(shape, dtype)
 
-    outs = (
-        [array(bf16, width, units)] * 3
-        + [array(bf16, width, hidden)] * 3
+    kept = (
+        [array(bf16, units, width)] * 3
         + [array(bf16, rows, width)] * 2
         + [array(f32, rows, units), array(f32, rows + 8 * batches, units), array(bf16, rows, units)]
         + [array(f32, rows, units)] * 3
-        + [array(f32, rows + 8 * batches, units)]
-        + [array(f32, 8, units), array(bf16, rows, units)]
+        + [array(f32, rows + 8 * batches, units), array(bf16, rows, units)]
+        + [array(bf16, units, units)] * 2
+    )
+    outs = (
+        [array(bf16, width, hidden)] * 2
+        + [array(bf16, hidden, width)]
+        + kept
+        + [array(f32, 8, units)]
         + [array(f32, rows // 4, width)] * 2
         + [array(bf16, rows, width)]
     )
@@ -1087,8 +1172,9 @@
         functools.partial(head_body, count, fsdp, batches),
         out_shape=tuple(outs),
         in_specs=[whole] * 4 + [place] * 6 + [whole] * 5,
-        out_specs=tuple([whole] * 3 + [place] * 3 + [whole] * (len(outs) - 6)),
+        out_specs=tuple([place] * (len(outs) - 4) + [whole] * 4),
         scratch_shapes=[
+            *[pltpu.VMEM(part.shape, part.dtype) for part in kept],
             pltpu.VMEM((rows, width), bf16),
             pltpu.VMEM((8, width), f32),
             pltpu.VMEM((rows, units), f32),
@@ -1103,6 +1189,7 @@
             pltpu.VMEM((rows // 4, width), bf16),
             pltpu.VMEM((rows // 4, width), bf16),
             pltpu.SemaphoreType.DMA((6,)),
+            pltpu.SemaphoreType.DMA((15,)),
             pltpu.SemaphoreType.DMA((head_copies,)),
             pltpu.SemaphoreType.DMA((head_copies,)),
         ],
@@ -1157,9 +1244,9 @@
                 )
 
     def serve(self, step, end=None):
-        for way in (0, 1):
-            k = (self.count - step) % self.count if way else step % self.count
-            own = self.terms[way](k)
+        slabs = (step % self.count, (self.count - step) % self.count)
+        terms = [term(k) for term, k in zip(self.terms, slabs)]
+        for way, own in enumerate(terms):
             if step == 1:
                 self.send(way, 1, own)
                 continue
@@ -1181,16 +1268,7 @@
     normed_ref,
     gate_low_ref,
     up_low_ref,
-    branch_pre,
-    padded,
-    conv_low,
-    gate_pre,
-    input_pre,
-    carries,
-    states,
     ends_ref,
-    gate_square_ref,
-    input_square_ref,
     own_middle,
     fresh_ref,
     taps_ref,
@@ -1200,18 +1278,28 @@
     up_all,
     down_all,
     out_all,
+    branch_pre_in,
+    padded_in,
+    conv_low_in,
+    gate_pre_in,
+    input_pre_in,
+    carries_in,
+    states_in,
+    gate_square_in,
+    input_square_in,
     mixed_out,
     middle_low,
     own_grad,
-    branch_low,
-    inner_low,
-    gate_low,
-    input_low,
     small_out,
+    blocks_out,
     gain_grad_out,
+    down_grad,
+    branch_low_out,
+    inner_low_out,
+    gate_low_out,
+    input_low_out,
     gate_grad,
     up_grad,
-    down_grad,
     half_sent,
     half_kept,
     half_got,
@@ -1229,7 +1317,22 @@
     stream_one,
     stream_two,
     stream_out,
+    stream_down,
     stage,
+    branch_pre,
+    padded,
+    conv_low,
+    gate_pre,
+    input_pre,
+    carries,
+    states,
+    gate_square_ref,
+    input_square_ref,
+    branch_low,
+    inner_low,
+    gate_low,
+    input_low,
+    move_sems,
     stream_sems,
     stage_sems,
     ring_sends,
@@ -1248,8 +1351,21 @@
     copies = Copies(send_sems, recv_sems)
     rows, width = cot_ref.shape
     units = branch_pre.shape[1]
+    moves = Moves(move_sems)
+    for source, target in (
+        (branch_pre_in, branch_pre),
+        (states_in, states),
+        (carries_in, carries),
+        (gate_pre_in, gate_pre),
+        (input_pre_in, input_pre),
+        (conv_low_in, conv_low),
+        (gate_square_in, gate_square_ref),
+        (input_square_in, input_square_ref),
+        (padded_in, padded),
+    ):
+        moves.start(source, target)
     length, slab = rows // batches, width // count
-    half = slab // 2
+    inner_half = hidden_ref.shape[1] // 2
     core, side = lax.rem(unit, 2), lax.rem(unit // 2, 2)
     mid, own = rows // 2, rows // 4
     kept_at, sent_at = rows_at(core * mid, mid), rows_at((1 - core) * mid, mid)
@@ -1266,8 +1382,8 @@
 
     def down_term(first):
         return lambda k: lax.dot_general(
-            cot_ref[:, k * slab + first : k * slab + first + half],
-            hidden_ref[...],
+            hidden_ref[:, first : first + inner_half],
+            cot_ref[:, k * slab : (k + 1) * slab],
             tn,
             preferred_element_type=f32,
         )
@@ -1282,7 +1398,7 @@
         neighbours,
     )
     down = RingSum(
-        [down_term(0), down_term(half)],
+        [down_term(0), down_term(inner_half)],
         down_slots,
         ring_sends.at[1],
         ring_arrivals.at[1],
@@ -1293,12 +1409,13 @@
     mlp.serve(1)
     down.serve(1)
 
-    def streamed(sources, buffers, first_sem):
+    def streamed(sources, buffers, first_sem, columns=False):
         def fetch(k):
             fetched = []
             for number, (source, buffer) in enumerate(zip(sources, buffers)):
+                here = pl.ds(k * slab, slab)
                 copy = pltpu.make_async_copy(
-                    source.at[pl.ds(k * slab, slab)],
+                    source.at[:, here] if columns else source.at[here],
                     buffer.at[k % 2],
                     stream_sems.at[first_sem + number * count + k],
                 )
@@ -1314,10 +1431,7 @@
                 fetched = fetch(k + 1)
             yield k, [buffer[k % 2] for buffer in buffers]
 
-    def nt(left, right):
-        return lax.dot_general(
-            left, right, (((1,), (1,)), ((), ())), preferred_element_type=f32
-        )
+    nt = dot_nt_here
 
     for k, (gate, up) in streamed((gate_all, up_all), (stream_one, stream_two), 0):
         part = slice(k * slab, (k + 1) * slab)
@@ -1351,13 +1465,13 @@
     down.serve(3)
     join_copy.wait_recv()
 
-    for k, (out,) in streamed((out_all,), (stream_out,), 2 * count):
+    for k, (out,) in streamed((out_all,), (stream_out,), 2 * count, True):
         for batch in range(batches):
             at = slice(batch * length, (batch + 1) * length)
-            more = jnp.dot(
-                middle_low[at, k * slab : (k + 1) * slab], out, preferred_element_type=f32
-            )
+            more = nt(middle_low[at, k * slab : (k + 1) * slab], out)
             adjoints[at, :] = more if k == 0 else adjoints[at, :] + more
+
+    moves.wait(9)
 
     def mixed_block(block, carry):
         batch = block // (length // row_block)
@@ -1369,6 +1483,7 @@
         return carry
 
     lax.fori_loop(0, rows // row_block, mixed_block, 0)
+    moves.start(branch_low, branch_low_out)
     scanned = scan_rows(carries, adjoints, prods, adjoints, batches, True)
     ends_sent[...] = ends_ref[...]
     for batch, (_, state) in enumerate(scanned):
@@ -1423,6 +1538,8 @@
         sums = lax.fori_loop(0, length // row_block, gate_block, sums)
         if batch == 0:
             down.serve(4)
+    moves.start(gate_low, gate_low_out)
+    moves.start(input_low, input_low_out)
     for batch in range(batches):
         at, top = slice(batch * length, (batch + 1) * length), batch * (length + 8)
         conv_grad[top : top + length, :] = (
@@ -1433,13 +1550,24 @@
         edges_sent[batch] = conv_grad[top : top + 8, :]
     edge_copy = copies.start(edges_sent, edges_got, along[count - 2])
     mlp.serve(5)
+    size = blocks_out.shape[1]
+    for number, right in enumerate((gate_low, input_low)):
+        square = lax.dot_general(conv_low[...], right[...], tn, preferred_element_type=f32)
+        for j in range(units // size):
+            at = slice(j * size, (j + 1) * size)
+            first = number * units + j * size
+            blocks_out[first : first + size, :] = square[at, at].astype(bf16)
 
     copies.sent(half_copy)
     copies.sent(own_copy)
-    for k, (turned,) in streamed((down_all,), (stream_one,), 3 * count):
+    for k, (right,) in streamed((down_all,), (stream_down,), 3 * count, True):
         part = slice(k * slab, (k + 1) * slab)
-        half_sent[:, part] = nt(hidden_ref[sent_at, :], turned).astype(bf16)
-        half_kept[:, part] = nt(hidden_ref[kept_at, :], turned)
+        half_sent[:, part] = jnp.dot(
+            hidden_ref[sent_at, :], right, preferred_element_type=f32
+        ).astype(bf16)
+        half_kept[:, part] = jnp.dot(
+            hidden_ref[kept_at, :], right, preferred_element_type=f32
+        )
     mixed_copy = copies.start(half_sent, half_got, beside[0])
     down.serve(5)
 
@@ -1462,6 +1590,7 @@
         )
 
     conv_sums = lax.fori_loop(0, rows // row_block, conv_block, (zero,) * 5)
+    moves.start(inner_low, inner_low_out)
     for number, total in enumerate((*conv_sums, sums[0], sums[1], sums[2] * slope)):
         small_out[number : number + 1, :] = total
 
@@ -1492,22 +1621,20 @@
         copy.wait()
 
     def down_end(way, total):
-        stage[way * half : (way + 1) * half, :] = total
+        down_grad[way * inner_half : (way + 1) * inner_half, :] = total
 
     mlp.serve(8, mlp_end)
     down.serve(8, down_end)
-    copy = pltpu.make_async_copy(stage, down_grad, stage_sems.at[2])
-    copy.start()
-    copy.wait()
+    moves.wait(4)
     copies.end()
 
 
-def back(count, fsdp, batches, *operands):
+def back(count, fsdp, batches, block_width, *operands):
     cot, hidden = operands[0], operands[1]
-    branch_pre = operands[5]
+    late = operands[-9:]
     rows, width = cot.shape
-    units, inner = branch_pre.shape[1], hidden.shape[1]
-    slab, length = width // count, rows // batches
+    units, inner = late[0].shape[1], hidden.shape[1]
+    slab = width // count
     whole, place = pl.BlockSpec(memory_space=pltpu.VMEM), pl.BlockSpec(memory_space=pl.ANY)
 
     def array(dtype, *shape):
@@ -1517,16 +1644,18 @@
         array(bf16, rows, width),
         array(bf16, rows, width),
         array(f32, rows // 4, width),
+        array(f32, 8, units),
+        array(bf16, 2 * units, block_width),
+        array(f32, 8, width),
+        array(f32, inner, slab),
         *[array(bf16, rows, units)] * 4,
-        array(f32, 8, units),
-        array(f32, 8, width),
-        *[array(f32, slab, inner)] * 3,
+        *[array(f32, slab, inner)] * 2,
     ]
     return pl.pallas_call(
         functools.partial(back_body, count, fsdp, batches),
         out_shape=tuple(outs),
-        in_specs=[whole] * (len(operands) - 4) + [place] * 4,
-        out_specs=tuple([whole] * 9 + [place] * 3),
+        in_specs=[whole] * (len(operands) - 13) + [place] * 13,
+        out_specs=tuple([whole] * 7 + [place] * 6),
         scratch_shapes=[
             pltpu.VMEM((rows // 2, width), bf16),
             pltpu.VMEM((rows // 2, width), f32),
@@ -1541,13 +1670,17 @@
             pltpu.VMEM((8, units), f32),
             pltpu.VMEM((count - 1, 8, units), f32),
             pltpu.VMEM((2, ring_slots, slab, inner), bf16),
-            pltpu.VMEM((2, ring_slots, slab // 2, inner), bf16),
+            pltpu.VMEM((2, ring_slots, inner // 2, slab), bf16),
             pltpu.VMEM((2, slab, inner), bf16),
             pltpu.VMEM((2, slab, inner), bf16),
-            pltpu.VMEM((2, slab, units), bf16),
+            pltpu.VMEM((2, units, slab), bf16),
+            pltpu.VMEM((2, inner, slab), bf16),
             pltpu.VMEM((slab, inner), f32),
+            *[pltpu.VMEM(part.shape, part.dtype) for part in late],
+            *[pltpu.VMEM((rows, units), bf16)] * 4,
+            pltpu.SemaphoreType.DMA((13,)),
             pltpu.SemaphoreType.DMA((4 * count,)),
-            pltpu.SemaphoreType.DMA((3,)),
+            pltpu.SemaphoreType.DMA((2,)),
             pltpu.SemaphoreType.DMA((2, 2, count - 1)),
             pltpu.SemaphoreType.DMA((2, 2, count - 1)),
             pltpu.SemaphoreType.REGULAR((2, 2)),
@@ -1558,6 +1691,46 @@
             collective_id=2, has_side_effects=True, vmem_limit_bytes=63 * 1024 * 1024
         ),
     )(*operands)
+
+
+def mlp_body(normed_ref, cot_ref, gate_ref, up_ref, down_ref, hidden_out, gate_out, up_out):
+    gate = jnp.dot(normed_ref[...], gate_ref[...], preferred_element_type=f32)
+    up = jnp.dot(normed_ref[...], up_ref[...], preferred_element_type=f32)
+    back = dot_nt_here(cot_ref[...], down_ref[...])
+    constant = 0.7978845608028654
+    square = gate * gate
+    bent = jnp.tanh(constant * (gate + 0.044715 * square * gate))
+    half = 0.5 * (1.0 + bent)
+    active = half * gate
+    slope = half + 0.5 * gate * (1.0 - bent * bent) * (
+        constant * (1.0 + 3.0 * 0.044715 * square)
+    )
+    hidden_out[...] = (active * up).astype(bf16)
+    gate_out[...] = (back * up * slope).astype(bf16)
+    up_out[...] = (back * active).astype(bf16)
+
+
+def feed_forward(normed, cot, gate_all, up_all, down_all):
+    rows, width = normed.shape
+    hidden = gate_all.shape[1]
+    wide = 256
+    resident = pl.BlockSpec((rows, width), lambda j: (0, 0))
+    columns = pl.BlockSpec((width, wide), lambda j: (0, j))
+    result = pl.BlockSpec((rows, wide), lambda j: (0, j))
+    return pl.pallas_call(
+        mlp_body,
+        grid=(hidden // wide,),
+        out_shape=(jax.ShapeDtypeStruct((rows, hidden), bf16),) * 3,
+        in_specs=[
+            resident,
+            resident,
+            columns,
+            columns,
+            pl.BlockSpec((wide, width), lambda j: (j, 0)),
+        ],
+        out_specs=(result,) * 3,
+        compiler_params=pltpu.CompilerParams(vmem_limit_bytes=62 * 1024 * 1024),
+    )(normed, cot, gate_all, up_all, down_all)
 
 
 def block_diagonal(blocks):
@@ -1646,7 +1819,6 @@
     steps = count - 1
     taps = conv_weight.astype(f32)
     decay = decay_param.astype(f32)
-    gate_square, input_square = block_diagonal(gate_blocks), block_diagonal(input_blocks)
     fresh_start = resets[:, :, None] > 0
     gain_one = gain_moved(norm_gain.astype(f32))
     gain_two = gain_moved(mlp_norm_gain.astype(f32))
@@ -1668,12 +1840,12 @@
             0,
         )
         (
+            gate_all,
+            up_all,
+            down_all,
             branch_all,
             inner_all,
             out_all,
-            gate_all,
-            up_all,
-            down_all,
             cot_low,
             normed,
             branch_pre,
@@ -1683,8 +1855,10 @@
             input_pre,
             carries,
             states,
+            mixed_low,
+            gate_square,
+            input_square,
             ends,
-            mixed_low,
             own_values,
             own_middle,
             normed_two,
@@ -1696,54 +1870,46 @@
             cotangent.reshape(rows, width),
             norm_gain.astype(f32)[None],
             mlp_norm_gain.astype(f32)[None],
-            branch_weight,
-            inner_weight,
-            out_turned,
+            branch_weight.T,
+            inner_weight.T,
+            out_weight,
             gate_weight,
             up_weight,
-            down_turned,
+            down_weight,
             taps,
             vectors,
-            gate_square,
-            input_square,
+            gate_blocks,
+            input_blocks,
             resets.reshape(rows, 1),
         )
-        gate_mlp, up_mlp = dot_nn(normed_two, gate_all), dot_nn(normed_two, up_all)
-        activated, act_pull = jax.vjp(gated_product, gate_mlp, up_mlp)
-        hidden_low = activated.astype(bf16)
-        grad_gate_mlp, grad_up_mlp = act_pull(dot_nn(cot_low, down_all))
+        hidden_low, gate_mlp_low, up_mlp_low = feed_forward(
+            normed_two, cot_low, gate_all, up_all, down_all
+        )
         (
             mixed,
             middle_low,
             own_grad,
+            small,
+            block_grads,
+            gain_two_grad,
+            down_grad,
             branch_low,
             inner_grad_low,
             gate_low,
             input_low,
-            small,
-            gain_two_grad,
             gate_grad,
             up_grad,
-            down_grad,
         ) = back(
             count,
             lax.axis_size("fsdp"),
             batches,
+            gate_blocks.shape[-1],
             cot_low,
             hidden_low,
             normed_two,
-            grad_gate_mlp.astype(bf16),
-            grad_up_mlp.astype(bf16),
-            branch_pre,
-            padded,
-            conv_flat,
-            gate_pre,
-            input_pre,
-            carries,
-            states,
+            gate_mlp_low,
+            up_mlp_low,
             ends,
-            gate_square,
-            input_square,
             own_middle,
             resets.reshape(rows, 1),
             taps,
@@ -1753,21 +1919,22 @@
             up_all,
             down_all,
             out_all,
-        )
-        block_count = gate_blocks.shape[0]
-        block_grads = jnp.concatenate(
-            [
-                diagonal_blocks(dot_tn(conv_flat, gate_low), block_count),
-                diagonal_blocks(dot_tn(conv_flat, input_low), block_count),
-            ],
-            0,
-        )
-        block_width = block_grads.shape[-1]
+            branch_pre,
+            padded,
+            conv_flat,
+            gate_pre,
+            input_pre,
+            carries,
+            states,
+            gate_square,
+            input_square,
+        )
+        block_count, block_width = gate_blocks.shape[:2]
         branch_grad, inner_grad, out_grad, tokens_grad, gains, small, block_grads = tail(
             count,
-            middle_low.T,
+            middle_low,
             mixed_low,
-            normed.T,
+            normed,
             branch_low,
             inner_grad_low,
             branch_all,
@@ -1777,15 +1944,15 @@
             gain_one[None],
             gain_two_grad[:1],
             small,
-            block_grads.reshape(-1, block_width).astype(bf16),
+            block_grads,
         )
         block_grads = block_grads.astype(f32).reshape(2, block_count, block_width, block_width)
         return (
             mixed.astype(f32).reshape(tokens.shape),
             tokens_grad.astype(f32).reshape(tokens.shape),
             gains[0],
-            branch_grad,
-            inner_grad,
+            branch_grad.T,
+            inner_grad.T,
             small[:4],
             small[4],
             block_grads[0],
@@ -1793,11 +1960,11 @@
             small[5],
             small[6],
             small[7],
-            out_grad.T,
+            out_grad,
             gains[1],
             gate_grad,
             up_grad,
-            down_grad.T,
+            down_grad,
         )
     else:
         branch_all, inner_all, out_all, gate_all, up_all, down_all = [
@@ -1811,6 +1978,7 @@
                 down_turned,
             )
         ]
+        gate_square, input_square = block_diagonal(gate_blocks), block_diagonal(input_blocks)
         tokens_low, cot_low = tokens.reshape(rows, width), cotangent.reshape(rows, width)
         values = tokens_low.astype(f32)
         normed = (values * inverse_rms(values) * gain_one).astype(bf16)

time: 688 us -> 643 us (0.935)
  matrix products: 19.7 us -> 0 us
  local copies, waits for them, and re-layouts: 36.2 us -> 21.5 us
  Pallas kernels: 609 us -> 600 us
    dot_general x5 -> x0, matrix products: 19.7 us -> none  [the longest x3 16.9 us: dot_nn(): return jnp.dot(left, right, preferred_element_type=f32)]
    pallas_call x0 -> x1, Pallas kernels: none -> 16.6 us  [feed_forward(): pl.pallas_call(mlp_body, grid=(hidden // wide,), out_shape=(jax.ShapeDtyp...]
    pallas_call x1, Pallas kernels: 292 us -> 277 us  [head(): pl.pallas_call(functools.partial(head_body, count, fsdp, batches), out_sh...]
    unnamed x79 -> x36, local copies, waits for them, and re-layouts: 18.6 us -> 11 us
    pallas_call x2 -> x0, local copies, waits for them, and re-layouts: 6.93 us -> none  [the longest x1 4.25 us: back(): pl.pallas_call(functools.partial(back_body, count, fsdp, batches), out_sh...]
where the time goes in v5:
time: 643 us; the launch traced here: 635 us
  Pallas kernels  600 us (93%)
  local copies, waits for them, and re-layouts  21.5 us (3%)
  other arithmetic  12.6 us (2%)
    pallas_call x1, Pallas kernels, head(): pl.pallas_call(functools.partial(head_body, count, fsdp, batches), out_sh...  277 us
    pallas_call x1, Pallas kernels, back(): pl.pallas_call(functools.partial(back_body, count, fsdp, batches), out_sh...  194 us
    pallas_call x1, Pallas kernels, tail(): pl.pallas_call(functools.partial(tail_body, count), out_shape=(grad, grad...  112 us
    pallas_call x1, Pallas kernels, feed_forward(): pl.pallas_call(mlp_body, grid=(hidden // wide,), out_shape=(jax.ShapeDtyp...  16.6 us

profile of v5, /device:TPU:0, one launch (start us, length us, event | category | flops | bytes accessed | tf_op | source)
XLA Modules:
  0.0 634.9 jit_solution(11316611567152465528)
XLA Ops:
  0.7 0.7 fusion.8
  1.4 0.7 reshape.139
  2.1 0.7 reshape.140
  4.7 0.9 copy.40
  5.6 1.3 convert_element_type.24.taps_ref
  6.9 1.3 convert_element_type.10
  8.2 1.3 convert_element_type.11
  9.5 276.8 %shard_map.323 = (bf16[2048,1536]{1,0:T(8,128)(2,1)}, bf16[2048,1536]{1,0:T(8,128)(2,1)}, bf16[1536,2048]{1,0:T(8,128)(2,1)}, bf16[704,2048]{1,0:T(8,128)(2,1)},...) custom-call(bf16[512,2048]{1,0:T(8,128)(2,1)} %bitcast.35, ...), custom_call_target="tpu_custom_call" | custom-call | tf_op jit(solution)/shard_map/pallas_call | solution.py:1171
  286.3 16.6 %shard_map.324 = (bf16[512,1536]{1,0:T(8,128)(2,1)}, bf16[512,1536]{1,0:T(8,128)(2,1)}, bf16[512,1536]{1,0:T(8,128)(2,1)}) custom-call(bf16[512,2048]{1,0:T(8,128)(2,1)} %get-tuple-element.61.normed_ref, bf16[512,2048]{1,0:T(8,128)(2,1)} %get-tuple-element.60.cot_ref, bf16[2048,1536]{1,0:T(8,128)(2,1)} %get-tuple-element.62.gate_ref.gate_all, ...), custom_call_target="tpu_custom_call" | custom-call | tf_op jit(solution)/shard_map/pallas_call | solution.py:1720
  306.8 193.6 %shard_map.325 = (bf16[512,2048]{1,0:T(8,128)(2,1)}, bf16[512,2048]{1,0:T(8,128)(2,1)}, f32[128,2048]{1,0:T(8,128)}, f32[8,704]{1,0:T(8,128)}, bf16[1408,176]{1,...) custom-call(bf16[512,2048]{1,0:T(8,128)(2,1)} %get-tuple-element.60., ...), custom_call_target="tpu_custom_call" | custom-call | tf_op jit(solution)/shard_map/pallas_call | solution.py:1654
  500.4 1.4 slice.32.gain_two_ref
  503.0 112.5 %shard_map.326 = (f32[704,256]{1,0:T(8,128)}, f32[704,256]{1,0:T(8,128)}, f32[704,256]{1,0:T(8,128)}, bf16[512,2048]{1,0:T(8,128)(2,1)}, f32[8,2048]{1,0:T(8,128...) custom-call(bf16[512,2048]{1,0:T(8,128)(2,1)} %get-tuple-element.81.emb_ref, ...), custom_call_target="tpu_custom_call" | custom-call | tf_op jit(solution)/shard_map/pallas_call | solution.py:710
  615.5 4.2 convert.6
  619.8 1.2 fusion.13
  621.0 1.5 fusion.14
  623.7 2.5 convert.5
  626.3 0.9 copy.49
  627.6 0.9 copy.50
  628.5 0.9 copy.51
  629.4 1.1 copy.52
  630.5 0.8 copy-done.4
  631.3 1.1 copy.53
  632.5 0.8 copy-done.3
  633.3 1.1 copy.54
  (44 shorter events, 8.7 us)
Async XLA Ops:
  286.3 16.7 %copy-start.12 = (s32[8]{0:T(128)S(1)}, s32[8]{0:T(128)}, u32[]{:S(2)}) copy-start(s32[8]{0:T(128)} %constant.37.clone) | copy-start | bytes 100
  286.3 17.9 %copy-start = (s32[8]{0:T(128)S(1)}, s32[8]{0:T(128)}, u32[]{:S(2)}) copy-start(s32[8]{0:T(128)} %constant.38.clone) | copy-start | bytes 100
  286.3 18.6 %copy-start.10 = (bf16[2048]{0:T(1024)(128)(2,1)S(1)}, bf16[2048]{0:T(1024)(128)(2,1)}, u32[]{:S(2)}) copy-start(bf16[2048]{0:T(1024)(128)(2,1)} %param.33) | copy-start | bytes 12292
  306.8 195.1 %copy-start.11 = (bf16[2048]{0:T(1024)(128)(2,1)S(1)}, bf16[2048]{0:T(1024)(128)(2,1)}, u32[]{:S(2)}) copy-start(bf16[2048]{0:T(1024)(128)(2,1)} %param.22) | copy-start | bytes 12292
  615.5 4.2 copy-start.1
  619.7 2.7 copy-start.9
  619.7 4.0 copy-start.2
  623.7 2.5 copy-start.8
  626.3 1.4 copy-start.7
  626.3 2.2 copy-start.6
  627.6 1.7 copy-start.5
  629.4 2.0 copy-start.4
  631.3 2.0 copy-start.3

commit v6 on v5

--- a/solution.py
+++ b/solution.py
@@ -447,7 +447,7 @@
     pl.semaphore_wait(barrier, len(devices))
 
 
-tail_copies = 28 + 4 + 6 + 3 + 5
+tail_copies = 28 + 4 + 3 + 3 + 5
 
 
 def tail_body(
@@ -485,11 +485,6 @@
     small_got,
     gain_sums,
     gain_got,
-    blocks_one,
-    blocks_two,
-    blocks_got_one,
-    blocks_got_two,
-    blocks_got_three,
     branch_all_ref,
     inner_all_ref,
     move_sems,
@@ -511,16 +506,6 @@
 
     greet([forth, back] + across + beside)
 
-    bits = [lax.rem(index // bit, 2) for bit in (1, 2, 4)]
-    high = blocks_ref.shape[0]
-    firsts = [high // 2, high // 4, high // 8]
-
-    blocks_copy = copies.start(
-        blocks_ref.at[rows_at((1 - bits[0]) * firsts[0], firsts[0])], blocks_got_one, across[0]
-    )
-    small_sums[0] = small_ref[...]
-    small_copy = copies.start(small_sums.at[0], small_got.at[0], across[0])
-
     cut = slim_got.shape[2]
     parts = (slice(0, cut), slice(cut, units))
 
@@ -572,6 +557,18 @@
             send(name, way, 0, term(name, way, 1))
     moves.wait(2)
 
+    high = blocks_out.shape[0]
+    bits = [lax.rem(index // bit, 2) for bit in (1, 2, 4)]
+    sizes = [high // 2, high // 4, high // 8]
+    starts = [bits[0] * sizes[0]]
+    for bit, size in zip(bits[1:], sizes[1:]):
+        starts.append(starts[-1] + bit * size)
+    at = [rows_at(start, size) for start, size in zip(starts, sizes)]
+    blocks_out[at[2], :] = blocks_ref[...]
+    blocks_copy = copies.start(blocks_out.at[at[2]], blocks_out.at[at[2]], across[2])
+    small_sums[0] = small_ref[...]
+    small_copy = copies.start(small_sums.at[0], small_got.at[0], across[0])
+
     core, side = lax.rem(unit, 2), lax.rem(unit // 2, 2)
     mid, own = rows // 2, rows // 4
 
@@ -601,13 +598,7 @@
     serve("front", 2)
 
     blocks_copy.wait_recv()
-    blocks_one[...] = (
-        blocks_ref[rows_at(bits[0] * firsts[0], firsts[0]), :].astype(f32)
-        + blocks_got_one[...].astype(f32)
-    ).astype(bf16)
-    blocks_copy = copies.start(
-        blocks_one.at[rows_at((1 - bits[1]) * firsts[1], firsts[1])], blocks_got_two, across[1]
-    )
+    blocks_copy = copies.start(blocks_out.at[at[1]], blocks_out.at[at[1]], across[1])
     small_copy.wait_recv()
     small_sums[1] = small_sums[0] + small_got[0]
     small_copy = copies.start(small_sums.at[1], small_got.at[1], across[1])
@@ -620,7 +611,7 @@
     unit_values = values * scale
     front = half_kept[mine, :] + half_got[mine, :].astype(f32) + own_got[...].astype(f32)
     gain_grad = jnp.sum(front * unit_values, 0, keepdims=True)
-    weighted = front * gain_ref[...]
+    weighted = front * gain_ref[0:1, :]
     result = grad_ref[...] + scale * (
         weighted - unit_values * jnp.mean(weighted * unit_values, axis=-1, keepdims=True)
     )
@@ -632,20 +623,14 @@
         part = slice(k * slab, (k + 1) * slab)
         tokens_out[own_at, to] = low[:, part]
         gain_sums[0, 0:1, to] = gain_grad[:, part]
-        gain_sums[0, 1:2, to] = gain_two_ref[:, part]
+        gain_sums[0, 1:2, to] = gain_two_ref[0:1, part]
     tokens_copy = copies.start(tokens_out.at[own_at], tokens_out.at[own_at], beside[1])
     gain_copy = copies.start(gain_sums.at[0], gain_got.at[0], across[0])
     serve("out", 4)
     serve("front", 4)
 
     blocks_copy.wait_recv()
-    blocks_two[...] = (
-        blocks_one[rows_at(bits[1] * firsts[1], firsts[1]), :].astype(f32)
-        + blocks_got_two[...].astype(f32)
-    ).astype(bf16)
-    blocks_copy = copies.start(
-        blocks_two.at[rows_at((1 - bits[2]) * firsts[2], firsts[2])], blocks_got_three, across[2]
-    )
+    blocks_copy = copies.start(blocks_out.at[at[0]], blocks_out.at[at[0]], across[0])
     small_copy.wait_recv()
     small_sums[2] = small_sums[1] + small_got[1]
     small_copy = copies.start(small_sums.at[2], small_got.at[2], across[2])
@@ -659,15 +644,6 @@
     serve("front", 5)
 
     blocks_copy.wait_recv()
-    starts = [bits[0] * firsts[0]]
-    for bit, first in zip(bits[1:], firsts[1:]):
-        starts.append(starts[-1] + bit * first)
-    at = [rows_at(start, first) for start, first in zip(starts, firsts)]
-    blocks_out[at[2], :] = (
-        blocks_two[rows_at(bits[2] * firsts[2], firsts[2]), :].astype(f32)
-        + blocks_got_three[...].astype(f32)
-    ).astype(bf16)
-    blocks_copy = copies.start(blocks_out.at[at[2]], blocks_out.at[at[2]], across[2])
     gain_copy.wait_recv()
     gain_sums[2] = gain_sums[1] + gain_got[1]
     gain_copy = copies.start(gain_sums.at[2], gain_got.at[2], across[2])
@@ -676,8 +652,6 @@
     serve("out", 6)
     serve("front", 6)
 
-    blocks_copy.wait_recv()
-    blocks_copy = copies.start(blocks_out.at[at[1]], blocks_out.at[at[1]], across[1])
     gain_copy.wait_recv()
     gain_sums[3] = gain_sums[2] + gain_got[2]
     gain_copy = copies.start(gain_sums.at[3], gain_got.at[3], beside[0])
@@ -686,13 +660,10 @@
     gain_sums[4] = gain_sums[3] + gain_got[3]
     gain_copy = copies.start(gain_sums.at[4], gain_got.at[4], beside[1])
     serve("front", 7)
-    blocks_copy.wait_recv()
-    blocks_copy = copies.start(blocks_out.at[at[0]], blocks_out.at[at[0]], across[0])
     serve("out", 8)
     gain_copy.wait_recv()
     gains_out[...] = gain_sums[4] + gain_got[4]
     tokens_copy.wait_recv()
-    blocks_copy.wait_recv()
     serve("front", 8)
     copies.end()
 
@@ -716,7 +687,7 @@
             jax.ShapeDtypeStruct((rows, width), bf16),
             jax.ShapeDtypeStruct((8, width), f32),
             jax.ShapeDtypeStruct(small.shape, f32),
-            jax.ShapeDtypeStruct(blocks.shape, bf16),
+            jax.ShapeDtypeStruct((8 * high, block_width), bf16),
         ),
         in_specs=[whole] * 5
         + [pl.BlockSpec(memory_space=pl.ANY)] * 2
@@ -736,11 +707,6 @@
             pltpu.VMEM((3, *small.shape), f32),
             pltpu.VMEM((5, 8, width), f32),
             pltpu.VMEM((5, 8, width), f32),
-            pltpu.VMEM((high // 2, block_width), bf16),
-            pltpu.VMEM((high // 4, block_width), bf16),
-            pltpu.VMEM((high // 2, block_width), bf16),
-            pltpu.VMEM((high // 4, block_width), bf16),
-            pltpu.VMEM((high // 8, block_width), bf16),
             pltpu.VMEM((units, width), bf16),
             pltpu.VMEM((units, width), bf16),
             pltpu.SemaphoreType.DMA((2,)),
@@ -832,8 +798,6 @@
     batches,
     tokens_ref,
     cot_ref,
-    gain_one_ref,
-    gain_two_ref,
     branch_ref,
     inner_ref,
     out_ref,
@@ -841,10 +805,16 @@
     up_ref,
     down_ref,
     taps_ref,
-    vectors_ref,
+    conv_bias_ref,
+    gate_bias_ref,
+    input_bias_ref,
+    rate_ref,
+    slope_ref,
+    gain_one_ref,
+    gain_two_ref,
+    resets_ref,
     gate_blocks_ref,
     input_blocks_ref,
-    fresh_ref,
     gate_all,
     up_all,
     down_all,
@@ -867,6 +837,9 @@
     own_values,
     own_middle,
     normed_two,
+    gains,
+    packed_ref,
+    fresh_ref,
     branch_all,
     inner_all,
     out_all,
@@ -883,7 +856,6 @@
     gate_square_ref,
     input_square_ref,
     tokens_low,
-    gains,
     prods,
     local_states,
     edges_sent,
@@ -965,12 +937,24 @@
     start("front", 1)
     start("out", 1)
 
+    packed_ref[...] = jnp.zeros_like(packed_ref)
+    packed_ref[0:4, :units] = taps_ref[...].astype(f32)
+    vectors = (conv_bias_ref, gate_bias_ref, input_bias_ref, rate_ref, slope_ref)
+    for row, vector in enumerate((*vectors, gain_one_ref, gain_two_ref)):
+        size = vector.shape[0]
+        packed_ref[row + 4 : row + 5, :size] = vector[...].astype(f32).reshape(1, size)
+    flags = jnp.concatenate(
+        [resets_ref[...].astype(f32), jnp.zeros((8 - batches, length), f32)], 0
+    ).T
+    for batch in range(batches):
+        fresh_ref[batch * length : (batch + 1) * length, :] = flags[:, batch : batch + 1]
+
     for k in range(count):
         plain = pl.ds(pl.multiple_of(ring_index(place - k, count) * slab, slab), slab)
         part = slice(k * slab, (k + 1) * slab)
         tokens_low[:, part] = tokens_ref[:, plain]
-        gains[0:1, part] = gain_one_ref[:, plain]
-        gains[1:2, part] = gain_two_ref[:, plain]
+        gains[0:1, part] = packed_ref[9:10, plain]
+        gains[1:2, part] = packed_ref[10:11, plain]
     start("front", 2)
     start("out", 2)
 
@@ -1020,13 +1004,13 @@
         top = batch * (length + 8)
         padded[top : top + 8, :] = jnp.where(index > 0, edges_got[batch], 0.0)
     start("mlp", 2)
-    bias, gate_bias, input_bias, rate = [vectors_ref[i : i + 1, :] for i in range(4)]
+    bias, gate_bias, input_bias, rate = [packed_ref[i : i + 1, :units] for i in range(4, 8)]
 
     def conv_block(block, carry):
         batch = block // (length // row_block)
         wide = padded[rows_at(block * row_block + batch * 8, row_block + 8, 8), :]
-        total = bias + taps_ref[0:1, :] * wide[8:] + taps_ref[1:2, :] * wide[7:-1]
-        total = total + taps_ref[2:3, :] * wide[6:-2] + taps_ref[3:4, :] * wide[5:-3]
+        total = bias + packed_ref[0:1, :units] * wide[8:] + packed_ref[1:2, :units] * wide[7:-1]
+        total = total + packed_ref[2:3, :units] * wide[6:-2] + packed_ref[3:4, :units] * wide[5:-3]
         conv_low[rows_at(block * row_block, row_block), :] = total.astype(bf16)
         return carry
 
@@ -1144,7 +1128,7 @@
 
 def head(count, fsdp, batches, *operands):
     tokens = operands[0]
-    branch, gate = operands[4], operands[7]
+    branch, gate = operands[2], operands[5]
     rows, width = tokens.shape
     units, hidden = branch.shape[0], gate.shape[1]
     whole, place = pl.BlockSpec(memory_space=pltpu.VMEM), pl.BlockSpec(memory_space=pl.ANY)
@@ -1166,17 +1150,17 @@
         + kept
         + [array(f32, 8, units)]
         + [array(f32, rows // 4, width)] * 2
-        + [array(bf16, rows, width)]
+        + [array(bf16, rows, width), array(f32, 8, width)]
+        + [array(f32, 16, width), array(f32, rows, 1)]
     )
     return pl.pallas_call(
         functools.partial(head_body, count, fsdp, batches),
         out_shape=tuple(outs),
-        in_specs=[whole] * 4 + [place] * 6 + [whole] * 5,
-        out_specs=tuple([place] * (len(outs) - 4) + [whole] * 4),
+        in_specs=[whole] * 2 + [place] * 6 + [whole] * 11,
+        out_specs=tuple([place] * (len(outs) - 7) + [whole] * 7),
         scratch_shapes=[
             *[pltpu.VMEM(part.shape, part.dtype) for part in kept],
             pltpu.VMEM((rows, width), bf16),
-            pltpu.VMEM((8, width), f32),
             pltpu.VMEM((rows, units), f32),
             pltpu.VMEM((rows, units), f32),
             pltpu.VMEM((batches, 8, units), f32),
@@ -1208,7 +1192,7 @@
 
 ring_slots = 3
 back_sends = 2 * 2 * (ring_count - 1)
-back_copies = 4 + 4 + (ring_count - 1) + 1
+back_copies = 4 + 4 + (ring_count - 1) + 1 + 3
 
 
 class RingSum:
@@ -1271,9 +1255,8 @@
     ends_ref,
     own_middle,
     fresh_ref,
-    taps_ref,
-    vectors_ref,
-    gain_two_ref,
+    packed_ref,
+    gains_ref,
     gate_all,
     up_all,
     down_all,
@@ -1332,6 +1315,12 @@
     inner_low,
     gate_low,
     input_low,
+    blocks,
+    blocks_one,
+    blocks_two,
+    blocks_got_one,
+    blocks_got_two,
+    blocks_got_three,
     move_sems,
     stream_sems,
     stage_sems,
@@ -1452,7 +1441,7 @@
     front = half_kept[mine, :] + half_got[mine, :].astype(f32) + own_got[...].astype(f32)
     gain_grad_out[...] = jnp.zeros_like(gain_grad_out)
     gain_grad_out[0:1, :] = jnp.sum(front * unit_values, 0, keepdims=True)
-    weighted = front * gain_two_ref[...]
+    weighted = front * gains_ref[1:2, :]
     result = cot_ref[own_at, :].astype(f32) + scale * (
         weighted - unit_values * jnp.mean(weighted * unit_values, axis=-1, keepdims=True)
     )
@@ -1498,7 +1487,7 @@
         copy.wait_recv()
     entries = entry_states(ends_sent, ends_got, index, count, batches, -1)
 
-    bias, gate_bias, input_bias, rate, slope = [vectors_ref[i : i + 1, :] for i in range(5)]
+    rate, slope = [packed_ref[i : i + 1, :units] for i in (7, 8)]
     zero = jnp.zeros((1, units), f32)
     sums = (zero, zero, zero)
     for batch in range(batches):
@@ -1550,13 +1539,28 @@
         edges_sent[batch] = conv_grad[top : top + 8, :]
     edge_copy = copies.start(edges_sent, edges_got, along[count - 2])
     mlp.serve(5)
-    size = blocks_out.shape[1]
+    size = blocks.shape[1]
     for number, right in enumerate((gate_low, input_low)):
         square = lax.dot_general(conv_low[...], right[...], tn, preferred_element_type=f32)
         for j in range(units // size):
             at = slice(j * size, (j + 1) * size)
             first = number * units + j * size
-            blocks_out[first : first + size, :] = square[at, at].astype(bf16)
+            blocks[first : first + size, :] = square[at, at].astype(bf16)
+    across = [{"seq": partner(index, bit)} for bit in (1, 2, 4)]
+    bits = [lax.rem(index // bit, 2) for bit in (1, 2, 4)]
+    firsts = [units, units // 2, units // 4]
+
+    def halves(source, stage):
+        kept = source[rows_at(bits[stage] * firsts[stage], firsts[stage]), :]
+        sent = source.at[rows_at((1 - bits[stage]) * firsts[stage], firsts[stage])]
+        got = (blocks_got_one, blocks_got_two, blocks_got_three)[stage]
+        return kept, copies.start(sent, got, across[stage]), got
+
+    def halved(kept, copy, got):
+        copy.wait_recv()
+        return (kept.astype(f32) + got[...].astype(f32)).astype(bf16)
+
+    halving = halves(blocks, 0)
 
     copies.sent(half_copy)
     copies.sent(own_copy)
@@ -1580,8 +1584,8 @@
         batch = block // (length // row_block)
         at = rows_at(block * row_block + batch * 8, row_block + 8, 8)
         wide, inner = conv_grad[at, :], padded[at, :]
-        total = taps_ref[0:1, :] * wide[:-8] + taps_ref[1:2, :] * wide[1:-7]
-        total = total + taps_ref[2:3, :] * wide[2:-6] + taps_ref[3:4, :] * wide[3:-5]
+        total = packed_ref[0:1, :units] * wide[:-8] + packed_ref[1:2, :units] * wide[1:-7]
+        total = total + packed_ref[2:3, :units] * wide[2:-6] + packed_ref[3:4, :units] * wide[3:-5]
         inner_low[rows_at(block * row_block, row_block), :] = total.astype(bf16)
         near = wide[:-8]
         terms = [near * inner[8 - k : 8 - k + row_block] for k in range(4)] + [near]
@@ -1599,6 +1603,8 @@
     own_copy = copies.start(own_sent, own_got, beside[1])
     mlp.serve(6)
     down.serve(6)
+    blocks_one[...] = halved(*halving)
+    halving = halves(blocks_one, 1)
     own_copy.wait_recv()
     final = own_middle[...] + (
         half_kept[mine, :] + half_got[mine, :].astype(f32) + own_got[...].astype(f32)
@@ -1609,6 +1615,8 @@
         mixed_out[own_at, to] = final[:, k * slab : (k + 1) * slab]
     join_copy = copies.start(mixed_out.at[own_at], mixed_out.at[own_at], beside[1])
     mlp.serve(7)
+    blocks_two[...] = halved(*halving)
+    halving = halves(blocks_two, 2)
     join_copy.wait_recv()
     join_copy = copies.start(mixed_out.at[kept_at], mixed_out.at[kept_at], beside[0])
     down.serve(7)
@@ -1624,6 +1632,7 @@
         down_grad[way * inner_half : (way + 1) * inner_half, :] = total
 
     mlp.serve(8, mlp_end)
+    blocks_out[...] = halved(*halving)
     down.serve(8, down_end)
     moves.wait(4)
     copies.end()
@@ -1645,7 +1654,7 @@
         array(bf16, rows, width),
         array(f32, rows // 4, width),
         array(f32, 8, units),
-        array(bf16, 2 * units, block_width),
+        array(bf16, units // 4, block_width),
         array(f32, 8, width),
         array(f32, inner, slab),
         *[array(bf16, rows, units)] * 4,
@@ -1678,6 +1687,10 @@
             pltpu.VMEM((slab, inner), f32),
             *[pltpu.VMEM(part.shape, part.dtype) for part in late],
             *[pltpu.VMEM((rows, units), bf16)] * 4,
+            *[
+                pltpu.VMEM((2 * units // part, block_width), bf16)
+                for part in (1, 2, 4, 2, 4, 8)
+            ],
             pltpu.SemaphoreType.DMA((13,)),
             pltpu.SemaphoreType.DMA((4 * count,)),
             pltpu.SemaphoreType.DMA((2,)),
@@ -1731,6 +1744,56 @@
         out_specs=(result,) * 3,
         compiler_params=pltpu.CompilerParams(vmem_limit_bytes=62 * 1024 * 1024),
     )(normed, cot, gate_all, up_all, down_all)
+
+
+def finish_body(large, *refs):
+    small, gains = refs[large : large + 2]
+    outs = refs[large + 2 :]
+    for source, target in zip(refs[:large], outs):
+        target[...] = source[...].astype(f32)
+    taps, *vectors = outs[large:]
+    taps[...] = small[0:4, :]
+    for row, vector in enumerate(vectors[:4]):
+        vector[...] = small[row + 4 : row + 5, :].reshape(vector.shape[0])
+    for row, vector in enumerate(vectors[4:]):
+        vector[...] = gains[row : row + 1, :].reshape(vector.shape[0])
+
+
+def finish(blocks, small, gains, *arrays):
+    parts = 4
+    half, block_width = blocks.shape[0] // 2, blocks.shape[1]
+
+    def rows_of(count, wide, first=0):
+        return pl.BlockSpec((count // parts, wide), lambda j: (j + first, 0))
+
+    def whole(*shape):
+        return pl.BlockSpec(shape, lambda j: (0,) * len(shape))
+
+    specs = [rows_of(*part.shape) for part in arrays]
+    blocks_out = rows_of(half, block_width)
+    vectors = [small.shape[1]] * 4 + [gains.shape[1]] * 2
+    shapes = [part.shape for part in arrays] + [(half, block_width)] * 2
+    shapes += [(4, small.shape[1])] + [(size,) for size in vectors]
+    return pl.pallas_call(
+        functools.partial(finish_body, len(arrays) + 2),
+        grid=(parts,),
+        out_shape=tuple(jax.ShapeDtypeStruct(shape, f32) for shape in shapes),
+        in_specs=[
+            *specs,
+            blocks_out,
+            rows_of(half, block_width, parts),
+            whole(*small.shape),
+            whole(*gains.shape),
+        ],
+        out_specs=(
+            *specs,
+            blocks_out,
+            blocks_out,
+            whole(4, small.shape[1]),
+            *[whole(size) for size in vectors],
+        ),
+        compiler_params=pltpu.CompilerParams(vmem_limit_bytes=62 * 1024 * 1024),
+    )(*arrays, blocks, blocks, small, gains)
 
 
 def block_diagonal(blocks):
@@ -1830,15 +1893,6 @@
         return values.reshape(batches, -1, values.shape[-1])
 
     if ringed:
-        vectors = jnp.stack(
-            [
-                conv_bias.astype(f32),
-                gate_bias.astype(f32),
-                input_bias.astype(f32),
-                -decay_scale * jax.nn.softplus(-decay),
-            ],
-            0,
-        )
         (
             gate_all,
             up_all,
@@ -1862,25 +1916,32 @@
             own_values,
             own_middle,
             normed_two,
+            ring_gains,
+            packed,
+            fresh,
         ) = head(
             count,
             lax.axis_size("fsdp"),
             batches,
             tokens.reshape(rows, width),
             cotangent.reshape(rows, width),
-            norm_gain.astype(f32)[None],
-            mlp_norm_gain.astype(f32)[None],
             branch_weight.T,
             inner_weight.T,
             out_weight,
             gate_weight,
             up_weight,
             down_weight,
-            taps,
-            vectors,
+            conv_weight,
+            conv_bias,
+            gate_bias,
+            input_bias,
+            -decay_scale * jax.nn.softplus(-decay),
+            decay_scale * jax.nn.sigmoid(-decay),
+            norm_gain,
+            mlp_norm_gain,
+            resets,
             gate_blocks,
             input_blocks,
-            resets.reshape(rows, 1),
         )
         hidden_low, gate_mlp_low, up_mlp_low = feed_forward(
             normed_two, cot_low, gate_all, up_all, down_all
@@ -1911,10 +1972,9 @@
             up_mlp_low,
             ends,
             own_middle,
-            resets.reshape(rows, 1),
-            taps,
-            jnp.concatenate([vectors, decay_scale * jax.nn.sigmoid(-decay)[None]], 0),
-            gain_two[None],
+            fresh,
+            packed,
+            ring_gains,
             gate_all,
             up_all,
             down_all,
@@ -1941,27 +2001,57 @@
             inner_all,
             own_values,
             own_grad,
-            gain_one[None],
-            gain_two_grad[:1],
+            ring_gains,
+            gain_two_grad,
             small,
             block_grads,
         )
-        block_grads = block_grads.astype(f32).reshape(2, block_count, block_width, block_width)
+        (
+            mixed,
+            tokens_grad,
+            gate_grad,
+            up_grad,
+            down_grad,
+            branch_grad,
+            inner_grad,
+            out_grad,
+            gate_blocks_grad,
+            input_blocks_grad,
+            taps_grad,
+            conv_bias_grad,
+            gate_bias_grad,
+            input_bias_grad,
+            decay_grad,
+            gain_one_grad,
+            gain_two_grad,
+        ) = finish(
+            block_grads,
+            small,
+            gains,
+            mixed,
+            tokens_grad,
+            gate_grad,
+            up_grad,
+            down_grad,
+            branch_grad,
+            inner_grad,
+            out_grad,
+        )
         return (
-            mixed.astype(f32).reshape(tokens.shape),
-            tokens_grad.astype(f32).reshape(tokens.shape),
-            gains[0],
+            mixed.reshape(tokens.shape),
+            tokens_grad.reshape(tokens.shape),
+            gain_one_grad,
             branch_grad.T,
             inner_grad.T,
-            small[:4],
-            small[4],
-            block_grads[0],
-            block_grads[1],
-            small[5],
-            small[6],
-            small[7],
+            taps_grad,
+            conv_bias_grad,
+            gate_blocks_grad.reshape(block_count, block_width, block_width),
+            input_blocks_grad.reshape(block_count, block_width, block_width),
+            gate_bias_grad,
+            input_bias_grad,
+            decay_grad,
             out_grad,
-            gains[1],
+            gain_two_grad,
             gate_grad,
             up_grad,
             down_grad,

time: 643 us -> 618 us (0.961)
  local copies, waits for them, and re-layouts: 21.5 us -> 0 us
  other arithmetic: 12.6 us -> 1.3 us
  Pallas kernels: 600 us -> 608 us
    pallas_call x0 -> x1, Pallas kernels: none -> 11.6 us  [finish(): pl.pallas_call(functools.partial(finish_body, len(arrays) + 2), grid=(par...]
    unnamed x36 -> x0, local copies, waits for them, and re-layouts: 11 us -> none
    pallas_call x1, Pallas kernels: 112 us -> 103 us  [tail(): pl.pallas_call(functools.partial(tail_body, count), out_shape=(grad, grad...]
    reshape x2 -> x0, other arithmetic: 6.74 us -> none  [the longest x1 4.2 us: local(): tokens_grad.astype(f32).reshape(tokens.shape)]
where the time goes in v6:
time: 618 us; the launch traced here: 610 us
  Pallas kernels  608 us (98%)
    pallas_call x1, Pallas kernels, head(): pl.pallas_call(functools.partial(head_body, count, fsdp, batches), out_sh...  277 us
    pallas_call x1, Pallas kernels, back(): pl.pallas_call(functools.partial(back_body, count, fsdp, batches), out_sh...  200 us
    pallas_call x1, Pallas kernels, tail(): pl.pallas_call(functools.partial(tail_body, count), out_shape=(grad, grad...  103 us
    pallas_call x1, Pallas kernels, feed_forward(): pl.pallas_call(mlp_body, grid=(hidden // wide,), out_shape=(jax.ShapeDtyp...  16.6 us

profile of v6, /device:TPU:0, one launch (start us, length us, event | category | flops | bytes accessed | tf_op | source)
XLA Modules:
  0.0 610.0 jit_solution(16303316629861159104)
XLA Ops:
  0.7 1.3 fusion.8
  2.0 276.9 %shard_map.305 = (bf16[2048,1536]{1,0:T(8,128)(2,1)}, bf16[2048,1536]{1,0:T(8,128)(2,1)}, bf16[1536,2048]{1,0:T(8,128)(2,1)}, bf16[704,2048]{1,0:T(8,128)(2,1)},...) custom-call(bf16[512,2048]{1,0:T(8,128)(2,1)} %bitcast.10, ...), custom_call_target="tpu_custom_call" | custom-call | tf_op jit(solution)/shard_map/pallas_call | solution.py:1156
  278.8 16.6 %shard_map.306 = (bf16[512,1536]{1,0:T(8,128)(2,1)}, bf16[512,1536]{1,0:T(8,128)(2,1)}, bf16[512,1536]{1,0:T(8,128)(2,1)}) custom-call(bf16[512,2048]{1,0:T(8,128)(2,1)} %get-tuple-element.81.normed_ref, bf16[512,2048]{1,0:T(8,128)(2,1)} %get-tuple-element.80.cot_ref, bf16[2048,1536]{1,0:T(8,128)(2,1)} %get-tuple-element.82.gate_ref.gate_all, ...), custom_call_target="tpu_custom_call" | custom-call | tf_op jit(solution)/shard_map/pallas_call | solution.py:1733
  295.5 199.6 %shard_map.307 = (bf16[512,2048]{1,0:T(8,128)(2,1)}, bf16[512,2048]{1,0:T(8,128)(2,1)}, f32[128,2048]{1,0:T(8,128)}, f32[8,704]{1,0:T(8,128)}, bf16[176,176]{1,0...) custom-call(bf16[512,2048]{1,0:T(8,128)(2,1)} %get-tuple-element.80., ...), custom_call_target="tpu_custom_call" | custom-call | tf_op jit(solution)/shard_map/pallas_call | solution.py:1663
  495.1 102.8 %shard_map.308 = (f32[704,256]{1,0:T(8,128)}, f32[704,256]{1,0:T(8,128)}, f32[704,256]{1,0:T(8,128)}, bf16[512,2048]{1,0:T(8,128)(2,1)}, f32[8,2048]{1,0:T(8,128...) custom-call(bf16[512,2048]{1,0:T(8,128)(2,1)} %get-tuple-element.104.emb_ref, ...), custom_call_target="tpu_custom_call" | custom-call | tf_op jit(solution)/shard_map/pallas_call | solution.py:681
  598.0 11.6 %shard_map.309 = (f32[512,2048]{1,0:T(8,128)}, f32[512,2048]{1,0:T(8,128)}, f32[256,1536]{1,0:T(8,128)}, f32[256,1536]{1,0:T(8,128)}, f32[1536,256]{1,0:T(8,128)...) custom-call(bf16[512,2048]{1,0:T(8,128)(2,1)} %get-tuple-element.103, ...), custom_call_target="tpu_custom_call" | custom-call | tf_op jit(solution)/shard_map/pallas_call | solution.py:1777

commit v7 on v6

--- a/solution.py
+++ b/solution.py
@@ -439,12 +439,17 @@
 
 
 def greet(devices):
-    barrier = pltpu.get_barrier_semaphore()
     for device in devices:
         pl.semaphore_signal(
-            barrier, inc=1, device_id=device, device_id_type=pl.DeviceIdType.MESH
-        )
-    pl.semaphore_wait(barrier, len(devices))
+            pltpu.get_barrier_semaphore(),
+            inc=1,
+            device_id=device,
+            device_id_type=pl.DeviceIdType.MESH,
+        )
+
+
+def greeted(devices):
+    pl.semaphore_wait(pltpu.get_barrier_semaphore(), len(devices))
 
 
 tail_copies = 28 + 4 + 3 + 3 + 5
@@ -459,8 +464,8 @@
     inner_ref,
     branch_all_in,
     inner_all_in,
-    values_ref,
-    grad_ref,
+    values_in,
+    grad_in,
     gain_ref,
     gain_two_ref,
     small_ref,
@@ -487,6 +492,8 @@
     gain_got,
     branch_all_ref,
     inner_all_ref,
+    values_ref,
+    grad_ref,
     move_sems,
     send_sems,
     recv_sems,
@@ -503,8 +510,11 @@
     moves = Moves(move_sems)
     moves.start(branch_all_in, branch_all_ref)
     moves.start(inner_all_in, inner_all_ref)
-
-    greet([forth, back] + across + beside)
+    moves.start(values_in, values_ref)
+    moves.start(grad_in, grad_ref)
+
+    others = [forth, back] + across + beside
+    greet(others)
 
     cut = slim_got.shape[2]
     parts = (slice(0, cut), slice(cut, units))
@@ -530,7 +540,8 @@
     def send(name, way, step, total):
         sent, got = (slim_sent, slim_got) if name == "out" else (wide_sent, wide_got)
         there = pl.ds(0, total.shape[0])
-        sent[way, step, there, :] = total.astype(bf16)
+        if step > 0:
+            sent[way, step, there, :] = total.astype(bf16)
         rings[name, way] = copies.start(
             sent.at[way, step, there], got.at[way, step, there], back if way else forth
         )
@@ -552,9 +563,13 @@
             else:
                 (inner_out if way else branch_out)[...] = total
 
-    for name in ("out", "front"):
-        for way in (0, 1):
-            send(name, way, 0, term(name, way, 1))
+    firsts = [(name, way, term(name, way, 1)) for name in ("out", "front") for way in (0, 1)]
+    for name, way, first in firsts:
+        sent = slim_sent if name == "out" else wide_sent
+        sent[way, 0, pl.ds(0, first.shape[0]), :] = first.astype(bf16)
+    greeted(others)
+    for name, way, first in firsts:
+        send(name, way, 0, first)
     moves.wait(2)
 
     high = blocks_out.shape[0]
@@ -606,6 +621,7 @@
     serve("front", 3)
 
     own_copy.wait_recv()
+    moves.wait(2)
     values = values_ref[...]
     scale = lax.rsqrt(jnp.mean(values * values, axis=-1, keepdims=True) + eps)
     unit_values = values * scale
@@ -690,8 +706,8 @@
             jax.ShapeDtypeStruct((8 * high, block_width), bf16),
         ),
         in_specs=[whole] * 5
-        + [pl.BlockSpec(memory_space=pl.ANY)] * 2
-        + [whole] * (len(operands) - 7),
+        + [pl.BlockSpec(memory_space=pl.ANY)] * 4
+        + [whole] * (len(operands) - 9),
         out_specs=(whole,) * 7,
         scratch_shapes=[
             pltpu.VMEM((2, steps, units, slab), bf16),
@@ -709,7 +725,9 @@
             pltpu.VMEM((5, 8, width), f32),
             pltpu.VMEM((units, width), bf16),
             pltpu.VMEM((units, width), bf16),
-            pltpu.SemaphoreType.DMA((2,)),
+            pltpu.VMEM((rows // 4, width), f32),
+            pltpu.VMEM((rows // 4, width), f32),
+            pltpu.SemaphoreType.DMA((4,)),
             pltpu.SemaphoreType.DMA((tail_copies,)),
             pltpu.SemaphoreType.DMA((tail_copies,)),
         ],
@@ -796,8 +814,8 @@
     count,
     fsdp,
     batches,
-    tokens_ref,
-    cot_ref,
+    tokens_in,
+    cot_in,
     branch_ref,
     inner_ref,
     out_ref,
@@ -833,10 +851,10 @@
     mixed_low_far,
     gate_square_far,
     input_square_far,
+    own_values_far,
+    own_middle_far,
+    normed_two_far,
     ends,
-    own_values,
-    own_middle,
-    normed_two,
     gains,
     packed_ref,
     fresh_ref,
@@ -855,6 +873,11 @@
     mixed_low,
     gate_square_ref,
     input_square_ref,
+    own_values,
+    own_middle,
+    normed_two,
+    tokens_ref,
+    cot_ref,
     tokens_low,
     prods,
     local_states,
@@ -877,11 +900,16 @@
     forth, back = {"seq": ring_index(place + 1, count)}, {"seq": ring_index(place - 1, count)}
     along, beside = peers(count, fsdp)
     copies = Copies(send_sems, recv_sems)
+    moves = Moves(far_sems)
+    moves.start(tokens_in, tokens_ref)
+    moves.start(cot_in, cot_ref)
     rows, width = tokens_ref.shape
     units, hidden = branch_ref.shape[0], down_ref.shape[0]
     length, slab = rows // batches, width // count
     core, side = lax.rem(unit, 2), lax.rem(unit // 2, 2)
     mid, own = rows // 2, rows // 4
+
+    greet(along + beside)
 
     locals_of = []
     for source, target in zip(
@@ -895,7 +923,7 @@
         copy.start()
         locals_of.append(copy)
 
-    greet(along + beside)
+    greeted(along + beside)
 
     pairs = {
         "front": ((branch_ref, branch_all, 0, units), (inner_ref, inner_all, 0, units)),
@@ -949,6 +977,7 @@
     for batch in range(batches):
         fresh_ref[batch * length : (batch + 1) * length, :] = flags[:, batch : batch + 1]
 
+    moves.wait(1)
     for k in range(count):
         plain = pl.ds(pl.multiple_of(ring_index(place - k, count) * slab, slab), slab)
         part = slice(k * slab, (k + 1) * slab)
@@ -977,6 +1006,7 @@
         size = blocks.shape[1]
         for j in range(blocks.shape[0]):
             square[j * size : (j + 1) * size, j * size : (j + 1) * size] = blocks[j]
+    moves.wait(1)
     for k in range(count):
         plain = pl.ds(pl.multiple_of(ring_index(place - k, count) * slab, slab), slab)
         cot_out[:, k * slab : (k + 1) * slab] = cot_ref[:, plain]
@@ -1101,7 +1131,6 @@
     for step in range(6, count):
         start("mlp", step)
         start("down", step)
-    moves = Moves(far_sems)
     for source, target in (
         (branch_all, branch_all_far),
         (inner_all, inner_all_far),
@@ -1118,11 +1147,14 @@
         (mixed_low, mixed_low_far),
         (gate_square_ref, gate_square_far),
         (input_square_ref, input_square_far),
+        (own_values, own_values_far),
+        (own_middle, own_middle_far),
+        (normed_two, normed_two_far),
     ):
         moves.start(source, target)
     finish("mlp")
     finish("down")
-    moves.wait(15)
+    moves.wait(18)
     copies.end()
 
 
@@ -1143,23 +1175,24 @@
         + [array(f32, rows, units)] * 3
         + [array(f32, rows + 8 * batches, units), array(bf16, rows, units)]
         + [array(bf16, units, units)] * 2
+        + [array(f32, rows // 4, width)] * 2
+        + [array(bf16, rows, width)]
     )
     outs = (
         [array(bf16, width, hidden)] * 2
         + [array(bf16, hidden, width)]
         + kept
-        + [array(f32, 8, units)]
-        + [array(f32, rows // 4, width)] * 2
-        + [array(bf16, rows, width), array(f32, 8, width)]
+        + [array(f32, 8, units), array(f32, 8, width)]
         + [array(f32, 16, width), array(f32, rows, 1)]
     )
     return pl.pallas_call(
         functools.partial(head_body, count, fsdp, batches),
         out_shape=tuple(outs),
-        in_specs=[whole] * 2 + [place] * 6 + [whole] * 11,
-        out_specs=tuple([place] * (len(outs) - 7) + [whole] * 7),
+        in_specs=[place] * 8 + [whole] * 11,
+        out_specs=tuple([place] * (len(outs) - 4) + [whole] * 4),
         scratch_shapes=[
             *[pltpu.VMEM(part.shape, part.dtype) for part in kept],
+            *[pltpu.VMEM((rows, width), bf16)] * 2,
             pltpu.VMEM((rows, width), bf16),
             pltpu.VMEM((rows, units), f32),
             pltpu.VMEM((rows, units), f32),
@@ -1173,7 +1206,7 @@
             pltpu.VMEM((rows // 4, width), bf16),
             pltpu.VMEM((rows // 4, width), bf16),
             pltpu.SemaphoreType.DMA((6,)),
-            pltpu.SemaphoreType.DMA((15,)),
+            pltpu.SemaphoreType.DMA((20,)),
             pltpu.SemaphoreType.DMA((head_copies,)),
             pltpu.SemaphoreType.DMA((head_copies,)),
         ],
@@ -1202,9 +1235,14 @@
         self.neighbours = neighbours
         self.copies = [[], []]
 
-    def send(self, way, step, total):
+    def prepare(self):
+        for way, k in ((0, 1), (1, self.count - 1)):
+            self.slots[way, 0] = self.terms[way](k).astype(bf16)
+
+    def send(self, way, step, total=None):
         here, there = (step - 1) % ring_slots, step % ring_slots
-        self.slots[way, here] = total.astype(bf16)
+        if step > 1:
+            self.slots[way, here] = total.astype(bf16)
         if step >= ring_slots:
             pl.semaphore_wait(self.credits.at[way], 1)
         copy = pltpu.make_async_remote_copy(
@@ -1228,12 +1266,13 @@
                 )
 
     def serve(self, step, end=None):
+        if step == 1:
+            self.send(0, 1)
+            self.send(1, 1)
+            return
         slabs = (step % self.count, (self.count - step) % self.count)
         terms = [term(k) for term, k in zip(self.terms, slabs)]
         for way, own in enumerate(terms):
-            if step == 1:
-                self.send(way, 1, own)
-                continue
             self.copies[way][step - 2].wait_recv()
             total = self.slots[way, (step - 1) % ring_slots].astype(f32) + own
             if step < self.count:
@@ -1270,9 +1309,6 @@
     states_in,
     gate_square_in,
     input_square_in,
-    mixed_out,
-    middle_low,
-    own_grad,
     small_out,
     blocks_out,
     gain_grad_out,
@@ -1283,6 +1319,9 @@
     input_low_out,
     gate_grad,
     up_grad,
+    mixed_far,
+    middle_far,
+    own_grad_far,
     half_sent,
     half_kept,
     half_got,
@@ -1321,6 +1360,9 @@
     blocks_got_one,
     blocks_got_two,
     blocks_got_three,
+    mixed_out,
+    middle_low,
+    own_grad,
     move_sems,
     stream_sems,
     stage_sems,
@@ -1395,6 +1437,9 @@
         count,
         neighbours,
     )
+    mlp.prepare()
+    down.prepare()
+    greeted(along + beside)
     mlp.serve(1)
     down.serve(1)
 
@@ -1539,16 +1584,19 @@
         edges_sent[batch] = conv_grad[top : top + 8, :]
     edge_copy = copies.start(edges_sent, edges_got, along[count - 2])
     mlp.serve(5)
-    size = blocks.shape[1]
+    size = blocks.shape[1] // 2
+    tall = blocks.shape[0] * size // units
+    blocks[...] = jnp.zeros_like(blocks)
     for number, right in enumerate((gate_low, input_low)):
         square = lax.dot_general(conv_low[...], right[...], tn, preferred_element_type=f32)
         for j in range(units // size):
             at = slice(j * size, (j + 1) * size)
-            first = number * units + j * size
-            blocks[first : first + size, :] = square[at, at].astype(bf16)
+            blocks[j * tall : j * tall + size, number * size : (number + 1) * size] = square[
+                at, at
+            ].astype(bf16)
     across = [{"seq": partner(index, bit)} for bit in (1, 2, 4)]
     bits = [lax.rem(index // bit, 2) for bit in (1, 2, 4)]
-    firsts = [units, units // 2, units // 4]
+    firsts = [blocks.shape[0] // part for part in (2, 4, 8)]
 
     def halves(source, stage):
         kept = source[rows_at(bits[stage] * firsts[stage], firsts[stage]), :]
@@ -1631,10 +1679,13 @@
     def down_end(way, total):
         down_grad[way * inner_half : (way + 1) * inner_half, :] = total
 
+    moves.start(middle_low, middle_far)
+    moves.start(own_grad, own_grad_far)
+    moves.start(mixed_out, mixed_far)
     mlp.serve(8, mlp_end)
     blocks_out[...] = halved(*halving)
     down.serve(8, down_end)
-    moves.wait(4)
+    moves.wait(7)
     copies.end()
 
 
@@ -1644,27 +1695,28 @@
     rows, width = cot.shape
     units, inner = late[0].shape[1], hidden.shape[1]
     slab = width // count
+    high = units // block_width * (-(-block_width // 32) * 32)
     whole, place = pl.BlockSpec(memory_space=pltpu.VMEM), pl.BlockSpec(memory_space=pl.ANY)
 
     def array(dtype, *shape):
         return jax.ShapeDtypeStruct(shape, dtype)
 
     outs = [
-        array(bf16, rows, width),
-        array(bf16, rows, width),
-        array(f32, rows // 4, width),
         array(f32, 8, units),
-        array(bf16, units // 4, block_width),
+        array(bf16, high // 8, 2 * block_width),
         array(f32, 8, width),
         array(f32, inner, slab),
         *[array(bf16, rows, units)] * 4,
         *[array(f32, slab, inner)] * 2,
+        array(bf16, rows, width),
+        array(bf16, rows, width),
+        array(f32, rows // 4, width),
     ]
     return pl.pallas_call(
         functools.partial(back_body, count, fsdp, batches),
         out_shape=tuple(outs),
         in_specs=[whole] * (len(operands) - 13) + [place] * 13,
-        out_specs=tuple([whole] * 7 + [place] * 6),
+        out_specs=tuple([whole] * 4 + [place] * 9),
         scratch_shapes=[
             pltpu.VMEM((rows // 2, width), bf16),
             pltpu.VMEM((rows // 2, width), f32),
@@ -1688,10 +1740,13 @@
             *[pltpu.VMEM(part.shape, part.dtype) for part in late],
             *[pltpu.VMEM((rows, units), bf16)] * 4,
             *[
-                pltpu.VMEM((2 * units // part, block_width), bf16)
+                pltpu.VMEM((high // part, 2 * block_width), bf16)
                 for part in (1, 2, 4, 2, 4, 8)
             ],
-            pltpu.SemaphoreType.DMA((13,)),
+            pltpu.VMEM((rows, width), bf16),
+            pltpu.VMEM((rows, width), bf16),
+            pltpu.VMEM((rows // 4, width), f32),
+            pltpu.SemaphoreType.DMA((16,)),
             pltpu.SemaphoreType.DMA((4 * count,)),
             pltpu.SemaphoreType.DMA((2,)),
             pltpu.SemaphoreType.DMA((2, 2, count - 1)),
@@ -1747,11 +1802,14 @@
 
 
 def finish_body(large, *refs):
-    small, gains = refs[large : large + 2]
-    outs = refs[large + 2 :]
+    blocks, small, gains = refs[large : large + 3]
+    outs = refs[large + 3 :]
     for source, target in zip(refs[:large], outs):
         target[...] = source[...].astype(f32)
-    taps, *vectors = outs[large:]
+    gate_blocks, input_blocks, taps, *vectors = outs[large:]
+    size = gate_blocks.shape[0]
+    gate_blocks[...] = blocks[0:size, 0:size].astype(f32)
+    input_blocks[...] = blocks[0:size, size : 2 * size].astype(f32)
     taps[...] = small[0:4, :]
     for row, vector in enumerate(vectors[:4]):
         vector[...] = small[row + 4 : row + 5, :].reshape(vector.shape[0])
@@ -1759,12 +1817,12 @@
         vector[...] = gains[row : row + 1, :].reshape(vector.shape[0])
 
 
-def finish(blocks, small, gains, *arrays):
-    parts = 4
-    half, block_width = blocks.shape[0] // 2, blocks.shape[1]
-
-    def rows_of(count, wide, first=0):
-        return pl.BlockSpec((count // parts, wide), lambda j: (j + first, 0))
+def finish(parts, blocks, small, gains, *arrays):
+    block_width = blocks.shape[1] // 2
+    half = parts * block_width
+
+    def rows_of(count, wide):
+        return pl.BlockSpec((count // parts, wide), lambda j: (j, 0))
 
     def whole(*shape):
         return pl.BlockSpec(shape, lambda j: (0,) * len(shape))
@@ -1775,13 +1833,12 @@
     shapes = [part.shape for part in arrays] + [(half, block_width)] * 2
     shapes += [(4, small.shape[1])] + [(size,) for size in vectors]
     return pl.pallas_call(
-        functools.partial(finish_body, len(arrays) + 2),
+        functools.partial(finish_body, len(arrays)),
         grid=(parts,),
         out_shape=tuple(jax.ShapeDtypeStruct(shape, f32) for shape in shapes),
         in_specs=[
             *specs,
-            blocks_out,
-            rows_of(half, block_width, parts),
+            rows_of(*blocks.shape),
             whole(*small.shape),
             whole(*gains.shape),
         ],
@@ -1793,7 +1850,7 @@
             *[whole(size) for size in vectors],
         ),
         compiler_params=pltpu.CompilerParams(vmem_limit_bytes=62 * 1024 * 1024),
-    )(*arrays, blocks, blocks, small, gains)
+    )(*arrays, blocks, small, gains)
 
 
 def block_diagonal(blocks):
@@ -1912,10 +1969,10 @@
             mixed_low,
             gate_square,
             input_square,
-            ends,
             own_values,
             own_middle,
             normed_two,
+            ends,
             ring_gains,
             packed,
             fresh,
@@ -1947,9 +2004,6 @@
             normed_two, cot_low, gate_all, up_all, down_all
         )
         (
-            mixed,
-            middle_low,
-            own_grad,
             small,
             block_grads,
             gain_two_grad,
@@ -1960,6 +2014,9 @@
             input_low,
             gate_grad,
             up_grad,
+            mixed,
+            middle_low,
+            own_grad,
         ) = back(
             count,
             lax.axis_size("fsdp"),
@@ -2025,6 +2082,7 @@
             gain_one_grad,
             gain_two_grad,
         ) = finish(
+            block_count,
             block_grads,
             small,
             gains,

time: 618 us -> 609 us (0.985)
  Pallas kernels: 608 us -> 598 us
where the time goes in v7:
time: 609 us; the launch traced here: 601 us
  Pallas kernels  598 us (98%)
    pallas_call x1, Pallas kernels, head(): pl.pallas_call(functools.partial(head_body, count, fsdp, batches), out_sh...  274 us
    pallas_call x1, Pallas kernels, back(): pl.pallas_call(functools.partial(back_body, count, fsdp, batches), out_sh...  196 us
    pallas_call x1, Pallas kernels, tail(): pl.pallas_call(functools.partial(tail_body, count), out_shape=(grad, grad...  100 us
    pallas_call x1, Pallas kernels, feed_forward(): pl.pallas_call(mlp_body, grid=(hidden // wide,), out_shape=(jax.ShapeDtyp...  16.6 us

profile of v7, /device:TPU:0, one launch (start us, length us, event | category | flops | bytes accessed | tf_op | source)
XLA Modules:
  0.0 600.7 jit_solution(8730036348367822794)
XLA Ops:
  0.7 1.3 fusion.8
  2.0 274.3 %shard_map.305 = (bf16[2048,1536]{1,0:T(8,128)(2,1)}, bf16[2048,1536]{1,0:T(8,128)(2,1)}, bf16[1536,2048]{1,0:T(8,128)(2,1)}, bf16[704,2048]{1,0:T(8,128)(2,1)},...) custom-call(bf16[512,2048]{1,0:T(8,128)(2,1)} %bitcast.10, ...), custom_call_target="tpu_custom_call" | custom-call | tf_op jit(solution)/shard_map/pallas_call | solution.py:1188
  276.3 16.6 %shard_map.306 = (bf16[512,1536]{1,0:T(8,128)(2,1)}, bf16[512,1536]{1,0:T(8,128)(2,1)}, bf16[512,1536]{1,0:T(8,128)(2,1)}) custom-call(bf16[512,2048]{1,0:T(8,128)(2,1)} %get-tuple-element.81.normed_ref, bf16[512,2048]{1,0:T(8,128)(2,1)} %get-tuple-element.80.cot_ref, bf16[2048,1536]{1,0:T(8,128)(2,1)} %get-tuple-element.82.gate_ref.gate_all, ...), custom_call_target="tpu_custom_call" | custom-call | tf_op jit(solution)/shard_map/pallas_call | solution.py:1788
  292.9 195.9 %shard_map.307 = (f32[8,704]{1,0:T(8,128)}, bf16[96,352]{1,0:T(8,128)(2,1)}, f32[8,2048]{1,0:T(8,128)}, f32[1536,256]{1,0:T(8,128)}, bf16[512,704]{1,0:T(8,128)(...) custom-call(bf16[512,2048]{1,0:T(8,128)(2,1)} %get-tuple-element.80., ...), custom_call_target="tpu_custom_call" | custom-call | tf_op jit(solution)/shard_map/pallas_call | solution.py:1715
  488.9 100.2 %shard_map.308 = (f32[704,256]{1,0:T(8,128)}, f32[704,256]{1,0:T(8,128)}, f32[704,256]{1,0:T(8,128)}, bf16[512,2048]{1,0:T(8,128)(2,1)}, f32[8,2048]{1,0:T(8,128...) custom-call(bf16[512,2048]{1,0:T(8,128)(2,1)} %get-tuple-element.104.emb_ref, ...), custom_call_target="tpu_custom_call" | custom-call | tf_op jit(solution)/shard_map/pallas_call | solution.py:697
  589.0 11.2 %shard_map.309 = (f32[512,2048]{1,0:T(8,128)}, f32[512,2048]{1,0:T(8,128)}, f32[256,1536]{1,0:T(8,128)}, f32[256,1536]{1,0:T(8,128)}, f32[1536,256]{1,0:T(8,128)...) custom-call(bf16[512,2048]{1,0:T(8,128)(2,1)} %get-tuple-element.103, ...), custom_call_target="tpu_custom_call" | custom-call | tf_op jit(solution)/shard_map/pallas_call | solution.py:1835

commit v8 on v7

--- a/solution.py
+++ b/solution.py
@@ -689,7 +689,7 @@
     small, blocks = operands[-2:]
     rows, width = emb.shape
     units = mixed.shape[1]
-    slab, cut = width // count, -(-units // 256) * 128
+    slab, cut = width // count, units // 2
     high, block_width = blocks.shape
     whole = pl.BlockSpec(memory_space=pltpu.VMEM)
     grad = jax.ShapeDtypeStruct((units, slab), f32)

time: 609 us -> 607 us (level)
  no operation moved by 1% of the time
where the time goes in v8:
time: 607 us; the launch traced here: 599 us
  Pallas kernels  596 us (98%)
    pallas_call x1, Pallas kernels, head(): pl.pallas_call(functools.partial(head_body, count, fsdp, batches), out_sh...  274 us
    pallas_call x1, Pallas kernels, back(): pl.pallas_call(functools.partial(back_body, count, fsdp, batches), out_sh...  196 us
    pallas_call x1, Pallas kernels, tail(): pl.pallas_call(functools.partial(tail_body, count), out_shape=(grad, grad...  98 us
    pallas_call x1, Pallas kernels, feed_forward(): pl.pallas_call(mlp_body, grid=(hidden // wide,), out_shape=(jax.ShapeDtyp...  16.6 us

profile of v8, /device:TPU:0, one launch (start us, length us, event | category | flops | bytes accessed | tf_op | source)
XLA Modules:
  0.0 598.6 jit_solution(14452829795501238263)
XLA Ops:
  0.7 1.3 fusion.8
  2.0 274.3 %shard_map.305 = (bf16[2048,1536]{1,0:T(8,128)(2,1)}, bf16[2048,1536]{1,0:T(8,128)(2,1)}, bf16[1536,2048]{1,0:T(8,128)(2,1)}, bf16[704,2048]{1,0:T(8,128)(2,1)},...) custom-call(bf16[512,2048]{1,0:T(8,128)(2,1)} %bitcast.10, ...), custom_call_target="tpu_custom_call" | custom-call | tf_op jit(solution)/shard_map/pallas_call | solution.py:1188
  276.3 16.6 %shard_map.306 = (bf16[512,1536]{1,0:T(8,128)(2,1)}, bf16[512,1536]{1,0:T(8,128)(2,1)}, bf16[512,1536]{1,0:T(8,128)(2,1)}) custom-call(bf16[512,2048]{1,0:T(8,128)(2,1)} %get-tuple-element.81.normed_ref, bf16[512,2048]{1,0:T(8,128)(2,1)} %get-tuple-element.80.cot_ref, bf16[2048,1536]{1,0:T(8,128)(2,1)} %get-tuple-element.82.gate_ref.gate_all, ...), custom_call_target="tpu_custom_call" | custom-call | tf_op jit(solution)/shard_map/pallas_call | solution.py:1788
  292.9 195.9 %shard_map.307 = (f32[8,704]{1,0:T(8,128)}, bf16[96,352]{1,0:T(8,128)(2,1)}, f32[8,2048]{1,0:T(8,128)}, f32[1536,256]{1,0:T(8,128)}, bf16[512,704]{1,0:T(8,128)(...) custom-call(bf16[512,2048]{1,0:T(8,128)(2,1)} %get-tuple-element.80., ...), custom_call_target="tpu_custom_call" | custom-call | tf_op jit(solution)/shard_map/pallas_call | solution.py:1715
  488.9 98.0 %shard_map.308 = (f32[704,256]{1,0:T(8,128)}, f32[704,256]{1,0:T(8,128)}, f32[704,256]{1,0:T(8,128)}, bf16[512,2048]{1,0:T(8,128)(2,1)}, f32[8,2048]{1,0:T(8,128...) custom-call(bf16[512,2048]{1,0:T(8,128)(2,1)} %get-tuple-element.104.emb_ref, ...), custom_call_target="tpu_custom_call" | custom-call | tf_op jit(solution)/shard_map/pallas_call | solution.py:697
  586.9 11.2 %shard_map.309 = (f32[512,2048]{1,0:T(8,128)}, f32[512,2048]{1,0:T(8,128)}, f32[256,1536]{1,0:T(8,128)}, f32[256,1536]{1,0:T(8,128)}, f32[1536,256]{1,0:T(8,128)...) custom-call(bf16[512,2048]{1,0:T(8,128)(2,1)} %get-tuple-element.103, ...), custom_call_target="tpu_custom_call" | custom-call | tf_op jit(solution)/shard_map/pallas_call | solution.py:1835
